TPU v7x, 32 devices: a whole 2x2x4 slice. The times are simulated.
32 devices in a mesh: seq: 8 (over y, x, core), mp: 4 (over z).
Axes of the slice: x: 2, y: 2, z: 4, core: 2. Of those that a mesh axis runs over, the one named last changes fastest.
Arguments:
- hidden_in: bfloat16 [4096, 5376], P('seq'), may hold values from -6 to 6
- norm_gain: float32 [5376], replicated, may hold values from 0.5 to 1.5
- query_weight: bfloat16 [5376, 512], P(None, 'mp'), as said below
- kv_weight: bfloat16 [5376, 1024], P(None, 'mp'), as said below
- out_weight: bfloat16 [512, 5376], P('mp'), may hold values from -0.75 to 0.75
Outputs:
- attn_out: bfloat16 [5376, 4096], P('mp', 'seq')
Inputs may be any that keep to these rules, and one draw needn't show every extreme that they name: `query_weight`: query projection columns of mean zero scaled by the fan-in. `kv_weight`: key and value projection columns of mean zero; the columns of query heads 2j and 2j+1 are equal, one key-value head shared by the pair.
All inputs are finite; a program needn't handle non-finite values.
Results may differ from a plain program's by a relative error of at most 0.023.
Values may be sent and summed in bfloat16 or wider, within the bound.
No kernel may reach another device: no remote copies, remote signals or barrier semaphores. Data moves between devices by JAX's collectives and lax.ppermute only.
A program may use at most 64 MiB of HBM per device.

v0:
```python
import math

import jax
import jax.numpy as jnp
from jax import lax
from jax.sharding import PartitionSpec as P

WINDOW = 1024


def shifted(block, axis, distance):
    devices = range(lax.axis_size(axis))
    route = [(i - distance, i) for i in devices if i - distance in devices]
    return lax.ppermute(block, axis, route)


def rotate_half(tensor, positions):
    half = tensor.shape[-1] // 2
    freq = jnp.exp(
        -math.log(10000.0) * jnp.arange(half, dtype=jnp.float32) * (2.0 / tensor.shape[-1])
    )
    angle = positions[:, None] * freq[None, :]
    cosine = jnp.cos(angle)
    sine = jnp.sin(angle)
    first = tensor[:, :half]
    second = tensor[:, half:]
    return jnp.concatenate(
        [first * cosine - second * sine, second * cosine + first * sine], axis=-1
    )


def per_device(hidden_in, norm_gain, query_weight, kv_weight, out_weight):
    rows = hidden_in.shape[0]
    head_size = query_weight.shape[1]
    widths = hidden_in.astype(jnp.float32)
    inverse = lax.rsqrt(jnp.mean(widths * widths, axis=-1, keepdims=True) + 1e-06)
    normed = (widths * inverse * norm_gain[None, :]).astype(jnp.bfloat16)
    first_pos = lax.axis_index("seq") * rows
    positions = (first_pos + jnp.arange(rows, dtype=jnp.int32)).astype(jnp.float32)
    queries = rotate_half(
        jnp.dot(normed, query_weight, preferred_element_type=jnp.float32), positions
    ).astype(jnp.bfloat16)
    projected = jnp.dot(normed, kv_weight, preferred_element_type=jnp.float32)
    keys = rotate_half(projected[:, :head_size], positions).astype(jnp.bfloat16)
    values = projected[:, head_size:].astype(jnp.bfloat16)
    reach = -(-WINDOW // rows)
    key_parts = []
    value_parts = []
    for distance in range(reach, 0, -1):
        moved_keys, moved_values = shifted((keys, values), "seq", distance)
        key_parts.append(moved_keys)
        value_parts.append(moved_values)
    context_keys = jnp.concatenate(key_parts + [keys], axis=0)
    context_values = jnp.concatenate(value_parts + [values], axis=0)
    context_pos = first_pos - reach * rows + jnp.arange((reach + 1) * rows, dtype=jnp.int32)
    block = min(rows, 512)
    scores = lax.dot_general(
        queries, context_keys, (((1,), (1,)), ((), ())), preferred_element_type=jnp.float32
    )
    scores = scores * (1.0 / math.sqrt(168.0))
    query_pos = first_pos + 0 + jnp.arange(block, dtype=jnp.int32)
    valid = (
        (context_pos[None, :] <= query_pos[:, None])
        & (query_pos[:, None] - context_pos[None, :] < WINDOW)
        & (context_pos[None, :] >= 0)
    )
    scores = jnp.where(valid, scores, jnp.float32(-1e30))
    highest = jnp.max(scores, axis=-1, keepdims=True)
    expo = jnp.exp(scores - highest)
    probs = (expo / jnp.sum(expo, axis=-1, keepdims=True)).astype(jnp.bfloat16)
    outputs = jnp.dot(probs, context_values, preferred_element_type=jnp.float32).astype(
        jnp.bfloat16
    )
    weight_cols = lax.all_to_all(out_weight, "mp", split_axis=1, concat_axis=0, tiled=True)
    feature_cols = weight_cols.shape[1]
    portion = lax.all_gather(outputs, "mp", axis=1, tiled=True)
    width_cols = portion.shape[1]
    heads_here = width_cols // head_size
    weight_part = weight_cols.reshape(heads_here, head_size, feature_cols)
    shaped = portion.reshape(rows, heads_here, head_size)
    terms = jnp.einsum(
        "rhc,hcd->hdr", shaped, weight_part, preferred_element_type=jnp.float32
    ).astype(jnp.bfloat16)
    terms = lax.optimization_barrier(terms)
    summed = jnp.sum(terms.astype(jnp.float32), axis=0)
    return summed.astype(jnp.bfloat16)


def solution(mesh):
    in_specs = (P("seq", None), P(), P(None, "mp"), P(None, "mp"), P("mp", None))
    out_specs = P("mp", "seq")
    return jax.shard_map(
        per_device, mesh=mesh, in_specs=in_specs, out_specs=out_specs, check_vma=False
    )
```

profile of v0, /device:TPU:0, one launch (start us, length us, event | category | flops | bytes accessed | tf_op | source)
XLA Modules:
  0.0 64.5 jit_solution(475590713270300999)
XLA Ops:
  0.0 0.0 copy-start
  0.0 2.6 %copy.6 = bf16[128,5376]{0,1:T(8,128)(2,1)} copy(bf16[128,5376]{1,0:T(8,128)(2,1)} %param.9) | data formatting | bytes 2752512 | tf_op args[4]
  2.7 6.3 %all-to-all-start = ((bf16[128,4,1344]{0,2,1:T(8,128)(2,1)}), bf16[128,4,1344]{0,2,1:T(8,128)(2,1)}, u32[]{:S(2)}, u32[]{:S(2)}) async-start(bf16[128,4,1344]{0,2,1:T(8,128)(2,1)} %bitcast.15), calls=%async_computation | async-start | bytes 2752512 | tf_op jit(solution)/shard_map/all_to_all | solution.py:74
  9.0 0.0 copy-start.1
  9.0 3.7 %fusion = f32[512]{0:T(512)S(1)} fusion(bf16[512,5376]{1,0:T(8,128)(2,1)} %param.5), kind=kLoop, calls=%fused_computation.2 | loop fusion | flops 8257024 | bytes 5507072 | tf_op jit(solution)/shard_map/reduce_sum | solution.py:36
  12.7 0.0 copy-done.1
  12.7 5.0 %fusion.9 = f32[512,128]{0,1:T(8,128)S(1)} fusion(bf16[5376,128]{1,0:T(8,128)(2,1)} %param.7, bf16[512,5376]{1,0:T(8,128)(2,1)} %param.5, f32[5376]{0:T(1024)S(1)} %copy-done.1, f32[512]{0:T(512)S(1)} %add_rsqrt_fusion), kind=kOutput, calls=%fused_computation.15 | convolution fusion | flops 715653120 | bytes 7166976 | tf_op jit(solution)/shard_map/dot_general | solution.py:41
  17.7 0.0 copy-done
  17.8 4.5 %fusion.7 = f32[512,256]{0,1:T(8,128)S(1)} fusion(bf16[5376,256]{1,0:T(8,128)(2,1)S(1)} %copy-done, bf16[512,5376]{1,0:T(8,128)(2,1)} %param.5, f32[5376]{0:T(1024)S(1)} %copy-done.1, f32[512]{0:T(512)S(1)} %add_rsqrt_fusion), kind=kOutput, calls=%fused_computation.14 | convolution fusion | flops 1420296192 | bytes 8805376 | tf_op jit(solution)/shard_map/dot_general | solution.py:43
  22.3 0.6 fusion.37
  22.9 2.1 %collective-permute-start.1 = (bf16[512,128]{0,1:T(8,128)(2,1)S(1)}, bf16[512,128]{0,1:T(8,128)(2,1)}, u32[]{:S(2)}, u32[]{:S(2)}) collective-permute-start(bf16[512,128]{0,1:T(8,128)(2,1)S(1)} %pad_maximum_fusion), channel_id=1, source_target_pairs={{0,4},{4,8},{8,12},{12,16},{16,20},{20,24},{24,28},{1,5},{5,9},{9,... | collective-permute-start | bytes 393224 | tf_op jit(solution)/shard_map/ppermute | solution.py:14
  25.0 3.9 %collective-permute-start = (bf16[512,128]{0,1:T(8,128)(2,1)S(1)}, bf16[512,128]{0,1:T(8,128)(2,1)}, u32[]{:S(2)}, u32[]{:S(2)}) collective-permute-start(bf16[512,128]{0,1:T(8,128)(2,1)S(1)} %pad_maximum_fusion), channel_id=1, source_target_pairs={{0,8},{4,12},{8,16},{12,20},{16,24},{20,28},{1,9},{5,13},{9,17},{1... | collective-permute-start | bytes 393224 | tf_op jit(solution)/shard_map/ppermute | solution.py:14
  28.9 3.2 %collective-permute-start.3 = (bf16[512,128]{0,1:T(8,128)(2,1)S(1)}, bf16[512,128]{0,1:T(8,128)(2,1)S(1)}, u32[]{:S(2)}, u32[]{:S(2)}) collective-permute-start(bf16[512,128]{0,1:T(8,128)(2,1)S(1)} %slice.38), channel_id=1, source_target_pairs={{0,4},{4,8},{8,12},{12,16},{16,20},{20,24},{24,28},{1,5},{5,9},{9,... | collective-permute-start | bytes 393224 | tf_op jit(solution)/shard_map/ppermute | solution.py:14
  32.2 2.8 %collective-permute-start.2 = (bf16[512,128]{0,1:T(8,128)(2,1)S(1)}, bf16[512,128]{0,1:T(8,128)(2,1)S(1)}, u32[]{:S(2)}, u32[]{:S(2)}) collective-permute-start(bf16[512,128]{0,1:T(8,128)(2,1)S(1)} %slice.38), channel_id=1, source_target_pairs={{0,8},{4,12},{8,16},{12,20},{16,24},{20,28},{1,9},{5,13},{9,17},{1... | collective-permute-start | bytes 393224 | tf_op jit(solution)/shard_map/ppermute | solution.py:14
  35.0 0.0 collective-permute-done.1
  35.0 0.0 collective-permute-done
  35.0 2.3 %fusion.50 = (f32[512]{0:T(512)S(1)}, f32[512,1536]{1,0:T(8,128)S(1)}) fusion(bf16[512,64]{0,1:T(8,128)(2,1)S(1)} %get-tuple-element.9, bf16[512,64]{0,1:T(8,128)(2,1)S(1)} %get-tuple-element.10, bf16[512,128]{0,1:T(8,128)(2,1)} %collective-permute-done.1, bf16[512,128]{0,1:T(8,128)(2,1)} %collective-permute-done, ...), kind=kOutput, calls=%fused_computation.64 | convolution fusion | flops 209452544 | bytes 3681792 | tf_op jit(solution)/shard_map/dot_general | solution.py:57
  37.3 0.6 fusion.6
  37.9 0.0 collective-permute-done.3
  37.9 0.3 collective-permute-done.2
  38.1 0.7 %fusion.13 = bf16[512,128]{1,0:T(8,128)(2,1)S(1)} fusion(f32[512,1536]{1,0:T(8,128)S(1)} %get-tuple-element.12, f32[512]{0:T(512)S(1)} %fusion.6, f32[512]{0:T(512)S(1)} %get-tuple-element.11, bf16[512,128]{0,1:T(8,128)(2,1)S(1)} %slice.38, bf16[512,128]{0,1:T(8,128)(2,1)S(1)} %collective-permute-done.3, bf16[512,128]{0,1:T(8,128)(2,1)S(1)} %collective-permute-done.2), kind=kOutput, calls=%fused_computation.18 | convolution fusion | flops 204931072 | bytes 3674112 | tf_op jit(solution)/shard_map/dot_general | solution.py:71
  38.8 15.4 %all_gather.3 = bf16[512,512]{1,0:T(8,128)(2,1)S(1)} all-gather(bf16[512,128]{1,0:T(8,128)(2,1)S(1)} %fusion.13), channel_id=1, replica_groups=mesh['seq'=8,'mp'=4] {'mp'}, dimensions={1}, use_global_device_ids=true | all-gather | bytes 655360 | tf_op jit(solution)/shard_map/all_gather | solution.py:76
  54.2 0.0 all-to-all-done
  54.2 5.3 %convert_bitcast_fusion = bf16[4,1344,512]{2,1,0:T(8,128)(2,1)} fusion(bf16[128,4,1344]{0,2,1:T(8,128)(2,1)} %all-to-all-done, bf16[512,512]{1,0:T(8,128)(2,1)S(1)} %all_gather.3), kind=kOutput, calls=%fused_computation.5 | convolution fusion | flops 707395584 | bytes 7405568 | tf_op jit(solution)/shard_map/rhc,hcd->hdr/dot_general | solution.py:81
  59.5 4.9 %reduce_sum.32 = bf16[1344,512]{1,0:T(8,128)(2,1)} reduce(bf16[4,1344,512]{2,1,0:T(8,128)(2,1)} %convert_bitcast_fusion, bf16[]{:T(256)} %constant.33.clone.1), dimensions={0}, to_apply=%region_3.4 | reduce | flops 2064384 | bytes 6881282 | tf_op jit(solution)/shard_map/reduce_sum | solution.py:85
  (8 shorter events, 0.1 us)
Async XLA Ops:
  0.0 17.7 %copy-start = (bf16[5376,256]{1,0:T(8,128)(2,1)S(1)}, bf16[5376,256]{1,0:T(8,128)(2,1)}, u32[]{:S(2)}) copy-start(bf16[5376,256]{1,0:T(8,128)(2,1)} %param.8) | copy-start | bytes 8257540
  2.7 51.6 %all-to-all-start = ((bf16[128,4,1344]{0,2,1:T(8,128)(2,1)}), bf16[128,4,1344]{0,2,1:T(8,128)(2,1)}, u32[]{:S(2)}, u32[]{:S(2)}) async-start(bf16[128,4,1344]{0,2,1:T(8,128)(2,1)} %bitcast.15), calls=%async_computation | async-start | bytes 2752512 | tf_op jit(solution)/shard_map/all_to_all | solution.py:74
  9.0 3.8 %copy-start.1 = (f32[5376]{0:T(1024)S(1)}, f32[5376]{0:T(1024)}, u32[]{:S(2)}) copy-start(f32[5376]{0:T(1024)} %param.6) | copy-start | bytes 64516
  22.9 12.0 %collective-permute-start.1 = (bf16[512,128]{0,1:T(8,128)(2,1)S(1)}, bf16[512,128]{0,1:T(8,128)(2,1)}, u32[]{:S(2)}, u32[]{:S(2)}) collective-permute-start(bf16[512,128]{0,1:T(8,128)(2,1)S(1)} %pad_maximum_fusion), channel_id=1, source_target_pairs={{0,4},{4,8},{8,12},{12,16},{16,20},{20,24},{24,28},{1,5},{5,9},{9,... | collective-permute-start | bytes 393224 | tf_op jit(solution)/shard_map/ppermute | solution.py:14
  25.0 10.0 %collective-permute-start = (bf16[512,128]{0,1:T(8,128)(2,1)S(1)}, bf16[512,128]{0,1:T(8,128)(2,1)}, u32[]{:S(2)}, u32[]{:S(2)}) collective-permute-start(bf16[512,128]{0,1:T(8,128)(2,1)S(1)} %pad_maximum_fusion), channel_id=1, source_target_pairs={{0,8},{4,12},{8,16},{12,20},{16,24},{20,28},{1,9},{5,13},{9,17},{1... | collective-permute-start | bytes 393224 | tf_op jit(solution)/shard_map/ppermute | solution.py:14
  28.9 8.9 %collective-permute-start.3 = (bf16[512,128]{0,1:T(8,128)(2,1)S(1)}, bf16[512,128]{0,1:T(8,128)(2,1)S(1)}, u32[]{:S(2)}, u32[]{:S(2)}) collective-permute-start(bf16[512,128]{0,1:T(8,128)(2,1)S(1)} %slice.38), channel_id=1, source_target_pairs={{0,4},{4,8},{8,12},{12,16},{16,20},{20,24},{24,28},{1,5},{5,9},{9,... | collective-permute-start | bytes 393224 | tf_op jit(solution)/shard_map/ppermute | solution.py:14
  32.2 5.9 %collective-permute-start.2 = (bf16[512,128]{0,1:T(8,128)(2,1)S(1)}, bf16[512,128]{0,1:T(8,128)(2,1)S(1)}, u32[]{:S(2)}, u32[]{:S(2)}) collective-permute-start(bf16[512,128]{0,1:T(8,128)(2,1)S(1)} %slice.38), channel_id=1, source_target_pairs={{0,8},{4,12},{8,16},{12,20},{16,24},{20,28},{1,9},{5,13},{9,17},{1... | collective-permute-start | bytes 393224 | tf_op jit(solution)/shard_map/ppermute | solution.py:14
where the time goes:
time: 64.9 us; the launch traced here: 64.5 us
  starting transfers between devices  18.3 us (28%)
  matrix products  17.9 us (28%)
  blocking collectives  15.4 us (24%)
  other arithmetic  9.85 us (15%)
  local copies, waits for them, and re-layouts  2.67 us (4%)
    all_gather x1, blocking collectives, per_device(): portion = lax.all_gather(outputs, 'mp', axis=1, tiled=True)  15.4 us
    ppermute x4, starting transfers between devices, shifted(): return lax.ppermute(block, axis, route)  12 us
    all_to_all x1, starting transfers between devices, per_device(): lax.all_to_all(out_weight, 'mp', split_axis=1, concat_axis=0, tiled=True)  6.32 us
    dot_general x1, matrix products, per_device(): jnp.einsum('rhc,hcd->hdr', shaped, weight_part, preferred_element_type=jn...  5.32 us
    dot_general x1, matrix products, per_device(): jnp.dot(normed, query_weight, preferred_element_type=jnp.float32)  5.02 us
    reduce_sum x1, other arithmetic, per_device(): summed = jnp.sum(terms.astype(jnp.float32), axis=0)  4.9 us
    dot_general x1, matrix products, per_device(): projected = jnp.dot(normed, kv_weight, preferred_element_type=jnp.float32)  4.54 us
    reduce_sum x1, other arithmetic, per_device(): jnp.mean(widths * widths, axis=-1, keepdims=True) + 1e-06  3.72 us
  transfers between devices with their start and end apart: 5, of which 1 were waited for; matrix products, arithmetic and copies ran while one was open for 27% of the time, Pallas kernels for 0%

commit v1 on v0

v1 whole, which is shorter than its diff:
```python
import functools
import math

import jax
import jax.numpy as jnp
import numpy as np
from jax import lax
from jax.experimental import pallas as pl
from jax.experimental.pallas import tpu as pltpu
from jax.sharding import PartitionSpec as P

WINDOW = 1024
LANES = 128
MASKED = -1e30
F32 = jnp.float32
BF16 = jnp.bfloat16


def around(block, axis, distance):
    size = lax.axis_size(axis)
    return lax.ppermute(block, axis, [(i, (i + distance) % size) for i in range(size)])


def other_core(block):
    return lax.ppermute(block, "seq", [(i, i ^ 1) for i in range(lax.axis_size("seq"))])


def call(kernel, name, out_shape, cost, vmem=48 * 2**20, **kwargs):
    flops, moved = cost
    return pl.pallas_call(
        kernel,
        name=name,
        out_shape=out_shape,
        cost_estimate=pl.CostEstimate(flops=flops, bytes_accessed=moved, transcendentals=0),
        compiler_params=pltpu.CompilerParams(vmem_limit_bytes=vmem),
        **kwargs,
    )


def matmul(left, right, dims=((1,), (0,))):
    return lax.dot_general(left, right, (dims, ((), ())), preferred_element_type=F32)


def rope_table(rows, head):
    freq = np.exp(-math.log(10000.0) * np.arange(head // 2) * (2.0 / head))
    angle = np.arange(rows)[:, None] * freq[None, :]
    return np.concatenate([np.cos(angle), np.sin(angle)], axis=1).astype(np.float32)


def rope(tensor, table, first_pos):
    head = tensor.shape[1]
    half = head // 2
    lane = lax.broadcasted_iota(jnp.int32, (1, head), 1)
    low = lane < half
    index = jnp.where(low, lane, lane - half).astype(F32)
    base = first_pos * jnp.exp(index * (-math.log(10000.0) * 2.0 / head))
    base_cos = jnp.cos(base)
    base_sin = jnp.where(low, -jnp.sin(base), jnp.sin(base))
    turned = pltpu.roll(table, half, 1)
    row_cos = jnp.where(low, table, turned)
    row_sin = jnp.where(low, -turned, table)
    cosine = base_cos * row_cos - base_sin * row_sin
    sine = base_sin * row_cos + base_cos * row_sin
    return tensor * cosine + pltpu.roll(tensor, half, 1) * sine


def project_kernel(finish, steps, width, x_ref, gain_ref, weight_ref, table_ref, *refs):
    outs, (total_ref, square_ref) = refs[:-2], refs[-2:]
    step = pl.program_id(0)

    @pl.when(step == 0)
    def _():
        total_ref[...] = jnp.zeros_like(total_ref)
        square_ref[...] = jnp.zeros_like(square_ref)

    x = x_ref[...].astype(F32)
    squares = x * x
    part = squares[:, :LANES]
    for start in range(LANES, x.shape[1], LANES):
        part = part + squares[:, start : start + LANES]
    square_ref[...] += part
    scaled = (x * gain_ref[...]).astype(BF16)
    total_ref[...] += matmul(scaled, weight_ref[...])

    @pl.when(step == steps - 1)
    def _():
        mean = jnp.sum(square_ref[...], axis=1, keepdims=True) * (1.0 / width)
        result = total_ref[...] * lax.rsqrt(mean + 1e-06)
        finish(result, table_ref[...], *outs)


def finish_keys_values(head, result, table, key_ref, value_ref):
    rows = result.shape[0]
    first_pos = (lax.axis_index("seq") * rows).astype(F32)
    key_ref[...] = rope(result[:, :head], table, first_pos).astype(BF16)
    value_ref[...] = result[:, head:].T.astype(BF16)


def finish_queries(scale, result, table, query_ref):
    rows = result.shape[0]
    first_pos = (lax.axis_index("seq") * rows).astype(F32)
    query_ref[...] = (rope(result, table, first_pos) * scale).astype(BF16)


def project(finish, name, hidden, gain, weight, table, out_shapes):
    rows, width = hidden.shape
    cols = weight.shape[1]
    block = 768 if width % 768 == 0 else width
    steps = width // block
    whole = lambda shape: pl.BlockSpec(shape, lambda k: (0, 0))
    return call(
        functools.partial(project_kernel, finish, steps, width),
        name,
        out_shapes,
        (2 * rows * width * cols, 2 * width * (rows + cols)),
        grid=(steps,),
        in_specs=[
            pl.BlockSpec((rows, block), lambda k: (0, k)),
            pl.BlockSpec((1, block), lambda k: (0, k)),
            pl.BlockSpec((block, cols), lambda k: (k, 0)),
            whole(table.shape),
        ],
        out_specs=[whole(s.shape) for s in out_shapes],
        scratch_shapes=[pltpu.VMEM((rows, cols), F32), pltpu.VMEM((rows, LANES), F32)],
    )(hidden, gain, weight, table)


def attention_kernel(q_ref, k0_ref, k1_ref, k2_ref, v0_ref, v1_ref, v2_ref, out_ref):
    rows = q_ref.shape[0]
    chunk = min(rows, 256)
    shard = lax.axis_index("seq")
    bias1 = jnp.where(shard < 1, MASKED, 0.0).astype(F32)
    bias2 = jnp.where(shard < 2, MASKED, 0.0).astype(F32)
    nt = ((1,), (1,))
    for start in range(0, rows, chunk):
        q = q_ref[start : start + chunk, :]
        key_index = lax.broadcasted_iota(jnp.int32, (rows, chunk), 0)
        query_index = lax.broadcasted_iota(jnp.int32, (rows, chunk), 1) + start
        own = key_index <= query_index
        near = matmul(k1_ref[...], q, nt) + bias1
        mixed = jnp.where(own, matmul(k0_ref[...], q, nt), matmul(k2_ref[...], q, nt) + bias2)
        highest = jnp.maximum(
            jnp.max(near, axis=0, keepdims=True), jnp.max(mixed, axis=0, keepdims=True)
        )
        near = jnp.exp2(near - highest)
        mixed = jnp.exp2(mixed - highest)
        norm = jnp.sum(near, axis=0, keepdims=True) + jnp.sum(mixed, axis=0, keepdims=True)
        out = matmul(v1_ref[...], near.astype(BF16))
        out += matmul(v0_ref[...], jnp.where(own, mixed, 0.0).astype(BF16))
        out += matmul(v2_ref[...], jnp.where(own, 0.0, mixed).astype(BF16))
        out_ref[:, start : start + chunk] = (out / norm).astype(BF16)


def attention(q, keys, values):
    rows, head = q.shape
    return call(
        attention_kernel,
        "attention",
        jax.ShapeDtypeStruct((head, rows), BF16),
        (12 * rows * rows * head, 16 * rows * head),
    )(q, *keys, *values)


def weight_window(width, mp):
    cols = width // mp
    tiles = max(-(-cols * (m + 1) // LANES) - cols * m // LANES for m in range(mp))
    return cols, tiles


def window_start(m, width, mp):
    cols, tiles = weight_window(width, mp)
    first = jnp.minimum(m * cols // LANES, width // LANES - tiles)
    return pl.multiple_of(first * LANES, LANES)


def cut_kernel(width, mp, weight_ref, *refs):
    outs, sems = refs[:-1], refs[-1]
    half, window = outs[0].shape
    m = lax.axis_index("mp")
    core = lax.axis_index("seq") % 2
    row = pl.multiple_of(core * half, half)
    copies = []
    for distance, out in enumerate(outs, 1):
        start = window_start((m + distance) % mp, width, mp)
        copies.append(
            pltpu.make_async_copy(
                weight_ref.at[pl.ds(row, half), pl.ds(start, window)], out, sems.at[distance - 1]
            )
        )
    for copy in copies:
        copy.start()
    for copy in copies:
        copy.wait()


def turn_kernel(width, mp, weight_ref, *refs):
    mine, theirs = refs[: mp - 1], refs[mp - 1 : 2 * mp - 2]
    out_ref, own_ref, sem = refs[2 * mp - 2 :]
    head, window = own_ref.shape
    half = head // 2
    m = lax.axis_index("mp")
    core = lax.axis_index("seq") % 2
    start = window_start(m, width, mp)
    copy = pltpu.make_async_copy(weight_ref.at[:, pl.ds(start, window)], own_ref, sem)
    copy.start()
    for i in range(mp - 1):
        a, b = mine[i][...], theirs[i][...]
        low = jnp.where(core == 0, a, b)
        high = jnp.where(core == 0, b, a)
        both = jnp.concatenate([low, high], axis=0)
        out_ref[:, (i + 1) * head : (i + 2) * head] = both.T
    copy.wait()
    out_ref[:, :head] = own_ref[...].T


def output_kernel(width, mp, chunk, weight_ref, *refs):
    heads, out_ref = refs[:-1], refs[-1]
    m = lax.axis_index("mp")
    cols = width // mp
    offset = m * cols - window_start(m, width, mp) + pl.program_id(0) * chunk
    weight = weight_ref[pl.ds(pl.multiple_of(offset, 16), chunk), :]
    taken = jnp.concatenate([h[...] for h in heads], axis=0)
    out_ref[...] = matmul(weight, taken).astype(BF16)


def per_device(hidden_in, norm_gain, query_weight, kv_weight, out_weight):
    rows, width = hidden_in.shape
    head = query_weight.shape[1]
    mp = lax.axis_size("mp")
    cols, tiles = weight_window(width, mp)
    window = tiles * LANES
    half = head // 2
    gain = norm_gain[None, :]
    table = jnp.asarray(rope_table(rows, head))
    anywhere = pl.BlockSpec(memory_space=pl.ANY)
    shape = lambda *dims: jax.ShapeDtypeStruct(dims, BF16)

    pieces = call(
        functools.partial(cut_kernel, width, mp),
        "cut_weight",
        [shape(half, window)] * (mp - 1),
        (0, 4 * (mp - 1) * half * window),
        in_specs=[anywhere],
        out_specs=[anywhere] * (mp - 1),
        scratch_shapes=[pltpu.SemaphoreType.DMA((mp - 1,))],
    )(out_weight)
    mine = [around(piece, "mp", d) for d, piece in enumerate(pieces, 1)]

    keys, values = project(
        functools.partial(finish_keys_values, head),
        "keys_values",
        hidden_in,
        gain,
        kv_weight,
        table,
        [shape(rows, head), shape(head, rows)],
    )
    key_parts = [keys] + [around(keys, "seq", d) for d in (1, 2)]
    value_parts = [values] + [around(values, "seq", d) for d in (1, 2)]
    scale = math.log2(math.e) / math.sqrt(168.0)
    (queries,) = project(
        functools.partial(finish_queries, scale),
        "queries",
        hidden_in,
        gain,
        query_weight,
        table,
        [shape(rows, head)],
    )
    head_out = attention(queries, key_parts, value_parts)
    outs = [head_out] + [around(head_out, "mp", d) for d in range(1, mp)]

    theirs = [other_core(piece) for piece in mine]
    turned = call(
        functools.partial(turn_kernel, width, mp),
        "turn_weight",
        shape(window, mp * head),
        (0, 4 * window * mp * head),
        in_specs=[anywhere] + [pl.BlockSpec(memory_space=pltpu.VMEM)] * (2 * mp - 2),
        scratch_shapes=[pltpu.VMEM((head, window), BF16), pltpu.SemaphoreType.DMA],
    )(out_weight, *mine, *theirs)

    chunk = max(c for c in range(16, min(cols, 448) + 1, 16) if cols % c == 0)
    return call(
        functools.partial(output_kernel, width, mp, chunk),
        "output",
        shape(cols, rows),
        (2 * cols * rows * mp * head, 2 * cols * (rows + mp * head)),
        grid=(cols // chunk,),
        in_specs=[pl.BlockSpec(memory_space=pltpu.VMEM)] * (mp + 1),
        out_specs=pl.BlockSpec((chunk, rows), lambda i: (i, 0)),
    )(turned, *outs)


def solution(mesh):
    in_specs = (P("seq", None), P(), P(None, "mp"), P(None, "mp"), P("mp", None))
    out_specs = P("mp", "seq")
    return jax.shard_map(
        per_device, mesh=mesh, in_specs=in_specs, out_specs=out_specs, check_vma=False
    )
```

time: 64.9 us -> 56.7 us (0.87)
  matrix products: 17.9 us -> 0 us
  Pallas kernels: 0 us -> 17.9 us
  waiting for transfers between devices: 0.27 us -> 16.1 us
  blocking collectives: 15.4 us -> 0 us
  other arithmetic: 9.85 us -> 0 us
  local copies, waits for them, and re-layouts: 2.67 us -> 3.88 us
    dot_general x5 -> x0, matrix products: 17.9 us -> none  [the longest x1 5.32 us: per_device(): jnp.einsum('rhc,hcd->hdr', shaped, weight_part, preferred_element_type=jn...]
    pallas_call x0 -> x6, Pallas kernels: none -> 17.9 us  [the longest x2 13.3 us: project(): call(functools.partial(project_kernel, finish, steps, width), name, out_s...]
    ppermute x4 -> x13, waiting for transfers between devices: 0.26 us -> 16.1 us  [the longest x10 16.1 us: around(): lax.ppermute(block, axis, [(i, (i + distance) % size) for i in range(size)])]
    all_gather x1 -> x0, blocking collectives: 15.4 us -> none  [per_device(): portion = lax.all_gather(outputs, 'mp', axis=1, tiled=True)]
    reduce_sum x3 -> x0, other arithmetic: 9.2 us -> none  [the longest x1 4.9 us: per_device(): summed = jnp.sum(terms.astype(jnp.float32), axis=0)]
    ppermute x4 -> x13, starting transfers between devices: 12 us -> 18.3 us  [the longest x10 16.1 us: around(): lax.ppermute(block, axis, [(i, (i + distance) % size) for i in range(size)])]
    all_to_all x1 -> x0, starting transfers between devices: 6.32 us -> none  [per_device(): lax.all_to_all(out_weight, 'mp', split_axis=1, concat_axis=0, tiled=True)]
    broadcast_in_dim x0 -> x1, local copies, waits for them, and re-layouts: none -> 0.75 us  [per_device(): gain = norm_gain[None, :]]
  transfers between devices with their start and end apart: 5 -> 13, of which waited for: 1 -> 3; matrix products, arithmetic and copies ran while one was open for 27% -> 1% of each run, Pallas kernels for 0% -> 27%
where the time goes in v1:
time: 56.7 us; the launch traced here: 56.2 us
  starting transfers between devices  18.3 us (32%)
  Pallas kernels  17.9 us (32%)
  waiting for transfers between devices  16.1 us (28%)
  local copies, waits for them, and re-layouts  3.88 us (7%)
    ppermute x10, starting transfers between devices, around(): lax.ppermute(block, axis, [(i, (i + distance) % size) for i in range(size)])  16.1 us
    ppermute x10, waiting for transfers between devices, around(): lax.ppermute(block, axis, [(i, (i + distance) % size) for i in range(size)])  16.1 us
    pallas_call x2, Pallas kernels, project(): call(functools.partial(project_kernel, finish, steps, width), name, out_s...  13.3 us
    unnamed x10, local copies, waits for them, and re-layouts  3.12 us
    pallas_call x1, Pallas kernels, per_device(): call(functools.partial(output_kernel, width, mp, chunk), 'output', shape(...  2.34 us
    ppermute x3, starting transfers between devices, other_core(): lax.ppermute(block, 'seq', [(i, i ^ 1) for i in range(lax.axis_size('seq'...  2.2 us
    pallas_call x1, Pallas kernels, attention(): call(attention_kernel, 'attention', jax.ShapeDtypeStruct((head, rows), BF...  1.59 us
  transfers between devices with their start and end apart: 13, of which 3 were waited for; matrix products, arithmetic and copies ran while one was open for 1% of the time, Pallas kernels for 27%

profile of v1, /device:TPU:0, one launch (start us, length us, event | category | flops | bytes accessed | tf_op | source)
XLA Modules:
  0.0 56.2 jit_solution(1017617130242200428)
XLA Ops:
  0.0 1.3 %copy-done = bf16[128,5376]{1,0:T(8,128)(2,1)S(1)} copy-done((bf16[128,5376]{1,0:T(8,128)(2,1)S(1)}, bf16[128,5376]{1,0:T(8,128)(2,1)}, u32[]{:S(2)}) %copy-start) | copy-done | bytes 1376280
  1.3 0.1 cut_weight.1
  1.5 3.1 %collective-permute-start = (bf16[64,1408]{1,0:T(8,128)(2,1)S(1)}, bf16[64,1408]{1,0:T(8,128)(2,1)S(1)}, u32[]{:S(2)}, u32[]{:S(2)}) collective-permute-start(bf16[64,1408]{1,0:T(8,128)(2,1)S(1)} %get-tuple-element.10), channel_id=1, source_target_pairs={{0,1},{1,2},{2,3},{3,0},{4,5},{5,6},{6,7},{7,4},{8,9},{9,10},{10,1... | collective-permute-start | bytes 540680 | tf_op jit(solution)/shard_map/ppermute | solution.py:21
  4.5 0.8 %broadcast_in_dim.3.gain_ref = f32[1,5376]{1,0:T(1,128)S(1)} reshape(f32[5376]{0:T(1024)} %param.7) | data formatting | bytes 43008 | tf_op jit(solution)/shard_map/broadcast_in_dim | solution.py:233
  5.3 0.0 copy-start.2
  5.3 1.8 %copy-done.2 = bf16[5376,256]{1,0:T(8,128)(2,1)S(1)} copy-done((bf16[5376,256]{1,0:T(8,128)(2,1)S(1)}, bf16[5376,256]{1,0:T(8,128)(2,1)}, u32[]{:S(2)}) %copy-start.2) | copy-done | bytes 2752536
  7.1 6.8 %keys_values.1 = (bf16[512,128]{1,0:T(8,128)(2,1)S(1)}, bf16[128,512]{1,0:T(8,128)(2,1)S(1)}) custom-call(bf16[512,5376]{1,0:T(8,128)(2,1)} %x_ref.3, f32[1,5376]{1,0:T(1,128)S(1)} %broadcast_in_dim.3.gain_ref, bf16[5376,256]{1,0:T(8,128)(2,1)S(1)} %copy-done.2, f32[512,128]{1,0:T(8,128)S(1)} %copy-done.4), custom_call_target="tpu_custom_call" | custom-call | flops 1409286144 | bytes 8257536 | tf_op jit(solution)/shard_map/keys_values/pallas_call | solution.py:111
  13.8 1.5 %collective-permute-start.7 = (bf16[512,128]{1,0:T(8,128)(2,1)S(1)}, bf16[512,128]{1,0:T(8,128)(2,1)S(1)}, u32[]{:S(2)}, u32[]{:S(2)}) collective-permute-start(bf16[512,128]{1,0:T(8,128)(2,1)S(1)} %get-tuple-element.13.k0_ref), channel_id=1, source_target_pairs={{0,8},{4,12},{8,16},{12,20},{16,24},{20,28},{24,0},{28,4},{1,9},{5... | collective-permute-start | bytes 393224 | tf_op jit(solution)/shard_map/ppermute | solution.py:21
  15.4 2.6 %collective-permute-start.1 = (bf16[64,1408]{1,0:T(8,128)(2,1)S(1)}, bf16[64,1408]{1,0:T(8,128)(2,1)S(1)}, u32[]{:S(2)}, u32[]{:S(2)}) collective-permute-start(bf16[64,1408]{1,0:T(8,128)(2,1)S(1)} %get-tuple-element.11), channel_id=1, source_target_pairs={{0,2},{1,3},{2,0},{3,1},{4,6},{5,7},{6,4},{7,5},{8,10},{9,11},{10,... | collective-permute-start | bytes 540680 | tf_op jit(solution)/shard_map/ppermute | solution.py:21
  18.0 1.4 %collective-permute-start.2 = (bf16[64,1408]{1,0:T(8,128)(2,1)S(1)}, bf16[64,1408]{1,0:T(8,128)(2,1)S(1)}, u32[]{:S(2)}, u32[]{:S(2)}) collective-permute-start(bf16[64,1408]{1,0:T(8,128)(2,1)S(1)} %get-tuple-element.12), channel_id=1, source_target_pairs={{0,3},{1,0},{2,1},{3,2},{4,7},{5,4},{6,5},{7,6},{8,11},{9,8},{10,9... | collective-permute-start | bytes 540680 | tf_op jit(solution)/shard_map/ppermute | solution.py:21
  19.3 1.0 %collective-permute-start.3 = (bf16[64,1408]{1,0:T(8,128)(2,1)S(1)}, bf16[64,1408]{1,0:T(8,128)(2,1)S(1)}, u32[]{:S(2)}, u32[]{:S(2)}) collective-permute-start(bf16[64,1408]{1,0:T(8,128)(2,1)S(1)} %collective-permute-done.refs_0_), channel_id=1, source_target_pairs={{0,4},{4,0},{8,12},{12,8},{16,20},{20,16},{24,28},{28,24},{1,5},{5... | collective-permute-start | bytes 540680 | tf_op jit(solution)/shard_map/ppermute | solution.py:25
  20.4 1.5 %collective-permute-start.9 = (bf16[128,512]{1,0:T(8,128)(2,1)S(1)}, bf16[128,512]{1,0:T(8,128)(2,1)S(1)}, u32[]{:S(2)}, u32[]{:S(2)}) collective-permute-start(bf16[128,512]{1,0:T(8,128)(2,1)S(1)} %get-tuple-element.14.v0_ref), channel_id=1, source_target_pairs={{0,8},{4,12},{8,16},{12,20},{16,24},{20,28},{24,0},{28,4},{1,9},{5... | collective-permute-start | bytes 393224 | tf_op jit(solution)/shard_map/ppermute | solution.py:21
  21.9 0.0 collective-permute-done.6.k1_ref
  21.9 0.0 collective-permute-start.8
  21.9 5.2 %collective-permute-done.1.refs_1_ = bf16[64,1408]{1,0:T(8,128)(2,1)S(1)} collective-permute-done((bf16[64,1408]{1,0:T(8,128)(2,1)S(1)}, bf16[64,1408]{1,0:T(8,128)(2,1)S(1)}, u32[]{:S(2)}, u32[]{:S(2)}) %collective-permute-start.1) | collective-permute-done | bytes 180256 | tf_op jit(solution)/shard_map/ppermute | solution.py:21
  27.1 1.2 %collective-permute-start.4 = (bf16[64,1408]{1,0:T(8,128)(2,1)S(1)}, bf16[64,1408]{1,0:T(8,128)(2,1)S(1)}, u32[]{:S(2)}, u32[]{:S(2)}) collective-permute-start(bf16[64,1408]{1,0:T(8,128)(2,1)S(1)} %collective-permute-done.1.refs_1_), channel_id=1, source_target_pairs={{0,4},{4,0},{8,12},{12,8},{16,20},{20,16},{24,28},{28,24},{1,5},{5... | collective-permute-start | bytes 540680 | tf_op jit(solution)/shard_map/ppermute | solution.py:25
  28.3 0.0 collective-permute-done.2.refs_2_
  28.3 0.0 collective-permute-start.5
  28.3 6.5 %queries.1.q_ref = bf16[512,128]{1,0:T(8,128)(2,1)S(1)} custom-call(bf16[512,5376]{1,0:T(8,128)(2,1)} %x_ref.3, f32[1,5376]{1,0:T(1,128)S(1)} %broadcast_in_dim.3.gain_ref, bf16[5376,128]{1,0:T(8,128)(2,1)S(1)} %copy-done.3, f32[512,128]{1,0:T(8,128)S(1)} %copy-done.4), custom_call_target="tpu_custom_call" | custom-call | flops 704643072 | bytes 6881280 | tf_op jit(solution)/shard_map/queries/pallas_call | solution.py:111
  34.8 0.0 copy-start.1
  34.8 0.0 collective-permute-done.9.v2_ref
  34.8 0.0 collective-permute-done.8.v1_ref
  34.8 1.6 %attention.1.refs_0_ = bf16[128,512]{1,0:T(8,128)(2,1)S(1)} custom-call(bf16[512,128]{1,0:T(8,128)(2,1)S(1)} %queries.1.q_ref, bf16[512,128]{1,0:T(8,128)(2,1)S(1)} %get-tuple-element.13.k0_ref, bf16[512,128]{1,0:T(8,128)(2,1)S(1)} %collective-permute-done.6.k1_ref, bf16[512,128]{1,0:T(8,128)(2,1)S(1)} %collective-permute-done.7.k2_ref, ...), custom_call_target="tpu_custom_call" | custom-call | flops 402653184 | bytes 1048576 | tf_op jit(solution)/shard_map/attention/pallas_call | solution.py:156
  36.4 5.4 %collective-permute-start.12 = (bf16[128,512]{1,0:T(8,128)(2,1)S(1)}, bf16[128,512]{1,0:T(8,128)(2,1)S(1)}, u32[]{:S(2)}, u32[]{:S(2)}) collective-permute-start(bf16[128,512]{1,0:T(8,128)(2,1)S(1)} %attention.1.refs_0_), channel_id=1, source_target_pairs={{0,3},{1,0},{2,1},{3,2},{4,7},{5,4},{6,5},{7,6},{8,11},{9,8},{10,9... | collective-permute-start | bytes 393224 | tf_op jit(solution)/shard_map/ppermute | solution.py:21
  41.8 0.0 collective-permute-start.11
  41.8 0.0 collective-permute-done.3.refs_3_
  41.8 0.6 %collective-permute-start.10 = (bf16[128,512]{1,0:T(8,128)(2,1)S(1)}, bf16[128,512]{1,0:T(8,128)(2,1)S(1)}, u32[]{:S(2)}, u32[]{:S(2)}) collective-permute-start(bf16[128,512]{1,0:T(8,128)(2,1)S(1)} %attention.1.refs_0_), channel_id=1, source_target_pairs={{0,1},{1,2},{2,3},{3,0},{4,5},{5,6},{6,7},{7,4},{8,9},{9,10},{10,1... | collective-permute-start | bytes 393224 | tf_op jit(solution)/shard_map/ppermute | solution.py:21
  42.5 0.0 collective-permute-done.4.refs_4_
  42.5 0.6 %turn_weight.1.weight_ref = bf16[1408,512]{1,0:T(8,128)(2,1)S(1)} custom-call(bf16[128,5376]{1,0:T(8,128)(2,1)S(1)} %copy-done.1, bf16[64,1408]{1,0:T(8,128)(2,1)S(1)} %collective-permute-done.refs_0_, bf16[64,1408]{1,0:T(8,128)(2,1)S(1)} %collective-permute-done.1.refs_1_, bf16[64,1408]{1,0:T(8,128)(2,1)S(1)} %collective-permute-done.2.refs_2_, ...), custom_call_target="tpu_custom_call" | custom-call | bytes 2883584 | tf_op jit(solution)/shard_map/turn_weight/pallas_call | solution.py:274
  43.0 2.7 %collective-permute-done.12.refs_3_ = bf16[128,512]{1,0:T(8,128)(2,1)S(1)} collective-permute-done((bf16[128,512]{1,0:T(8,128)(2,1)S(1)}, bf16[128,512]{1,0:T(8,128)(2,1)S(1)}, u32[]{:S(2)}, u32[]{:S(2)}) %collective-permute-start.12) | collective-permute-done | bytes 131104 | tf_op jit(solution)/shard_map/ppermute | solution.py:21
  45.7 8.2 %collective-permute-done.11.refs_2_ = bf16[128,512]{1,0:T(8,128)(2,1)S(1)} collective-permute-done((bf16[128,512]{1,0:T(8,128)(2,1)S(1)}, bf16[128,512]{1,0:T(8,128)(2,1)S(1)}, u32[]{:S(2)}, u32[]{:S(2)}) %collective-permute-start.11) | collective-permute-done | bytes 131104 | tf_op jit(solution)/shard_map/ppermute | solution.py:21
  53.9 2.3 %output.1 = bf16[1344,512]{1,0:T(8,128)(2,1)} custom-call(bf16[1408,512]{1,0:T(8,128)(2,1)S(1)} %turn_weight.1.weight_ref, bf16[128,512]{1,0:T(8,128)(2,1)S(1)} %attention.1.refs_0_, bf16[128,512]{1,0:T(8,128)(2,1)S(1)} %collective-permute-done.10.refs_1_, bf16[128,512]{1,0:T(8,128)(2,1)S(1)} %collective-permute-done.11.refs_2_, ...), custom_call_target="tpu_custom_call" | custom-call | flops 704643072 | bytes 2752512 | tf_op jit(solution)/shard_map/output/pallas_call | solution.py:284
  (11 shorter events, 0.0 us)
Async XLA Ops:
  0.0 1.3 %copy-start = (bf16[128,5376]{1,0:T(8,128)(2,1)S(1)}, bf16[128,5376]{1,0:T(8,128)(2,1)}, u32[]{:S(2)}) copy-start(bf16[128,5376]{1,0:T(8,128)(2,1)} %weight_ref.5) | copy-start | bytes 4128772
  1.3 4.0 %copy-start.4 = (f32[512,128]{1,0:T(8,128)S(1)}, f32[512,128]{1,0:T(8,128)}, u32[]{:S(2)}) copy-start(f32[512,128]{1,0:T(8,128)} %constant.2.clone.table_ref) | copy-start | bytes 786436
  1.5 17.9 %collective-permute-start = (bf16[64,1408]{1,0:T(8,128)(2,1)S(1)}, bf16[64,1408]{1,0:T(8,128)(2,1)S(1)}, u32[]{:S(2)}, u32[]{:S(2)}) collective-permute-start(bf16[64,1408]{1,0:T(8,128)(2,1)S(1)} %get-tuple-element.10), channel_id=1, source_target_pairs={{0,1},{1,2},{2,3},{3,0},{4,5},{5,6},{6,7},{7,4},{8,9},{9,10},{10,1... | collective-permute-start | bytes 540680 | tf_op jit(solution)/shard_map/ppermute | solution.py:21
  5.3 1.8 %copy-start.2 = (bf16[5376,256]{1,0:T(8,128)(2,1)S(1)}, bf16[5376,256]{1,0:T(8,128)(2,1)}, u32[]{:S(2)}) copy-start(bf16[5376,256]{1,0:T(8,128)(2,1)} %weight_ref.7) | copy-start | bytes 8257540
  7.1 21.2 %copy-start.3 = (bf16[5376,128]{1,0:T(8,128)(2,1)S(1)}, bf16[5376,128]{1,0:T(8,128)(2,1)}, u32[]{:S(2)}) copy-start(bf16[5376,128]{1,0:T(8,128)(2,1)} %weight_ref.6) | copy-start | bytes 4128772
  13.8 6.5 %collective-permute-start.7 = (bf16[512,128]{1,0:T(8,128)(2,1)S(1)}, bf16[512,128]{1,0:T(8,128)(2,1)S(1)}, u32[]{:S(2)}, u32[]{:S(2)}) collective-permute-start(bf16[512,128]{1,0:T(8,128)(2,1)S(1)} %get-tuple-element.13.k0_ref), channel_id=1, source_target_pairs={{0,8},{4,12},{8,16},{12,20},{16,24},{20,28},{24,0},{28,4},{1,9},{5... | collective-permute-start | bytes 393224 | tf_op jit(solution)/shard_map/ppermute | solution.py:21
  15.4 6.5 %collective-permute-start.6 = (bf16[512,128]{1,0:T(8,128)(2,1)S(1)}, bf16[512,128]{1,0:T(8,128)(2,1)S(1)}, u32[]{:S(2)}, u32[]{:S(2)}) collective-permute-start(bf16[512,128]{1,0:T(8,128)(2,1)S(1)} %get-tuple-element.13.k0_ref), channel_id=1, source_target_pairs={{0,4},{4,8},{8,12},{12,16},{16,20},{20,24},{24,28},{28,0},{1,5},{5... | collective-permute-start | bytes 393224 | tf_op jit(solution)/shard_map/ppermute | solution.py:21
  15.4 11.7 %collective-permute-start.1 = (bf16[64,1408]{1,0:T(8,128)(2,1)S(1)}, bf16[64,1408]{1,0:T(8,128)(2,1)S(1)}, u32[]{:S(2)}, u32[]{:S(2)}) collective-permute-start(bf16[64,1408]{1,0:T(8,128)(2,1)S(1)} %get-tuple-element.11), channel_id=1, source_target_pairs={{0,2},{1,3},{2,0},{3,1},{4,6},{5,7},{6,4},{7,5},{8,10},{9,11},{10,... | collective-permute-start | bytes 540680 | tf_op jit(solution)/shard_map/ppermute | solution.py:21
  18.0 10.3 %collective-permute-start.2 = (bf16[64,1408]{1,0:T(8,128)(2,1)S(1)}, bf16[64,1408]{1,0:T(8,128)(2,1)S(1)}, u32[]{:S(2)}, u32[]{:S(2)}) collective-permute-start(bf16[64,1408]{1,0:T(8,128)(2,1)S(1)} %get-tuple-element.12), channel_id=1, source_target_pairs={{0,3},{1,0},{2,1},{3,2},{4,7},{5,4},{6,5},{7,6},{8,11},{9,8},{10,9... | collective-permute-start | bytes 540680 | tf_op jit(solution)/shard_map/ppermute | solution.py:21
  19.3 22.5 %collective-permute-start.3 = (bf16[64,1408]{1,0:T(8,128)(2,1)S(1)}, bf16[64,1408]{1,0:T(8,128)(2,1)S(1)}, u32[]{:S(2)}, u32[]{:S(2)}) collective-permute-start(bf16[64,1408]{1,0:T(8,128)(2,1)S(1)} %collective-permute-done.refs_0_), channel_id=1, source_target_pairs={{0,4},{4,0},{8,12},{12,8},{16,20},{20,16},{24,28},{28,24},{1,5},{5... | collective-permute-start | bytes 540680 | tf_op jit(solution)/shard_map/ppermute | solution.py:25
  20.4 14.4 %collective-permute-start.9 = (bf16[128,512]{1,0:T(8,128)(2,1)S(1)}, bf16[128,512]{1,0:T(8,128)(2,1)S(1)}, u32[]{:S(2)}, u32[]{:S(2)}) collective-permute-start(bf16[128,512]{1,0:T(8,128)(2,1)S(1)} %get-tuple-element.14.v0_ref), channel_id=1, source_target_pairs={{0,8},{4,12},{8,16},{12,20},{16,24},{20,28},{24,0},{28,4},{1,9},{5... | collective-permute-start | bytes 393224 | tf_op jit(solution)/shard_map/ppermute | solution.py:21
  21.9 12.9 %collective-permute-start.8 = (bf16[128,512]{1,0:T(8,128)(2,1)S(1)}, bf16[128,512]{1,0:T(8,128)(2,1)S(1)}, u32[]{:S(2)}, u32[]{:S(2)}) collective-permute-start(bf16[128,512]{1,0:T(8,128)(2,1)S(1)} %get-tuple-element.14.v0_ref), channel_id=1, source_target_pairs={{0,4},{4,8},{8,12},{12,16},{16,20},{20,24},{24,28},{28,0},{1,5},{5... | collective-permute-start | bytes 393224 | tf_op jit(solution)/shard_map/ppermute | solution.py:21
  27.1 15.4 %collective-permute-start.4 = (bf16[64,1408]{1,0:T(8,128)(2,1)S(1)}, bf16[64,1408]{1,0:T(8,128)(2,1)S(1)}, u32[]{:S(2)}, u32[]{:S(2)}) collective-permute-start(bf16[64,1408]{1,0:T(8,128)(2,1)S(1)} %collective-permute-done.1.refs_1_), channel_id=1, source_target_pairs={{0,4},{4,0},{8,12},{12,8},{16,20},{20,16},{24,28},{28,24},{1,5},{5... | collective-permute-start | bytes 540680 | tf_op jit(solution)/shard_map/ppermute | solution.py:25
  28.3 14.2 %collective-permute-start.5 = (bf16[64,1408]{1,0:T(8,128)(2,1)S(1)}, bf16[64,1408]{1,0:T(8,128)(2,1)S(1)}, u32[]{:S(2)}, u32[]{:S(2)}) collective-permute-start(bf16[64,1408]{1,0:T(8,128)(2,1)S(1)} %collective-permute-done.2.refs_2_), channel_id=1, source_target_pairs={{0,4},{4,0},{8,12},{12,8},{16,20},{20,16},{24,28},{28,24},{1,5},{5... | collective-permute-start | bytes 540680 | tf_op jit(solution)/shard_map/ppermute | solution.py:25
  34.8 7.7 %copy-start.1 = (bf16[128,5376]{1,0:T(8,128)(2,1)S(1)}, bf16[128,5376]{1,0:T(8,128)(2,1)}, u32[]{:S(2)}) copy-start(bf16[128,5376]{1,0:T(8,128)(2,1)} %weight_ref.5) | copy-start | bytes 4128772
  36.4 9.3 %collective-permute-start.12 = (bf16[128,512]{1,0:T(8,128)(2,1)S(1)}, bf16[128,512]{1,0:T(8,128)(2,1)S(1)}, u32[]{:S(2)}, u32[]{:S(2)}) collective-permute-start(bf16[128,512]{1,0:T(8,128)(2,1)S(1)} %attention.1.refs_0_), channel_id=1, source_target_pairs={{0,3},{1,0},{2,1},{3,2},{4,7},{5,4},{6,5},{7,6},{8,11},{9,8},{10,9... | collective-permute-start | bytes 393224 | tf_op jit(solution)/shard_map/ppermute | solution.py:21
  41.8 12.1 %collective-permute-start.11 = (bf16[128,512]{1,0:T(8,128)(2,1)S(1)}, bf16[128,512]{1,0:T(8,128)(2,1)S(1)}, u32[]{:S(2)}, u32[]{:S(2)}) collective-permute-start(bf16[128,512]{1,0:T(8,128)(2,1)S(1)} %attention.1.refs_0_), channel_id=1, source_target_pairs={{0,2},{1,3},{2,0},{3,1},{4,6},{5,7},{6,4},{7,5},{8,10},{9,11},{10,... | collective-permute-start | bytes 393224 | tf_op jit(solution)/shard_map/ppermute | solution.py:21
  41.8 12.1 %collective-permute-start.10 = (bf16[128,512]{1,0:T(8,128)(2,1)S(1)}, bf16[128,512]{1,0:T(8,128)(2,1)S(1)}, u32[]{:S(2)}, u32[]{:S(2)}) collective-permute-start(bf16[128,512]{1,0:T(8,128)(2,1)S(1)} %attention.1.refs_0_), channel_id=1, source_target_pairs={{0,1},{1,2},{2,3},{3,0},{4,5},{5,6},{6,7},{7,4},{8,9},{9,10},{10,1... | collective-permute-start | bytes 393224 | tf_op jit(solution)/shard_map/ppermute | solution.py:21

commit v2 on v0

v2 whole, which is shorter than its diff:
```python
import functools
import math

import jax
import jax.numpy as jnp
import numpy as np
from jax import lax
from jax.experimental import pallas as pl
from jax.experimental.pallas import tpu as pltpu
from jax.sharding import PartitionSpec as P

WINDOW = 1024
LANES = 128
MASKED = -1e30
F32 = jnp.float32
BF16 = jnp.bfloat16


def around(block, axis, distance):
    size = lax.axis_size(axis)
    return lax.ppermute(block, axis, [(i, (i + distance) % size) for i in range(size)])


def other_core(block):
    return lax.ppermute(block, "seq", [(i, i ^ 1) for i in range(lax.axis_size("seq"))])


def call(kernel, name, out_shape, vmem=16 * 2**20, flops=1, **kwargs):
    return pl.pallas_call(
        kernel,
        name=name,
        out_shape=out_shape,
        cost_estimate=pl.CostEstimate(flops=flops, bytes_accessed=1, transcendentals=0),
        compiler_params=pltpu.CompilerParams(vmem_limit_bytes=vmem),
        **kwargs,
    )


def matmul(left, right, dims=((1,), (0,))):
    return lax.dot_general(left, right, (dims, ((), ())), preferred_element_type=F32)


def rope_factors(rope_ref, first_pos):
    rows, head = rope_ref.shape[1:]
    half = head // 2
    step = 8

    def turn(count, stride, start):
        lane = lax.broadcasted_iota(jnp.int32, (count, head), 1)
        low = lane < half
        freq = jnp.exp(
            jnp.where(low, lane, lane - half).astype(F32) * (-math.log(10000.0) * 2.0 / head)
        )
        place = lax.broadcasted_iota(jnp.int32, (count, head), 0) * stride + start
        angle = place.astype(F32) * freq
        return jnp.cos(angle), jnp.sin(angle), jnp.where(low, -1.0, 1.0)

    fine_cos, fine_sin, _ = turn(step, 1, 0)
    coarse_cos, coarse_sin, sign = turn(rows // step, step, first_pos)
    for a in range(rows // step):
        span = slice(a * step, (a + 1) * step)
        c, s = coarse_cos[a : a + 1, :], coarse_sin[a : a + 1, :]
        rope_ref[0, span, :] = c * fine_cos - s * fine_sin
        rope_ref[1, span, :] = (s * fine_cos + c * fine_sin) * sign[:step, :]


def rope(tensor, cosine, sine):
    return tensor * cosine + pltpu.roll(tensor, tensor.shape[1] // 2, 1) * sine


def project_kernel(finish, block, ahead, x_ref, gain_ref, weight_ref, out_ref, *scratch):
    x_buf, gain_buf, weight_buf, rope_buf, scaled_ref, total_ref, square_ref, sems = scratch
    rows, width = x_ref.shape
    steps = width // block
    gain_copy = pltpu.make_async_copy(gain_ref, gain_buf, sems.at[2, 0])
    copies = []
    for k in range(steps):
        part = pl.ds(k * block, block)
        copies.append(
            (
                pltpu.make_async_copy(x_ref.at[:, part], x_buf.at[:, part], sems.at[0, k]),
                pltpu.make_async_copy(
                    weight_ref.at[part, :], weight_buf.at[part, :], sems.at[1, k]
                ),
            )
        )
    gain_copy.start()
    for pair in copies[:ahead]:
        for copy in pair:
            copy.start()
    rope_factors(rope_buf, lax.axis_index("seq") * rows)
    gain_copy.wait()
    chunk = 64
    for k in range(steps):
        for copy in copies[k]:
            copy.wait()
        if k + ahead < steps:
            for copy in copies[k + ahead]:
                copy.start()
        for r in range(0, rows, chunk):
            part = None
            for t in range(k * block, (k + 1) * block, LANES):
                x = x_buf[r : r + chunk, t : t + LANES]
                gain = gain_buf[t // LANES : t // LANES + 1, :].astype(BF16)
                scaled_ref[r : r + chunk, t : t + LANES] = x * gain
                square = x * x
                part = square if part is None else part + square
            part = part.astype(F32)
            square_ref[r : r + chunk, :] = part if k == 0 else square_ref[r : r + chunk, :] + part
        span = slice(k * block, (k + 1) * block)
        product = matmul(scaled_ref[:, span], weight_buf[span, :])
        total_ref[...] = product if k == 0 else total_ref[...] + product
    mean = jnp.sum(square_ref[...], axis=1, keepdims=True) * (1.0 / width)
    finish(total_ref, lax.rsqrt(mean + 1e-06), rope_buf, out_ref)


def keys_values_kernel(width, mp, block, ahead, cut, x_ref, gain_ref, weight_ref, *refs):
    out_weight_ref, first_piece_ref, kv_ref, *refs = refs
    pieces, scratch, cut_sems = refs[: len(cut)], refs[len(cut) : -1], refs[-1]
    copies = cut_copies(width, mp, cut, out_weight_ref, pieces, cut_sems)
    finish = functools.partial(finish_keys_values, copies)
    project_kernel(finish, block, ahead, x_ref, gain_ref, weight_ref, kv_ref, *scratch)
    for copy in copies:
        copy.wait()


def finish_keys_values(copies, total_ref, inverse, rope_buf, out_ref):
    for copy in copies:
        copy.start()
    rows = total_ref.shape[0]
    head = total_ref.shape[1] // 2
    keys = total_ref[:, :head] * inverse
    out_ref[:rows, :] = rope(keys, rope_buf[0], rope_buf[1]).astype(BF16)
    for t in range(rows // LANES):
        span = slice(t * LANES, (t + 1) * LANES)
        values = total_ref[span, head:] * inverse[span, :]
        out_ref[rows + t * head : rows + (t + 1) * head, :] = values.T.astype(BF16)


def finish_queries(scale, total_ref, inverse, rope_buf, out_ref):
    queries = rope(total_ref[...] * inverse, rope_buf[0], rope_buf[1])
    out_ref[...] = (queries * scale).astype(BF16)


def queries_kernel(scale, block, ahead, x_ref, gain_ref, weight_ref, first_piece_ref, *refs):
    finish = functools.partial(finish_queries, scale)
    project_kernel(finish, block, ahead, x_ref, gain_ref, weight_ref, *refs)


BLOCK = 768
AHEAD = 4


def project_scratch(rows, width, cols, head):
    return [
        pltpu.VMEM((rows, width), BF16),
        pltpu.VMEM((width // LANES, LANES), F32),
        pltpu.VMEM((width, cols), BF16),
        pltpu.VMEM((2, rows, head), F32),
        pltpu.VMEM((rows, width), BF16),
        pltpu.VMEM((rows, cols), F32),
        pltpu.VMEM((rows, LANES), F32),
        pltpu.SemaphoreType.DMA((3, max(2, width // BLOCK))),
    ]


def values_of(block_ref, rows):
    head = block_ref.shape[1]
    tiles = [block_ref[rows + t * head : rows + (t + 1) * head, :] for t in range(rows // LANES)]
    return jnp.concatenate(tiles, axis=1)


def attention_kernel(q_ref, kv0_ref, kv1_ref, kv2_ref, out_ref):
    rows, head = q_ref.shape
    chunk = min(rows, 256)
    shard = lax.axis_index("seq")
    bias1 = jnp.where(shard < 1, MASKED, 0.0).astype(F32)
    bias2 = jnp.where(shard < 2, MASKED, 0.0).astype(F32)
    nt = ((1,), (1,))
    values = [values_of(ref, rows) for ref in (kv0_ref, kv1_ref, kv2_ref)]
    for start in range(0, rows, chunk):
        span = slice(start, start + chunk)
        q = q_ref[span, :]
        key_index = lax.broadcasted_iota(jnp.int32, (rows, chunk), 0)
        query_index = lax.broadcasted_iota(jnp.int32, (rows, chunk), 1) + start
        own = key_index <= query_index
        near = matmul(kv1_ref[:rows, :], q, nt) + bias1
        far = matmul(kv2_ref[:rows, :], q, nt) + bias2
        mixed = jnp.where(own, matmul(kv0_ref[:rows, :], q, nt), far)
        highest = jnp.maximum(
            jnp.max(near, axis=0, keepdims=True), jnp.max(mixed, axis=0, keepdims=True)
        )
        near = jnp.exp2(near - highest)
        mixed = jnp.exp2(mixed - highest)
        norm = jnp.sum(near, axis=0, keepdims=True) + jnp.sum(mixed, axis=0, keepdims=True)
        out = matmul(values[1], near.astype(BF16))
        out += matmul(values[0], jnp.where(own, mixed, 0.0).astype(BF16))
        out += matmul(values[2], jnp.where(own, 0.0, mixed).astype(BF16))
        out_ref[:, span] = (out * (1.0 / norm)).astype(BF16)


def weight_window(width, mp):
    cols = width // mp
    tiles = max(-(-cols * (m + 1) // LANES) - cols * m // LANES for m in range(mp))
    return cols, tiles


def window_start(m, width, mp):
    cols, tiles = weight_window(width, mp)
    first = jnp.minimum(m * cols // LANES, width // LANES - tiles)
    return pl.multiple_of(first * LANES, LANES)


def cut_copies(width, mp, distances, weight_ref, outs, sems):
    m = lax.axis_index("mp")
    core = lax.axis_index("seq") % 2
    copies = []
    for i, (distance, out) in enumerate(zip(distances, outs)):
        half, window = out.shape
        row = pl.multiple_of(core * half, half)
        start = window_start((m + distance) % mp, width, mp)
        source = weight_ref.at[pl.ds(row, half), pl.ds(start, window)]
        copies.append(pltpu.make_async_copy(source, out, sems.at[i]))
    return copies


def cut_kernel(width, mp, distances, weight_ref, *refs):
    copies = cut_copies(width, mp, distances, weight_ref, refs[:-1], refs[-1])
    for copy in copies:
        copy.start()
    for copy in copies:
        copy.wait()


def turn_kernel(width, mp, weight_ref, *refs):
    pieces, (out_ref, own_ref, sem) = refs[: mp - 1], refs[-3:]
    half, window = own_ref.shape
    (copy,) = cut_copies(width, mp, [0], weight_ref, [own_ref], sem)
    copy.start()
    pair = []
    copy.wait()
    for i, piece in enumerate([own_ref, *pieces]):
        pair.append(piece[...])
        if i % 2:
            out_ref[:, (i - 1) * half : (i + 1) * half] = jnp.concatenate(pair, axis=0).T
            pair = []


def collect_kernel(*refs):
    heads, out_ref = refs[:-1], refs[-1]
    head = heads[0].shape[0]
    half = head // 2
    core = lax.axis_index("seq") % 2
    for i, block in enumerate(heads):
        for place in range(2):
            row = pl.multiple_of((core if place == 0 else 1 - core) * half, half)
            to = (place * len(heads) + i) * half
            out_ref[to : to + half, :] = block[pl.ds(row, half), :]


def output_kernel(width, mp, chunk, mine_ref, theirs_ref, heads_ref, out_ref, buf_ref, sems):
    cols = out_ref.shape[0]
    m = lax.axis_index("mp")
    offset = m * cols - window_start(m, width, mp)
    half = mine_ref.shape[1]
    copies = []
    for i in range(cols // chunk):
        span = pl.ds(i * chunk, chunk)
        rows = pl.ds(pl.multiple_of(offset + i * chunk, 16), chunk)
        total = matmul(mine_ref[rows, :], heads_ref[:half, :])
        total += matmul(theirs_ref[rows, :], heads_ref[half:, :])
        buf_ref[span, :] = total.astype(BF16)
        copies.append(pltpu.make_async_copy(buf_ref.at[span, :], out_ref.at[span, :], sems.at[i]))
        copies[-1].start()
    for copy in copies:
        copy.wait()


def per_device(hidden_in, norm_gain, query_weight, kv_weight, out_weight):
    rows, width = hidden_in.shape
    head = query_weight.shape[1]
    mp = lax.axis_size("mp")
    assert 2 * rows == WINDOW and width % BLOCK == 0 and head == LANES
    cols, tiles = weight_window(width, mp)
    window = tiles * LANES
    half = head // 2
    gain = norm_gain.reshape(width // LANES, LANES)
    hbm = pl.BlockSpec(memory_space=pltpu.HBM)
    vmem = pl.BlockSpec(memory_space=pltpu.VMEM)
    dma = pltpu.SemaphoreType.DMA
    shape = lambda *dims: jax.ShapeDtypeStruct(dims, BF16)
    large = 52 * 2**20

    order = sorted(range(1, mp), key=lambda d: abs(d - mp // 2))
    first, later = order[:1], order[1:]
    pieces = call(
        functools.partial(cut_kernel, width, mp, first),
        "cut_weight",
        [shape(half, window)] * len(first),
        vmem=large,
        in_specs=[hbm],
        out_specs=[vmem] * len(first),
        scratch_shapes=[dma((len(first),))],
    )(out_weight)
    kv, *rest = call(
        functools.partial(keys_values_kernel, width, mp, BLOCK, AHEAD, later),
        "keys_values",
        [shape(2 * rows, head)] + [shape(half, window)] * len(later),
        vmem=large,
        in_specs=[hbm] * 4 + [pl.BlockSpec(memory_space=pl.ANY)],
        out_specs=[vmem] * (1 + len(later)),
        scratch_shapes=project_scratch(rows, width, 2 * head, head) + [dma((len(later),))],
    )(hidden_in, gain, kv_weight, out_weight, pieces[0])
    kv2 = around(kv, "seq", 2)
    kv1 = around(kv, "seq", 1)
    mine = [around(piece, "mp", d) for d, piece in zip(order, list(pieces) + rest)]
    scale = math.log2(math.e) / math.sqrt(168.0)
    queries = call(
        functools.partial(queries_kernel, scale, BLOCK, AHEAD),
        "queries",
        shape(rows, head),
        vmem=large,
        flops=2 * 10**10,
        in_specs=[hbm] * 3 + [pl.BlockSpec(memory_space=pl.ANY)],
        out_specs=vmem,
        scratch_shapes=project_scratch(rows, width, head, head),
    )(hidden_in, gain, query_weight, mine[0])
    head_out = call(
        attention_kernel,
        "attention",
        shape(head, rows),
        in_specs=[vmem] * 4,
        out_specs=vmem,
    )(queries, kv, kv1, kv2)
    heads = [head_out] + [around(head_out, "mp", d) for d in order]

    mine_turned = call(
        functools.partial(turn_kernel, width, mp),
        "turn_weight",
        shape(window, mp * half),
        in_specs=[hbm] + [vmem] * (mp - 1) + [pl.BlockSpec(memory_space=pl.ANY)],
        out_specs=vmem,
        scratch_shapes=[pltpu.VMEM((half, window), BF16), dma((1,))],
    )(out_weight, *mine, head_out)
    theirs_turned = other_core(mine_turned)
    taken = call(
        collect_kernel,
        "collect_heads",
        shape(mp * head, rows),
        flops=3 * 10**10,
        in_specs=[vmem] * mp,
        out_specs=vmem,
    )(*heads)

    chunk = max(c for c in range(16, min(cols, 448) + 1, 16) if cols % c == 0)
    return call(
        functools.partial(output_kernel, width, mp, chunk),
        "output",
        shape(cols, rows),
        in_specs=[vmem] * 3,
        out_specs=hbm,
        scratch_shapes=[pltpu.VMEM((cols, rows), BF16), dma((cols // chunk,))],
    )(mine_turned, theirs_turned, taken)


def solution(mesh):
    in_specs = (P("seq", None), P(), P(None, "mp"), P(None, "mp"), P("mp", None))
    out_specs = P("mp", "seq")
    return jax.shard_map(
        per_device, mesh=mesh, in_specs=in_specs, out_specs=out_specs, check_vma=False
    )
```

time: 64.9 us -> 40.2 us (0.62)
  matrix products: 17.9 us -> 0 us
  blocking collectives: 15.4 us -> 0 us
  Pallas kernels: 0 us -> 14.2 us
  waiting for transfers between devices: 0.27 us -> 11.7 us
  other arithmetic: 9.85 us -> 0 us
  starting transfers between devices: 18.3 us -> 12.6 us
  local copies, waits for them, and re-layouts: 2.67 us -> 1.35 us
    dot_general x5 -> x0, matrix products: 17.9 us -> none  [the longest x1 5.32 us: per_device(): jnp.einsum('rhc,hcd->hdr', shaped, weight_part, preferred_element_type=jn...]
    all_gather x1 -> x0, blocking collectives: 15.4 us -> none  [per_device(): portion = lax.all_gather(outputs, 'mp', axis=1, tiled=True)]
    pallas_call x0 -> x7, Pallas kernels: none -> 14.2 us  [the longest x1 5.44 us: per_device(): call(functools.partial(queries_kernel, scale, BLOCK, AHEAD), 'queries', s...]
    ppermute x4 -> x9, waiting for transfers between devices: 0.26 us -> 11.7 us  [the longest x8 11.7 us: around(): lax.ppermute(block, axis, [(i, (i + distance) % size) for i in range(size)])]
    reduce_sum x3 -> x0, other arithmetic: 9.2 us -> none  [the longest x1 4.9 us: per_device(): summed = jnp.sum(terms.astype(jnp.float32), axis=0)]
    all_to_all x1 -> x0, starting transfers between devices: 6.32 us -> none  [per_device(): lax.all_to_all(out_weight, 'mp', split_axis=1, concat_axis=0, tiled=True)]
    unnamed x5 -> x8, local copies, waits for them, and re-layouts: 2.65 us -> 1.35 us
    ppermute x4 -> x9, starting transfers between devices: 12 us -> 12.6 us  [the longest x8 12.6 us: around(): lax.ppermute(block, axis, [(i, (i + distance) % size) for i in range(size)])]
  transfers between devices with their start and end apart: 5 -> 9, of which waited for: 1 -> 4; matrix products, arithmetic and copies ran while one was open for 27% -> 0% of each run, Pallas kernels for 0% -> 31%
where the time goes in v2:
time: 40.2 us; the launch traced here: 40 us
  Pallas kernels  14.2 us (35%)
  starting transfers between devices  12.6 us (31%)
  waiting for transfers between devices  11.7 us (29%)
  local copies, waits for them, and re-layouts  1.35 us (3%)
    ppermute x8, starting transfers between devices, around(): lax.ppermute(block, axis, [(i, (i + distance) % size) for i in range(size)])  12.6 us
    ppermute x8, waiting for transfers between devices, around(): lax.ppermute(block, axis, [(i, (i + distance) % size) for i in range(size)])  11.7 us
    pallas_call x1, Pallas kernels, per_device(): call(functools.partial(queries_kernel, scale, BLOCK, AHEAD), 'queries', s...  5.44 us
    pallas_call x1, Pallas kernels, per_device(): call(functools.partial(keys_values_kernel, width, mp, BLOCK, AHEAD, later...  5.21 us
    pallas_call x1, Pallas kernels, per_device(): call(functools.partial(output_kernel, width, mp, chunk), 'output', shape(...  1.68 us
    pallas_call x1, Pallas kernels, per_device(): call(attention_kernel, 'attention', shape(head, rows), in_specs=[vmem] *...  1.55 us
    unnamed x8, local copies, waits for them, and re-layouts  1.35 us
  transfers between devices with their start and end apart: 9, of which 4 were waited for; matrix products, arithmetic and copies ran while one was open for 0% of the time, Pallas kernels for 31%

profile of v2, /device:TPU:0, one launch (start us, length us, event | category | flops | bytes accessed | tf_op | source)
XLA Modules:
  0.0 40.0 jit_solution(7654521896791682773)
XLA Ops:
  0.0 0.0 copy-start
  0.0 1.3 %copy-done = bf16[128,5376]{1,0:T(8,128)(2,1)S(1)} copy-done((bf16[128,5376]{1,0:T(8,128)(2,1)S(1)}, bf16[128,5376]{1,0:T(8,128)(2,1)}, u32[]{:S(2)}) %copy-start) | copy-done | bytes 1376280
  1.3 0.0 copy-start.2
  1.4 4.1 %collective-permute-start = (bf16[64,1408]{1,0:T(8,128)(2,1)S(1)}, bf16[64,1408]{1,0:T(8,128)(2,1)S(1)}, u32[]{:S(2)}, u32[]{:S(2)}) collective-permute-start(bf16[64,1408]{1,0:T(8,128)(2,1)S(1)} %cut_weight.1.refs_1_), channel_id=1, source_target_pairs={{0,2},{1,3},{2,0},{3,1},{4,6},{5,7},{6,4},{7,5},{8,10},{9,11},{10,... | collective-permute-start | bytes 540680 | tf_op jit(solution)/shard_map/ppermute | solution.py:21
  5.5 0.0 copy-done.2
  5.5 0.0 copy-start.3
  5.5 5.2 %keys_values.1 = (bf16[1024,128]{1,0:T(8,128)(2,1)S(1)}, bf16[64,1408]{1,0:T(8,128)(2,1)S(1)}, bf16[64,1408]{1,0:T(8,128)(2,1)S(1)}) custom-call(bf16[512,5376]{1,0:T(8,128)(2,1)} %x_ref.3, f32[42,128]{1,0:T(8,128)S(1)} %bitcast.1, bf16[5376,256]{1,0:T(8,128)(2,1)} %weight_ref.5, bf16[128,5376]{1,0:T(8,128)(2,1)} %weight_ref.7, ...), custom_call_target="tpu_custom_call" | custom-call | flops 1 | bytes 1 | tf_op jit(solution)/shard_map/keys_values/pallas_call | solution.py:305
  10.7 1.5 %collective-permute-start.4 = (bf16[1024,128]{1,0:T(8,128)(2,1)S(1)}, bf16[1024,128]{1,0:T(8,128)(2,1)S(1)}, u32[]{:S(2)}, u32[]{:S(2)}) collective-permute-start(bf16[1024,128]{1,0:T(8,128)(2,1)S(1)} %get-tuple-element.10.kv0_ref), channel_id=1, source_target_pairs={{0,8},{4,12},{8,16},{12,20},{16,24},{20,28},{24,0},{28,4},{1,9},{5... | collective-permute-start | bytes 786440 | tf_op jit(solution)/shard_map/ppermute | solution.py:21
  12.2 0.0 collective-permute-start.3
  12.2 1.6 %collective-permute-start.1 = (bf16[64,1408]{1,0:T(8,128)(2,1)S(1)}, bf16[64,1408]{1,0:T(8,128)(2,1)S(1)}, u32[]{:S(2)}, u32[]{:S(2)}) collective-permute-start(bf16[64,1408]{1,0:T(8,128)(2,1)S(1)} %get-tuple-element.8), channel_id=1, source_target_pairs={{0,1},{1,2},{2,3},{3,0},{4,5},{5,6},{6,7},{7,4},{8,9},{9,10},{10,1... | collective-permute-start | bytes 540680 | tf_op jit(solution)/shard_map/ppermute | solution.py:21
  13.8 2.2 %collective-permute-start.2 = (bf16[64,1408]{1,0:T(8,128)(2,1)S(1)}, bf16[64,1408]{1,0:T(8,128)(2,1)S(1)}, u32[]{:S(2)}, u32[]{:S(2)}) collective-permute-start(bf16[64,1408]{1,0:T(8,128)(2,1)S(1)} %get-tuple-element.9), channel_id=1, source_target_pairs={{0,3},{1,0},{2,1},{3,2},{4,7},{5,4},{6,5},{7,6},{8,11},{9,8},{10,9... | collective-permute-start | bytes 540680 | tf_op jit(solution)/shard_map/ppermute | solution.py:21
  16.1 0.0 collective-permute-done.first_piece_ref.refs_0_
  16.1 0.0 copy-done.3
  16.1 0.0 copy-start.1
  16.1 5.4 %queries.1.q_ref = bf16[512,128]{1,0:T(8,128)(2,1)S(1)} custom-call(bf16[512,5376]{1,0:T(8,128)(2,1)} %x_ref.3, f32[42,128]{1,0:T(8,128)S(1)} %bitcast.2, bf16[5376,128]{1,0:T(8,128)(2,1)S(1)} %copy-done.3, bf16[64,1408]{1,0:T(8,128)(2,1)S(1)} %collective-permute-done.first_piece_ref.refs_0_), custom_call_target="tpu_custom_call" | custom-call | flops 20000000000 | bytes 1 | tf_op jit(solution)/shard_map/queries/pallas_call | solution.py:318
  21.5 0.0 collective-permute-done.4.kv2_ref
  21.5 0.7 %collective-permute-done.3.kv1_ref = bf16[1024,128]{1,0:T(8,128)(2,1)S(1)} collective-permute-done((bf16[1024,128]{1,0:T(8,128)(2,1)S(1)}, bf16[1024,128]{1,0:T(8,128)(2,1)S(1)}, u32[]{:S(2)}, u32[]{:S(2)}) %collective-permute-start.3) | collective-permute-done | bytes 262176 | tf_op jit(solution)/shard_map/ppermute | solution.py:21
  22.2 1.5 %attention.1.refs_3_.refs_0_ = bf16[128,512]{1,0:T(8,128)(2,1)S(1)} custom-call(bf16[512,128]{1,0:T(8,128)(2,1)S(1)} %queries.1.q_ref, bf16[1024,128]{1,0:T(8,128)(2,1)S(1)} %get-tuple-element.10.kv0_ref, bf16[1024,128]{1,0:T(8,128)(2,1)S(1)} %collective-permute-done.3.kv1_ref, bf16[1024,128]{1,0:T(8,128)(2,1)S(1)} %collective-permute-done.4.kv2_ref), custom_call_target="tpu_custom_call" | custom-call | flops 1 | bytes 1 | tf_op jit(solution)/shard_map/attention/pallas_call | solution.py:328
  23.8 2.0 %collective-permute-start.8 = (bf16[128,512]{1,0:T(8,128)(2,1)S(1)}, bf16[128,512]{1,0:T(8,128)(2,1)S(1)}, u32[]{:S(2)}, u32[]{:S(2)}) collective-permute-start(bf16[128,512]{1,0:T(8,128)(2,1)S(1)} %attention.1.refs_3_.refs_0_), channel_id=1, source_target_pairs={{0,3},{1,0},{2,1},{3,2},{4,7},{5,4},{6,5},{7,6},{8,11},{9,8},{10,9... | collective-permute-start | bytes 393224 | tf_op jit(solution)/shard_map/ppermute | solution.py:21
  25.8 0.1 collective-permute-start.7
  25.9 1.0 %collective-permute-start.6 = (bf16[128,512]{1,0:T(8,128)(2,1)S(1)}, bf16[128,512]{1,0:T(8,128)(2,1)S(1)}, u32[]{:S(2)}, u32[]{:S(2)}) collective-permute-start(bf16[128,512]{1,0:T(8,128)(2,1)S(1)} %attention.1.refs_3_.refs_0_), channel_id=1, source_target_pairs={{0,2},{1,3},{2,0},{3,1},{4,6},{5,7},{6,4},{7,5},{8,10},{9,11},{10,... | collective-permute-start | bytes 393224 | tf_op jit(solution)/shard_map/ppermute | solution.py:21
  26.9 0.0 collective-permute-done.1.refs_1_
  26.9 0.0 collective-permute-done.2.refs_2_
  26.9 0.0 copy-done.1
  26.9 0.3 turn_weight.1.mine_ref
  27.2 0.1 collective-permute-start.5
  27.3 3.9 %collective-permute-done.8.refs_3_ = bf16[128,512]{1,0:T(8,128)(2,1)S(1)} collective-permute-done((bf16[128,512]{1,0:T(8,128)(2,1)S(1)}, bf16[128,512]{1,0:T(8,128)(2,1)S(1)}, u32[]{:S(2)}, u32[]{:S(2)}) %collective-permute-start.8) | collective-permute-done | bytes 131104 | tf_op jit(solution)/shard_map/ppermute | solution.py:21
  31.2 2.2 %collective-permute-done.7.refs_2_ = bf16[128,512]{1,0:T(8,128)(2,1)S(1)} collective-permute-done((bf16[128,512]{1,0:T(8,128)(2,1)S(1)}, bf16[128,512]{1,0:T(8,128)(2,1)S(1)}, u32[]{:S(2)}, u32[]{:S(2)}) %collective-permute-start.7) | collective-permute-done | bytes 131104 | tf_op jit(solution)/shard_map/ppermute | solution.py:21
  33.4 4.9 %collective-permute-done.6.refs_1_ = bf16[128,512]{1,0:T(8,128)(2,1)S(1)} collective-permute-done((bf16[128,512]{1,0:T(8,128)(2,1)S(1)}, bf16[128,512]{1,0:T(8,128)(2,1)S(1)}, u32[]{:S(2)}, u32[]{:S(2)}) %collective-permute-start.6) | collective-permute-done | bytes 131104 | tf_op jit(solution)/shard_map/ppermute | solution.py:21
  38.3 0.0 collective-permute-done.5.theirs_ref
  38.3 1.7 %output.1 = bf16[1344,512]{1,0:T(8,128)(2,1)} custom-call(bf16[1408,256]{1,0:T(8,128)(2,1)S(1)} %turn_weight.1.mine_ref, bf16[1408,256]{1,0:T(8,128)(2,1)S(1)} %collective-permute-done.5.theirs_ref, bf16[512,512]{1,0:T(8,128)(2,1)S(1)} %collect_heads.1.heads_ref), custom_call_target="tpu_custom_call" | custom-call | flops 1 | bytes 1 | tf_op jit(solution)/shard_map/output/pallas_call | solution.py:356
  (2 shorter events, 0.1 us)
Async XLA Ops:
  0.0 1.3 %copy-start = (bf16[128,5376]{1,0:T(8,128)(2,1)S(1)}, bf16[128,5376]{1,0:T(8,128)(2,1)}, u32[]{:S(2)}) copy-start(bf16[128,5376]{1,0:T(8,128)(2,1)} %weight_ref.7) | copy-start | bytes 4128772
  1.3 4.1 %copy-start.2 = (f32[5376]{0:T(1024)S(1)}, f32[5376]{0:T(1024)}, u32[]{:S(2)}) copy-start(f32[5376]{0:T(1024)} %param.6) | copy-start | bytes 64516
  1.4 14.7 %collective-permute-start = (bf16[64,1408]{1,0:T(8,128)(2,1)S(1)}, bf16[64,1408]{1,0:T(8,128)(2,1)S(1)}, u32[]{:S(2)}, u32[]{:S(2)}) collective-permute-start(bf16[64,1408]{1,0:T(8,128)(2,1)S(1)} %cut_weight.1.refs_1_), channel_id=1, source_target_pairs={{0,2},{1,3},{2,0},{3,1},{4,6},{5,7},{6,4},{7,5},{8,10},{9,11},{10,... | collective-permute-start | bytes 540680 | tf_op jit(solution)/shard_map/ppermute | solution.py:21
  5.5 10.6 %copy-start.3 = (bf16[5376,128]{1,0:T(8,128)(2,1)S(1)}, bf16[5376,128]{1,0:T(8,128)(2,1)}, u32[]{:S(2)}) copy-start(bf16[5376,128]{1,0:T(8,128)(2,1)} %weight_ref.6) | copy-start | bytes 4128772
  10.7 10.8 %collective-permute-start.4 = (bf16[1024,128]{1,0:T(8,128)(2,1)S(1)}, bf16[1024,128]{1,0:T(8,128)(2,1)S(1)}, u32[]{:S(2)}, u32[]{:S(2)}) collective-permute-start(bf16[1024,128]{1,0:T(8,128)(2,1)S(1)} %get-tuple-element.10.kv0_ref), channel_id=1, source_target_pairs={{0,8},{4,12},{8,16},{12,20},{16,24},{20,28},{24,0},{28,4},{1,9},{5... | collective-permute-start | bytes 786440 | tf_op jit(solution)/shard_map/ppermute | solution.py:21
  12.2 10.0 %collective-permute-start.3 = (bf16[1024,128]{1,0:T(8,128)(2,1)S(1)}, bf16[1024,128]{1,0:T(8,128)(2,1)S(1)}, u32[]{:S(2)}, u32[]{:S(2)}) collective-permute-start(bf16[1024,128]{1,0:T(8,128)(2,1)S(1)} %get-tuple-element.10.kv0_ref), channel_id=1, source_target_pairs={{0,4},{4,8},{8,12},{12,16},{16,20},{20,24},{24,28},{28,0},{1,5},{5... | collective-permute-start | bytes 786440 | tf_op jit(solution)/shard_map/ppermute | solution.py:21
  12.2 14.6 %collective-permute-start.1 = (bf16[64,1408]{1,0:T(8,128)(2,1)S(1)}, bf16[64,1408]{1,0:T(8,128)(2,1)S(1)}, u32[]{:S(2)}, u32[]{:S(2)}) collective-permute-start(bf16[64,1408]{1,0:T(8,128)(2,1)S(1)} %get-tuple-element.8), channel_id=1, source_target_pairs={{0,1},{1,2},{2,3},{3,0},{4,5},{5,6},{6,7},{7,4},{8,9},{9,10},{10,1... | collective-permute-start | bytes 540680 | tf_op jit(solution)/shard_map/ppermute | solution.py:21
  13.8 13.1 %collective-permute-start.2 = (bf16[64,1408]{1,0:T(8,128)(2,1)S(1)}, bf16[64,1408]{1,0:T(8,128)(2,1)S(1)}, u32[]{:S(2)}, u32[]{:S(2)}) collective-permute-start(bf16[64,1408]{1,0:T(8,128)(2,1)S(1)} %get-tuple-element.9), channel_id=1, source_target_pairs={{0,3},{1,0},{2,1},{3,2},{4,7},{5,4},{6,5},{7,6},{8,11},{9,8},{10,9... | collective-permute-start | bytes 540680 | tf_op jit(solution)/shard_map/ppermute | solution.py:21
  16.1 10.8 %copy-start.1 = (bf16[128,5376]{1,0:T(8,128)(2,1)S(1)}, bf16[128,5376]{1,0:T(8,128)(2,1)}, u32[]{:S(2)}) copy-start(bf16[128,5376]{1,0:T(8,128)(2,1)} %weight_ref.7) | copy-start | bytes 4128772
  23.8 7.4 %collective-permute-start.8 = (bf16[128,512]{1,0:T(8,128)(2,1)S(1)}, bf16[128,512]{1,0:T(8,128)(2,1)S(1)}, u32[]{:S(2)}, u32[]{:S(2)}) collective-permute-start(bf16[128,512]{1,0:T(8,128)(2,1)S(1)} %attention.1.refs_3_.refs_0_), channel_id=1, source_target_pairs={{0,3},{1,0},{2,1},{3,2},{4,7},{5,4},{6,5},{7,6},{8,11},{9,8},{10,9... | collective-permute-start | bytes 393224 | tf_op jit(solution)/shard_map/ppermute | solution.py:21
  25.8 7.6 %collective-permute-start.7 = (bf16[128,512]{1,0:T(8,128)(2,1)S(1)}, bf16[128,512]{1,0:T(8,128)(2,1)S(1)}, u32[]{:S(2)}, u32[]{:S(2)}) collective-permute-start(bf16[128,512]{1,0:T(8,128)(2,1)S(1)} %attention.1.refs_3_.refs_0_), channel_id=1, source_target_pairs={{0,1},{1,2},{2,3},{3,0},{4,5},{5,6},{6,7},{7,4},{8,9},{9,10},{10,1... | collective-permute-start | bytes 393224 | tf_op jit(solution)/shard_map/ppermute | solution.py:21
  25.9 12.4 %collective-permute-start.6 = (bf16[128,512]{1,0:T(8,128)(2,1)S(1)}, bf16[128,512]{1,0:T(8,128)(2,1)S(1)}, u32[]{:S(2)}, u32[]{:S(2)}) collective-permute-start(bf16[128,512]{1,0:T(8,128)(2,1)S(1)} %attention.1.refs_3_.refs_0_), channel_id=1, source_target_pairs={{0,2},{1,3},{2,0},{3,1},{4,6},{5,7},{6,4},{7,5},{8,10},{9,11},{10,... | collective-permute-start | bytes 393224 | tf_op jit(solution)/shard_map/ppermute | solution.py:21
  27.2 11.1 %collective-permute-start.5 = (bf16[1408,256]{1,0:T(8,128)(2,1)S(1)}, bf16[1408,256]{1,0:T(8,128)(2,1)S(1)}, u32[]{:S(2)}, u32[]{:S(2)}) collective-permute-start(bf16[1408,256]{1,0:T(8,128)(2,1)S(1)} %turn_weight.1.mine_ref), channel_id=1, source_target_pairs={{0,4},{4,0},{8,12},{12,8},{16,20},{20,16},{24,28},{28,24},{1,5},{5... | collective-permute-start | bytes 2162696 | tf_op jit(solution)/shard_map/ppermute | solution.py:25

commit v3 on v2

v3 whole, which is shorter than its diff:
```python
import functools
import math

import jax
import jax.numpy as jnp
import numpy as np
from jax import lax
from jax.experimental import pallas as pl
from jax.experimental.pallas import tpu as pltpu
from jax.sharding import PartitionSpec as P

WINDOW = 1024
LANES = 128
MASKED = -1e30
F32 = jnp.float32
BF16 = jnp.bfloat16


def around(block, axis, distance):
    size = lax.axis_size(axis)
    return lax.ppermute(block, axis, [(i, (i + distance) % size) for i in range(size)])


def other_core(block):
    return lax.ppermute(block, "seq", [(i, i ^ 1) for i in range(lax.axis_size("seq"))])


def next_chip(block):
    return lax.ppermute(block, "seq", [(i, i ^ 2) for i in range(lax.axis_size("seq"))])


def partner(m, distance, mp):
    return m ^ distance if mp == 4 else (m + distance) % mp


def exchanged(block, distance):
    mp = lax.axis_size("mp")
    return lax.ppermute(block, "mp", [(i, partner(i, distance, mp)) for i in range(mp)])


def call(kernel, name, out_shape, vmem=16 * 2**20, flops=1, **kwargs):
    return pl.pallas_call(
        kernel,
        name=name,
        out_shape=out_shape,
        cost_estimate=pl.CostEstimate(flops=flops, bytes_accessed=1, transcendentals=0),
        compiler_params=pltpu.CompilerParams(vmem_limit_bytes=vmem),
        **kwargs,
    )


def matmul(left, right, dims=((1,), (0,))):
    return lax.dot_general(left, right, (dims, ((), ())), preferred_element_type=F32)


def rope_factors(rope_ref, first_pos):
    rows, head = rope_ref.shape[1:]
    half = head // 2
    step = 8

    def turn(count, stride, start):
        lane = lax.broadcasted_iota(jnp.int32, (count, head), 1)
        low = lane < half
        freq = jnp.exp(
            jnp.where(low, lane, lane - half).astype(F32) * (-math.log(10000.0) * 2.0 / head)
        )
        place = lax.broadcasted_iota(jnp.int32, (count, head), 0) * stride + start
        angle = place.astype(F32) * freq
        return jnp.cos(angle), jnp.sin(angle), jnp.where(low, -1.0, 1.0)

    fine_cos, fine_sin, _ = turn(step, 1, 0)
    coarse_cos, coarse_sin, sign = turn(rows // step, step, first_pos)
    for a in range(rows // step):
        span = slice(a * step, (a + 1) * step)
        c, s = coarse_cos[a : a + 1, :], coarse_sin[a : a + 1, :]
        rope_ref[0, span, :] = c * fine_cos - s * fine_sin
        rope_ref[1, span, :] = (s * fine_cos + c * fine_sin) * sign[:step, :]


def rope(tensor, cosine, sine):
    return tensor * cosine + pltpu.roll(tensor, tensor.shape[1] // 2, 1) * sine


def project_kernel(blocks, ahead, x_ref, gain_ref, weight_refs, *scratch):
    x_buf, weight_buf, rope_buf, scaled_ref, total_ref, square_ref, sems = scratch
    rows, width = x_ref.shape
    copies = []
    ends = [sum(blocks[: k + 1]) for k in range(len(blocks))]
    for k, (size, end) in enumerate(zip(blocks, ends)):
        part = pl.ds(end - size, size)
        group = [pltpu.make_async_copy(x_ref.at[:, part], x_buf.at[:, part], sems.at[0, k])]
        first = 0
        for i, weight_ref in enumerate(weight_refs):
            to = weight_buf.at[part, pl.ds(first, weight_ref.shape[1])]
            group.append(pltpu.make_async_copy(weight_ref.at[part, :], to, sems.at[1 + i, k]))
            first += weight_ref.shape[1]
        copies.append(group)
    for pair in copies[:ahead]:
        for copy in pair:
            copy.start()
    rope_factors(rope_buf, lax.axis_index("seq") * rows)
    chunk = 64
    for k, (size, end) in enumerate(zip(blocks, ends)):
        for copy in copies[k]:
            copy.wait()
        if k + ahead < len(blocks):
            for copy in copies[k + ahead]:
                copy.start()
        for r in range(0, rows, chunk):
            part = None
            for t in range(end - size, end, LANES):
                x = x_buf[r : r + chunk, t : t + LANES]
                gain = gain_ref[t // LANES : t // LANES + 1, :].astype(BF16)
                scaled_ref[r : r + chunk, t : t + LANES] = x * gain
                square = x * x
                part = square if part is None else part + square
            part = part.astype(F32)
            square_ref[r : r + chunk, :] = part if k == 0 else square_ref[r : r + chunk, :] + part
        span = slice(end - size, end)
        product = matmul(scaled_ref[:, span], weight_buf[span, :])
        total_ref[...] = product if k == 0 else total_ref[...] + product
    mean = jnp.sum(square_ref[...], axis=1, keepdims=True) * (1.0 / width)
    return lax.rsqrt(mean + 1e-06)


def project_all_kernel(scale, width, mp, blocks, ahead, cut, x_ref, gain_ref, *refs):
    kv_weight_ref, query_weight_ref, out_weight_ref, *refs = refs
    queries_ref, kv_ref, *refs = refs
    pieces, scratch, cut_sems = refs[: len(cut)], refs[len(cut) : -1], refs[-1]
    copies = cut_copies(width, mp, cut, out_weight_ref, pieces, cut_sems)
    for copy in copies:
        copy.start()
    weights = (kv_weight_ref, query_weight_ref)
    inverse = project_kernel(blocks, ahead, x_ref, gain_ref, weights, *scratch)
    rope_buf, total_ref = scratch[2], scratch[4]
    rows, head = queries_ref.shape
    cosine, sine = rope_buf[0], rope_buf[1]
    kv_ref[:rows, :] = rope(total_ref[:, :head] * inverse, cosine, sine).astype(BF16)
    for t in range(rows // LANES):
        span = slice(t * LANES, (t + 1) * LANES)
        values = total_ref[span, head : 2 * head] * inverse[span, :]
        kv_ref[rows + t * head : rows + (t + 1) * head, :] = values.T.astype(BF16)
    queries = rope(total_ref[:, 2 * head :] * (inverse * scale), cosine, sine)
    queries_ref[...] = queries.astype(BF16)
    for copy in copies:
        copy.wait()


BLOCKS = (1280, 1280, 1280, 1024, 512)
AHEAD = 4
MIXED_COST = 10**11


def project_scratch(rows, width, cols, head):
    return [
        pltpu.VMEM((rows, width), BF16),
        pltpu.VMEM((width, cols), BF16),
        pltpu.VMEM((2, rows, head), F32),
        pltpu.VMEM((rows, width), BF16),
        pltpu.VMEM((rows, cols), F32),
        pltpu.VMEM((rows, LANES), F32),
        pltpu.SemaphoreType.DMA((3, len(BLOCKS))),
    ]


def values_of(block_ref, start):
    head = block_ref.shape[1]
    tiles = [block_ref[r : r + head, :] for r in range(start, block_ref.shape[0], head)]
    return jnp.concatenate(tiles, axis=1)


def pass_kernel(own_ref, far_ref, keys_ref, values_ref):
    core = lax.axis_index("seq") % 2
    rows = keys_ref.shape[0]
    keys_ref[...] = jnp.where(core == 0, own_ref[:rows, :], far_ref[:rows, :])
    values_ref[...] = jnp.where(core == 0, own_ref[rows:, :], far_ref[rows:, :])


NT = ((1,), (1,))


def mixed_kernel(q_ref, own_ref, far_ref, out_ref, stats_ref):
    rows = q_ref.shape[0]
    chunk = min(rows, 256)
    bias = jnp.where(lax.axis_index("seq") < 2, MASKED, 0.0).astype(F32)
    own_values, far_values = values_of(own_ref, rows), values_of(far_ref, rows)
    for start in range(0, rows, chunk):
        span = slice(start, start + chunk)
        q = q_ref[span, :]
        key_index = lax.broadcasted_iota(jnp.int32, (rows, chunk), 0)
        query_index = lax.broadcasted_iota(jnp.int32, (rows, chunk), 1) + start
        own = key_index <= query_index
        far = matmul(far_ref[:rows, :], q, NT) + bias
        scores = jnp.where(own, matmul(own_ref[:rows, :], q, NT), far)
        highest = jnp.max(scores, axis=0, keepdims=True)
        expo = jnp.exp2(scores - highest)
        stats_ref[0:1, span] = highest
        stats_ref[1:2, span] = jnp.sum(expo, axis=0, keepdims=True)
        out = matmul(own_values, jnp.where(own, expo, 0.0).astype(BF16))
        out_ref[:, span] = out + matmul(far_values, jnp.where(own, 0.0, expo).astype(BF16))


def near_kernel(q_ref, keys_ref, values_ref, mixed_ref, stats_ref, out_ref):
    rows = q_ref.shape[0]
    chunk = min(rows, 256)
    bias = jnp.where(lax.axis_index("seq") < 1, MASKED, 0.0).astype(F32)
    values = values_of(values_ref, 0)
    for start in range(0, rows, chunk):
        span = slice(start, start + chunk)
        scores = matmul(keys_ref[...], q_ref[span, :], NT) + bias
        before = stats_ref[0:1, span]
        highest = jnp.maximum(before, jnp.max(scores, axis=0, keepdims=True))
        expo = jnp.exp2(scores - highest)
        scale = jnp.exp2(before - highest)
        norm = stats_ref[1:2, span] * scale + jnp.sum(expo, axis=0, keepdims=True)
        out = mixed_ref[:, span] * scale + matmul(values, expo.astype(BF16))
        out_ref[:, span] = (out * (1.0 / norm)).astype(BF16)


def weight_window(width, mp):
    cols = width // mp
    tiles = max(-(-cols * (m + 1) // LANES) - cols * m // LANES for m in range(mp))
    return cols, tiles


def window_start(m, width, mp):
    cols, tiles = weight_window(width, mp)
    first = jnp.minimum(m * cols // LANES, width // LANES - tiles)
    return first * LANES


def cut_copies(width, mp, distances, weight_ref, outs, sems):
    m = lax.axis_index("mp")
    place = lax.axis_index("seq")
    half = weight_ref.shape[0] // 2
    copies = []
    for i, (distance, out) in enumerate(zip(distances, outs)):
        count, window = out.shape
        row = place % 2 * half + place // 2 % 2 * (half - count)
        start = window_start(partner(m, distance, mp), width, mp)
        source = weight_ref.at[
            pl.ds(pl.multiple_of(row, 16), count), pl.ds(pl.multiple_of(start, LANES), window)
        ]
        copies.append(pltpu.make_async_copy(source, out, sems.at[i]))
    return copies


def turn_kernel(width, mp, split, *refs):
    pieces, (weight_ref, out_ref, own_ref, sem) = list(refs[:-5]), refs[-4:]
    half, window = own_ref.shape
    (copy,) = cut_copies(width, mp, [0], weight_ref, [own_ref], sem)
    copy.start()
    chip = lax.axis_index("seq") // 2 % 2
    copy.wait()
    blocks = {-1: own_ref[...]}
    for i in sorted(range(mp - 1), key=lambda i: not split[i]):
        block = pieces.pop(0)[...]
        if split[i]:
            other = pieces.pop(0)[...]
            low = jnp.where(chip == 0, block, other)
            high = jnp.where(chip == 0, other, block)
            block = jnp.concatenate([low, high], axis=0)
        blocks[i] = block
    for i in range(0, mp, 2):
        pair = jnp.concatenate([blocks[i - 1], blocks[i]], axis=0)
        out_ref[:, i * half : (i + 2) * half] = pair.T


def collect_kernel(pairs, *refs):
    heads, out_ref = refs[:-1], refs[-1]
    head, rows = heads[0].shape
    half = head // 2
    core = lax.axis_index("seq") % 2
    for place in range(2):
        row = pl.multiple_of((core if place == 0 else 1 - core) * half, half)
        for i in range(pairs):
            to = (place * pairs + i) * half
            if i < len(heads):
                out_ref[to : to + half, :] = heads[i][pl.ds(row, half), :]
            else:
                out_ref[to : to + half, :] = jnp.zeros((half, rows), BF16)


def first_heads_kernel(mine_ref, theirs_ref, heads_ref, out_ref):
    half = mine_ref.shape[1]
    chunk = max(c for c in range(16, 513, 16) if mine_ref.shape[0] % c == 0)
    for start in range(0, mine_ref.shape[0], chunk):
        span = slice(start, start + chunk)
        total = matmul(mine_ref[span, :], heads_ref[:half, :])
        out_ref[span, :] = total + matmul(theirs_ref[span, :], heads_ref[half:, :])


def output_kernel(width, mp, chunk, mine_ref, theirs_ref, first_ref, last_ref, *refs):
    out_ref, heads_ref, buf_ref, sems = refs
    cols = out_ref.shape[0]
    head = last_ref.shape[0]
    half = head // 2
    m = lax.axis_index("mp")
    offset = m * cols - window_start(m, width, mp)
    core = lax.axis_index("seq") % 2
    heads_ref[...] = jnp.zeros_like(heads_ref)
    for place in range(2):
        row = pl.multiple_of((core if place == 0 else 1 - core) * half, half)
        heads_ref[place * head + half : (place + 1) * head, :] = last_ref[pl.ds(row, half), :]
    copies = []
    for i in range(cols // chunk):
        span = pl.ds(i * chunk, chunk)
        rows = pl.ds(pl.multiple_of(offset + i * chunk, 16), chunk)
        weight = jnp.concatenate([mine_ref[rows, -LANES:], theirs_ref[rows, -LANES:]], axis=1)
        total = first_ref[rows, :] + matmul(weight, heads_ref[...])
        buf_ref[span, :] = total.astype(BF16)
        copies.append(pltpu.make_async_copy(buf_ref.at[span, :], out_ref.at[span, :], sems.at[i]))
        copies[-1].start()
    for copy in copies:
        copy.wait()


def per_device(hidden_in, norm_gain, query_weight, kv_weight, out_weight):
    rows, width = hidden_in.shape
    head = query_weight.shape[1]
    mp = lax.axis_size("mp")
    assert 2 * rows == WINDOW and width == sum(BLOCKS) and head == LANES
    cols, tiles = weight_window(width, mp)
    window = tiles * LANES
    half = head // 2
    gain = norm_gain.reshape(width // LANES, LANES)
    anywhere = pl.BlockSpec(memory_space=pl.ANY)
    hbm = pl.BlockSpec(memory_space=pltpu.HBM)
    vmem = pl.BlockSpec(memory_space=pltpu.VMEM)
    dma = pltpu.SemaphoreType.DMA
    shape = lambda *dims: jax.ShapeDtypeStruct(dims, BF16)
    large = 52 * 2**20

    order = [2, 1, 3] if mp == 4 else list(range(1, mp))
    split = [mp == 4 and d > 1 for d in order]
    counts = [half // 2 if in_two else half for in_two in split]
    scale = math.log2(math.e) / math.sqrt(168.0)
    queries, kv, *pieces = call(
        functools.partial(project_all_kernel, scale, width, mp, BLOCKS, AHEAD, order),
        "project",
        [shape(rows, head), shape(2 * rows, head)] + [shape(c, window) for c in counts],
        vmem=large,
        in_specs=[hbm, vmem, hbm, hbm, hbm],
        out_specs=[vmem] * (2 + len(order)),
        scratch_shapes=project_scratch(rows, width, 3 * head, head) + [dma((len(order),))],
    )(hidden_in, gain, kv_weight, query_weight, out_weight)
    far = around(kv, "seq", 2)
    mine = [exchanged(piece, d) for d, piece in zip(order, pieces)]
    passed = call(
        pass_kernel,
        "pass_on",
        [shape(rows, head), shape(rows, head)],
        in_specs=[vmem] * 2,
        out_specs=[vmem] * 2,
    )(kv, far)
    near = [other_core(block) for block in passed]
    mixed, stats = call(
        mixed_kernel,
        "mixed_blocks",
        [jax.ShapeDtypeStruct((head, rows), F32), jax.ShapeDtypeStruct((2, rows), F32)],
        flops=MIXED_COST,
        in_specs=[vmem] * 3,
        out_specs=[vmem] * 2,
    )(queries, kv, far)
    head_out = call(
        near_kernel,
        "near_block",
        shape(head, rows),
        in_specs=[vmem] * 5,
        out_specs=vmem,
    )(queries, *near, mixed, stats)
    heads = [head_out] + [exchanged(head_out, d) for d in order[:-1]]
    if mp == 4:
        last_head = exchanged(heads[1], 1)
    else:
        last_head = exchanged(head_out, order[-1])

    parts = []
    for i in sorted(range(mp - 1), key=lambda i: not split[i]):
        parts += [mine[i], next_chip(mine[i])] if split[i] else [mine[i]]
    mine_turned = call(
        functools.partial(turn_kernel, width, mp, split),
        "turn_weight",
        shape(window, mp * half),
        in_specs=[vmem] * len(parts) + [anywhere, hbm],
        out_specs=vmem,
        scratch_shapes=[pltpu.VMEM((half, window), BF16), dma((1,))],
    )(*parts, head_out, out_weight)
    theirs_turned = other_core(mine_turned)
    taken = call(
        functools.partial(collect_kernel, mp),
        "collect_heads",
        shape(mp * head, rows),
        flops=3 * 10**10,
        in_specs=[vmem] * (mp - 1),
        out_specs=vmem,
    )(*heads)
    first_sum = call(
        first_heads_kernel,
        "first_heads",
        jax.ShapeDtypeStruct((window, rows), F32),
        in_specs=[vmem] * 3,
        out_specs=vmem,
    )(mine_turned, theirs_turned, taken)

    chunk = max(c for c in range(16, min(cols, 448) + 1, 16) if cols % c == 0)
    return call(
        functools.partial(output_kernel, width, mp, chunk),
        "output",
        shape(cols, rows),
        in_specs=[vmem] * 4,
        out_specs=hbm,
        scratch_shapes=[
            pltpu.VMEM((2 * head, rows), BF16),
            pltpu.VMEM((cols, rows), BF16),
            dma((cols // chunk,)),
        ],
    )(mine_turned, theirs_turned, first_sum, last_head)


def solution(mesh):
    in_specs = (P("seq", None), P(), P(None, "mp"), P(None, "mp"), P("mp", None))
    out_specs = P("mp", "seq")
    return jax.shard_map(
        per_device, mesh=mesh, in_specs=in_specs, out_specs=out_specs, check_vma=False
    )
```

time: 40.2 us -> 37.2 us (0.925)
  Pallas kernels: 14.2 us -> 9.79 us
  starting transfers between devices: 12.6 us -> 14.8 us
  local copies, waits for them, and re-layouts: 1.35 us -> 0.74 us
    ppermute x0 -> x8, starting transfers between devices: none -> 11.1 us  [the longest x6 9.11 us: exchanged(): lax.ppermute(block, 'mp', [(i, partner(i, distance, mp)) for i in range(m...]
    ppermute x8 -> x1, starting transfers between devices: 12.6 us -> 2.99 us  [around(): lax.ppermute(block, axis, [(i, (i + distance) % size) for i in range(size)])]
    ppermute x8 -> x1, waiting for transfers between devices: 11.7 us -> 3.09 us  [around(): lax.ppermute(block, axis, [(i, (i + distance) % size) for i in range(size)])]
    ppermute x0 -> x8, waiting for transfers between devices: none -> 6.96 us  [the longest x2 4.12 us: next_chip(): lax.ppermute(block, 'seq', [(i, i ^ 2) for i in range(lax.axis_size('seq'...]
    pallas_call x6 -> x7, Pallas kernels: 12.6 us -> 8.41 us  [the longest x1 5.13 us: per_device(): call(functools.partial(project_all_kernel, scale, width, mp, BLOCKS, AHEA...]
    ppermute x1 -> x3, waiting for transfers between devices: 0.01 us -> 1.6 us  [other_core(): lax.ppermute(block, 'seq', [(i, i ^ 1) for i in range(lax.axis_size('seq'...]
    unnamed x8 -> x4, local copies, waits for them, and re-layouts: 1.35 us -> 0.74 us
    ppermute x1 -> x3, starting transfers between devices: 0.07 us -> 0.64 us  [other_core(): lax.ppermute(block, 'seq', [(i, i ^ 1) for i in range(lax.axis_size('seq'...]
  transfers between devices with their start and end apart: 9 -> 12, of which waited for: 4 -> 5; matrix products, arithmetic and copies ran while one was open for 0% -> 0% of each run, Pallas kernels for 31% -> 9%
where the time goes in v3:
time: 37.2 us; the launch traced here: 37.1 us
  starting transfers between devices  14.8 us (40%)
  waiting for transfers between devices  11.7 us (31%)
  Pallas kernels  9.79 us (26%)
  local copies, waits for them, and re-layouts  0.74 us (2%)
    ppermute x6, starting transfers between devices, exchanged(): lax.ppermute(block, 'mp', [(i, partner(i, distance, mp)) for i in range(m...  9.11 us
    pallas_call x1, Pallas kernels, per_device(): call(functools.partial(project_all_kernel, scale, width, mp, BLOCKS, AHEA...  5.13 us
    ppermute x2, waiting for transfers between devices, next_chip(): lax.ppermute(block, 'seq', [(i, i ^ 2) for i in range(lax.axis_size('seq'...  4.12 us
    ppermute x1, waiting for transfers between devices, around(): lax.ppermute(block, axis, [(i, (i + distance) % size) for i in range(size)])  3.09 us
    ppermute x1, starting transfers between devices, around(): lax.ppermute(block, axis, [(i, (i + distance) % size) for i in range(size)])  2.99 us
    ppermute x6, waiting for transfers between devices, exchanged(): lax.ppermute(block, 'mp', [(i, partner(i, distance, mp)) for i in range(m...  2.84 us
    ppermute x2, starting transfers between devices, next_chip(): lax.ppermute(block, 'seq', [(i, i ^ 2) for i in range(lax.axis_size('seq'...  2.03 us
    ppermute x3, waiting for transfers between devices, other_core(): lax.ppermute(block, 'seq', [(i, i ^ 1) for i in range(lax.axis_size('seq'...  1.6 us
  transfers between devices with their start and end apart: 12, of which 5 were waited for; matrix products, arithmetic and copies ran while one was open for 0% of the time, Pallas kernels for 9%

profile of v3, /device:TPU:0, one launch (start us, length us, event | category | flops | bytes accessed | tf_op | source)
XLA Modules:
  0.0 37.1 jit_solution(6835087220578735352)
XLA Ops:
  0.0 0.7 %copy-done.1 = f32[5376]{0:T(1024)S(1)} copy-done((f32[5376]{0:T(1024)S(1)}, f32[5376]{0:T(1024)}, u32[]{:S(2)}) %copy-start.1) | copy-done | bytes 21528
  0.7 5.1 %project.1 = (bf16[512,128]{1,0:T(8,128)(2,1)S(1)}, bf16[1024,128]{1,0:T(8,128)(2,1)S(1)}, bf16[32,1408]{1,0:T(8,128)(2,1)S(1)}, bf16[64,1408]{1,0:T(8,128)(2,1)S(1)}, bf16[32,1408]{1,0:T(8,128)(2,1)S(1)}) custom-call(bf16[512,5376]{1,0:T(8,128)(2,1)} %x_ref.1, f32[42,128]{1,0:T(8,128)S(1)} %bitcast.1, bf16[5376,256]{1,0:T(8,128)(2,1)} %refs_0_.1, ...), custom_call_target="tpu_custom_call" | custom-call | flops 1 | bytes 1 | tf_op jit(solution)/shard_map/project/pallas_call | solution.py:338
  5.9 3.0 %collective-permute-start.5 = (bf16[1024,128]{1,0:T(8,128)(2,1)S(1)}, bf16[1024,128]{1,0:T(8,128)(2,1)S(1)}, u32[]{:S(2)}, u32[]{:S(2)}) collective-permute-start(bf16[1024,128]{1,0:T(8,128)(2,1)S(1)} %get-tuple-element.18.own_ref), channel_id=1, source_target_pairs={{0,8},{4,12},{8,16},{12,20},{16,24},{20,28},{24,0},{28,4},{1,9},{5... | collective-permute-start | bytes 786440 | tf_op jit(solution)/shard_map/ppermute | solution.py:21
  8.9 2.6 %collective-permute-start = (bf16[32,1408]{1,0:T(8,128)(2,1)S(1)}, bf16[32,1408]{1,0:T(8,128)(2,1)S(1)}, u32[]{:S(2)}, u32[]{:S(2)}) collective-permute-start(bf16[32,1408]{1,0:T(8,128)(2,1)S(1)} %get-tuple-element.14), channel_id=1, source_target_pairs={{0,2},{1,3},{2,0},{3,1},{4,6},{5,7},{6,4},{7,5},{8,10},{9,11},{10,... | collective-permute-start | bytes 270344 | tf_op jit(solution)/shard_map/ppermute | solution.py:38
  11.5 1.3 %collective-permute-start.2 = (bf16[32,1408]{1,0:T(8,128)(2,1)S(1)}, bf16[32,1408]{1,0:T(8,128)(2,1)S(1)}, u32[]{:S(2)}, u32[]{:S(2)}) collective-permute-start(bf16[32,1408]{1,0:T(8,128)(2,1)S(1)} %get-tuple-element.15), channel_id=1, source_target_pairs={{0,3},{1,2},{2,1},{3,0},{4,7},{5,6},{6,5},{7,4},{8,11},{9,10},{10,... | collective-permute-start | bytes 270344 | tf_op jit(solution)/shard_map/ppermute | solution.py:38
  12.8 0.2 collective-permute-start.4
  13.0 3.1 %collective-permute-done.5.far_ref = bf16[1024,128]{1,0:T(8,128)(2,1)S(1)} collective-permute-done((bf16[1024,128]{1,0:T(8,128)(2,1)S(1)}, bf16[1024,128]{1,0:T(8,128)(2,1)S(1)}, u32[]{:S(2)}, u32[]{:S(2)}) %collective-permute-start.5) | collective-permute-done | bytes 262176 | tf_op jit(solution)/shard_map/ppermute | solution.py:21
  16.1 0.1 pass_on.1
  16.2 0.1 collective-permute-start.6
  16.3 0.5 %collective-permute-start.7 = (bf16[512,128]{1,0:T(8,128)(2,1)S(1)}, bf16[512,128]{1,0:T(8,128)(2,1)S(1)}, u32[]{:S(2)}, u32[]{:S(2)}) collective-permute-start(bf16[512,128]{1,0:T(8,128)(2,1)S(1)} %get-tuple-element.20), channel_id=1, source_target_pairs={{0,4},{4,0},{8,12},{12,8},{16,20},{20,16},{24,28},{28,24},{1,5},{5... | collective-permute-start | bytes 393224 | tf_op jit(solution)/shard_map/ppermute | solution.py:25
  16.8 1.1 %mixed_blocks.1 = (f32[128,512]{1,0:T(8,128)S(1)}, f32[2,512]{1,0:T(2,128)S(1)}) custom-call(bf16[512,128]{1,0:T(8,128)(2,1)S(1)} %get-tuple-element.17.q_ref, bf16[1024,128]{1,0:T(8,128)(2,1)S(1)} %get-tuple-element.18.own_ref, bf16[1024,128]{1,0:T(8,128)(2,1)S(1)} %collective-permute-done.5.far_ref), custom_call_target="tpu_custom_call" | custom-call | flops 99999997952 | bytes 1 | tf_op jit(solution)/shard_map/mixed_blocks/pallas_call | solution.py:357
  17.9 0.0 collective-permute-done.6.keys_ref
  17.9 0.0 collective-permute-done.7.values_ref
  17.9 0.9 %near_block.1.refs_5_.refs_0_ = bf16[128,512]{1,0:T(8,128)(2,1)S(1)} custom-call(bf16[512,128]{1,0:T(8,128)(2,1)S(1)} %get-tuple-element.17.q_ref, bf16[512,128]{1,0:T(8,128)(2,1)S(1)} %collective-permute-done.6.keys_ref, bf16[512,128]{1,0:T(8,128)(2,1)S(1)} %collective-permute-done.7.values_ref, f32[128,512]{1,0:T(8,128)S(1)} %get-tuple-element.21.mixed_ref, ...), custom_call_target="tpu_custom_call" | custom-call | flops 1 | bytes 1 | tf_op jit(solution)/shard_map/near_block/pallas_call | solution.py:365
  18.8 2.8 %collective-permute-start.9 = (bf16[128,512]{1,0:T(8,128)(2,1)S(1)}, bf16[128,512]{1,0:T(8,128)(2,1)S(1)}, u32[]{:S(2)}, u32[]{:S(2)}) collective-permute-start(bf16[128,512]{1,0:T(8,128)(2,1)S(1)} %near_block.1.refs_5_.refs_0_), channel_id=1, source_target_pairs={{0,2},{1,3},{2,0},{3,1},{4,6},{5,7},{6,4},{7,5},{8,10},{9,11},{10,... | collective-permute-start | bytes 393224 | tf_op jit(solution)/shard_map/ppermute | solution.py:38
  21.6 1.6 %collective-permute-start.10 = (bf16[128,512]{1,0:T(8,128)(2,1)S(1)}, bf16[128,512]{1,0:T(8,128)(2,1)S(1)}, u32[]{:S(2)}, u32[]{:S(2)}) collective-permute-start(bf16[128,512]{1,0:T(8,128)(2,1)S(1)} %near_block.1.refs_5_.refs_0_), channel_id=1, source_target_pairs={{0,1},{1,0},{2,3},{3,2},{4,5},{5,4},{6,7},{7,6},{8,9},{9,8},{10,11... | collective-permute-start | bytes 393224 | tf_op jit(solution)/shard_map/ppermute | solution.py:38
  23.2 0.0 collective-permute-done.refs_0_
  23.2 0.6 %collective-permute-start.1 = (bf16[32,1408]{1,0:T(8,128)(2,1)S(1)}, bf16[32,1408]{1,0:T(8,128)(2,1)S(1)}, u32[]{:S(2)}, u32[]{:S(2)}) collective-permute-start(bf16[32,1408]{1,0:T(8,128)(2,1)S(1)} %collective-permute-done.refs_0_), channel_id=1, source_target_pairs={{0,8},{4,12},{8,0},{12,4},{16,24},{20,28},{24,16},{28,20},{1,9},{5... | collective-permute-start | bytes 270344 | tf_op jit(solution)/shard_map/ppermute | solution.py:29
  23.8 0.0 collective-permute-done.2.refs_2_
  23.8 1.4 %collective-permute-start.3 = (bf16[32,1408]{1,0:T(8,128)(2,1)S(1)}, bf16[32,1408]{1,0:T(8,128)(2,1)S(1)}, u32[]{:S(2)}, u32[]{:S(2)}) collective-permute-start(bf16[32,1408]{1,0:T(8,128)(2,1)S(1)} %collective-permute-done.2.refs_2_), channel_id=1, source_target_pairs={{0,8},{4,12},{8,0},{12,4},{16,24},{20,28},{24,16},{28,20},{1,9},{5... | collective-permute-start | bytes 270344 | tf_op jit(solution)/shard_map/ppermute | solution.py:29
  25.3 3.2 %collective-permute-done.1.refs_1_ = bf16[32,1408]{1,0:T(8,128)(2,1)S(1)} collective-permute-done((bf16[32,1408]{1,0:T(8,128)(2,1)S(1)}, bf16[32,1408]{1,0:T(8,128)(2,1)S(1)}, u32[]{:S(2)}, u32[]{:S(2)}) %collective-permute-start.1) | collective-permute-done | bytes 90144 | tf_op jit(solution)/shard_map/ppermute | solution.py:29
  28.4 1.0 %collective-permute-done.3.refs_3_ = bf16[32,1408]{1,0:T(8,128)(2,1)S(1)} collective-permute-done((bf16[32,1408]{1,0:T(8,128)(2,1)S(1)}, bf16[32,1408]{1,0:T(8,128)(2,1)S(1)}, u32[]{:S(2)}, u32[]{:S(2)}) %collective-permute-start.3) | collective-permute-done | bytes 90144 | tf_op jit(solution)/shard_map/ppermute | solution.py:29
  29.4 0.0 collective-permute-done.4.refs_4_
  29.4 0.3 turn_weight.1.mine_ref
  29.7 0.1 collective-permute-start.8
  29.8 0.0 collective-permute-done.9.refs_1_
  29.8 0.5 %collective-permute-start.11 = (bf16[128,512]{1,0:T(8,128)(2,1)S(1)}, bf16[128,512]{1,0:T(8,128)(2,1)S(1)}, u32[]{:S(2)}, u32[]{:S(2)}) collective-permute-start(bf16[128,512]{1,0:T(8,128)(2,1)S(1)} %collective-permute-done.9.refs_1_), channel_id=1, source_target_pairs={{0,1},{1,0},{2,3},{3,2},{4,5},{5,4},{6,7},{7,6},{8,9},{9,8},{10,11... | collective-permute-start | bytes 393224 | tf_op jit(solution)/shard_map/ppermute | solution.py:38
  30.3 0.0 collective-permute-done.10.refs_2_
  30.3 1.6 %collective-permute-done.8.theirs_ref = bf16[1408,256]{1,0:T(8,128)(2,1)S(1)} collective-permute-done((bf16[1408,256]{1,0:T(8,128)(2,1)S(1)}, bf16[1408,256]{1,0:T(8,128)(2,1)S(1)}, u32[]{:S(2)}, u32[]{:S(2)}) %collective-permute-start.8) | collective-permute-done | bytes 720928 | tf_op jit(solution)/shard_map/ppermute | solution.py:25
  31.9 0.9 %first_heads.1.first_ref = f32[1408,512]{1,0:T(8,128)S(1)} custom-call(bf16[1408,256]{1,0:T(8,128)(2,1)S(1)} %turn_weight.1.mine_ref, bf16[1408,256]{1,0:T(8,128)(2,1)S(1)} %collective-permute-done.8.theirs_ref, bf16[512,512]{1,0:T(8,128)(2,1)S(1)} %collect_heads.1.heads_ref), custom_call_target="tpu_custom_call" | custom-call | flops 1 | bytes 1 | tf_op jit(solution)/shard_map/first_heads/pallas_call | solution.py:398
  32.8 2.8 %collective-permute-done.11.last_ref = bf16[128,512]{1,0:T(8,128)(2,1)S(1)} collective-permute-done((bf16[128,512]{1,0:T(8,128)(2,1)S(1)}, bf16[128,512]{1,0:T(8,128)(2,1)S(1)}, u32[]{:S(2)}, u32[]{:S(2)}) %collective-permute-start.11) | collective-permute-done | bytes 131104 | tf_op jit(solution)/shard_map/ppermute | solution.py:38
  35.7 1.4 %output.1 = bf16[1344,512]{1,0:T(8,128)(2,1)} custom-call(bf16[1408,256]{1,0:T(8,128)(2,1)S(1)} %turn_weight.1.mine_ref, bf16[1408,256]{1,0:T(8,128)(2,1)S(1)} %collective-permute-done.8.theirs_ref, f32[1408,512]{1,0:T(8,128)S(1)} %first_heads.1.first_ref, bf16[128,512]{1,0:T(8,128)(2,1)S(1)} %collective-permute-done.11.last_ref), custom_call_target="tpu_custom_call" | custom-call | flops 1 | bytes 1 | tf_op jit(solution)/shard_map/output/pallas_call | solution.py:407
  (4 shorter events, 0.0 us)
Async XLA Ops:
  0.0 0.7 %copy-start.1 = (f32[5376]{0:T(1024)S(1)}, f32[5376]{0:T(1024)}, u32[]{:S(2)}) copy-start(f32[5376]{0:T(1024)} %param.6) | copy-start | bytes 64516
  5.9 10.3 %collective-permute-start.5 = (bf16[1024,128]{1,0:T(8,128)(2,1)S(1)}, bf16[1024,128]{1,0:T(8,128)(2,1)S(1)}, u32[]{:S(2)}, u32[]{:S(2)}) collective-permute-start(bf16[1024,128]{1,0:T(8,128)(2,1)S(1)} %get-tuple-element.18.own_ref), channel_id=1, source_target_pairs={{0,8},{4,12},{8,16},{12,20},{16,24},{20,28},{24,0},{28,4},{1,9},{5... | collective-permute-start | bytes 786440 | tf_op jit(solution)/shard_map/ppermute | solution.py:21
  8.9 14.4 %collective-permute-start = (bf16[32,1408]{1,0:T(8,128)(2,1)S(1)}, bf16[32,1408]{1,0:T(8,128)(2,1)S(1)}, u32[]{:S(2)}, u32[]{:S(2)}) collective-permute-start(bf16[32,1408]{1,0:T(8,128)(2,1)S(1)} %get-tuple-element.14), channel_id=1, source_target_pairs={{0,2},{1,3},{2,0},{3,1},{4,6},{5,7},{6,4},{7,5},{8,10},{9,11},{10,... | collective-permute-start | bytes 270344 | tf_op jit(solution)/shard_map/ppermute | solution.py:38
  11.5 12.4 %collective-permute-start.2 = (bf16[32,1408]{1,0:T(8,128)(2,1)S(1)}, bf16[32,1408]{1,0:T(8,128)(2,1)S(1)}, u32[]{:S(2)}, u32[]{:S(2)}) collective-permute-start(bf16[32,1408]{1,0:T(8,128)(2,1)S(1)} %get-tuple-element.15), channel_id=1, source_target_pairs={{0,3},{1,2},{2,1},{3,0},{4,7},{5,6},{6,5},{7,4},{8,11},{9,10},{10,... | collective-permute-start | bytes 270344 | tf_op jit(solution)/shard_map/ppermute | solution.py:38
  12.8 16.6 %collective-permute-start.4 = (bf16[64,1408]{1,0:T(8,128)(2,1)S(1)}, bf16[64,1408]{1,0:T(8,128)(2,1)S(1)}, u32[]{:S(2)}, u32[]{:S(2)}) collective-permute-start(bf16[64,1408]{1,0:T(8,128)(2,1)S(1)} %get-tuple-element.16), channel_id=1, source_target_pairs={{0,1},{1,0},{2,3},{3,2},{4,5},{5,4},{6,7},{7,6},{8,9},{9,8},{10,11... | collective-permute-start | bytes 540680 | tf_op jit(solution)/shard_map/ppermute | solution.py:38
  16.2 1.6 %collective-permute-start.6 = (bf16[512,128]{1,0:T(8,128)(2,1)S(1)}, bf16[512,128]{1,0:T(8,128)(2,1)S(1)}, u32[]{:S(2)}, u32[]{:S(2)}) collective-permute-start(bf16[512,128]{1,0:T(8,128)(2,1)S(1)} %get-tuple-element.19), channel_id=1, source_target_pairs={{0,4},{4,0},{8,12},{12,8},{16,20},{20,16},{24,28},{28,24},{1,5},{5... | collective-permute-start | bytes 393224 | tf_op jit(solution)/shard_map/ppermute | solution.py:25
  16.3 1.6 %collective-permute-start.7 = (bf16[512,128]{1,0:T(8,128)(2,1)S(1)}, bf16[512,128]{1,0:T(8,128)(2,1)S(1)}, u32[]{:S(2)}, u32[]{:S(2)}) collective-permute-start(bf16[512,128]{1,0:T(8,128)(2,1)S(1)} %get-tuple-element.20), channel_id=1, source_target_pairs={{0,4},{4,0},{8,12},{12,8},{16,20},{20,16},{24,28},{28,24},{1,5},{5... | collective-permute-start | bytes 393224 | tf_op jit(solution)/shard_map/ppermute | solution.py:25
  16.8 12.6 %copy-start = (bf16[128,5376]{1,0:T(8,128)(2,1)S(1)}, bf16[128,5376]{1,0:T(8,128)(2,1)}, u32[]{:S(2)}) copy-start(bf16[128,5376]{1,0:T(8,128)(2,1)} %refs_6_.1) | copy-start | bytes 4128772
  18.8 11.0 %collective-permute-start.9 = (bf16[128,512]{1,0:T(8,128)(2,1)S(1)}, bf16[128,512]{1,0:T(8,128)(2,1)S(1)}, u32[]{:S(2)}, u32[]{:S(2)}) collective-permute-start(bf16[128,512]{1,0:T(8,128)(2,1)S(1)} %near_block.1.refs_5_.refs_0_), channel_id=1, source_target_pairs={{0,2},{1,3},{2,0},{3,1},{4,6},{5,7},{6,4},{7,5},{8,10},{9,11},{10,... | collective-permute-start | bytes 393224 | tf_op jit(solution)/shard_map/ppermute | solution.py:38
  21.6 8.6 %collective-permute-start.10 = (bf16[128,512]{1,0:T(8,128)(2,1)S(1)}, bf16[128,512]{1,0:T(8,128)(2,1)S(1)}, u32[]{:S(2)}, u32[]{:S(2)}) collective-permute-start(bf16[128,512]{1,0:T(8,128)(2,1)S(1)} %near_block.1.refs_5_.refs_0_), channel_id=1, source_target_pairs={{0,1},{1,0},{2,3},{3,2},{4,5},{5,4},{6,7},{7,6},{8,9},{9,8},{10,11... | collective-permute-start | bytes 393224 | tf_op jit(solution)/shard_map/ppermute | solution.py:38
  23.2 5.2 %collective-permute-start.1 = (bf16[32,1408]{1,0:T(8,128)(2,1)S(1)}, bf16[32,1408]{1,0:T(8,128)(2,1)S(1)}, u32[]{:S(2)}, u32[]{:S(2)}) collective-permute-start(bf16[32,1408]{1,0:T(8,128)(2,1)S(1)} %collective-permute-done.refs_0_), channel_id=1, source_target_pairs={{0,8},{4,12},{8,0},{12,4},{16,24},{20,28},{24,16},{28,20},{1,9},{5... | collective-permute-start | bytes 270344 | tf_op jit(solution)/shard_map/ppermute | solution.py:29
  23.8 5.5 %collective-permute-start.3 = (bf16[32,1408]{1,0:T(8,128)(2,1)S(1)}, bf16[32,1408]{1,0:T(8,128)(2,1)S(1)}, u32[]{:S(2)}, u32[]{:S(2)}) collective-permute-start(bf16[32,1408]{1,0:T(8,128)(2,1)S(1)} %collective-permute-done.2.refs_2_), channel_id=1, source_target_pairs={{0,8},{4,12},{8,0},{12,4},{16,24},{20,28},{24,16},{28,20},{1,9},{5... | collective-permute-start | bytes 270344 | tf_op jit(solution)/shard_map/ppermute | solution.py:29
  29.7 2.3 %collective-permute-start.8 = (bf16[1408,256]{1,0:T(8,128)(2,1)S(1)}, bf16[1408,256]{1,0:T(8,128)(2,1)S(1)}, u32[]{:S(2)}, u32[]{:S(2)}) collective-permute-start(bf16[1408,256]{1,0:T(8,128)(2,1)S(1)} %turn_weight.1.mine_ref), channel_id=1, source_target_pairs={{0,4},{4,0},{8,12},{12,8},{16,20},{20,16},{24,28},{28,24},{1,5},{5... | collective-permute-start | bytes 2162696 | tf_op jit(solution)/shard_map/ppermute | solution.py:25
  29.8 5.9 %collective-permute-start.11 = (bf16[128,512]{1,0:T(8,128)(2,1)S(1)}, bf16[128,512]{1,0:T(8,128)(2,1)S(1)}, u32[]{:S(2)}, u32[]{:S(2)}) collective-permute-start(bf16[128,512]{1,0:T(8,128)(2,1)S(1)} %collective-permute-done.9.refs_1_), channel_id=1, source_target_pairs={{0,1},{1,0},{2,3},{3,2},{4,5},{5,4},{6,7},{7,6},{8,9},{9,8},{10,11... | collective-permute-start | bytes 393224 | tf_op jit(solution)/shard_map/ppermute | solution.py:38

commit v4 on v3

--- a/solution.py
+++ b/solution.py
@@ -169,11 +169,9 @@
     return jnp.concatenate(tiles, axis=1)
 
 
-def pass_kernel(own_ref, far_ref, keys_ref, values_ref):
+def pass_kernel(own_ref, far_ref, out_ref):
     core = lax.axis_index("seq") % 2
-    rows = keys_ref.shape[0]
-    keys_ref[...] = jnp.where(core == 0, own_ref[:rows, :], far_ref[:rows, :])
-    values_ref[...] = jnp.where(core == 0, own_ref[rows:, :], far_ref[rows:, :])
+    out_ref[...] = jnp.where(core == 0, own_ref[...], far_ref[...])
 
 
 NT = ((1,), (1,))
@@ -181,7 +179,7 @@
 
 def mixed_kernel(q_ref, own_ref, far_ref, out_ref, stats_ref):
     rows = q_ref.shape[0]
-    chunk = min(rows, 256)
+    chunk = rows
     bias = jnp.where(lax.axis_index("seq") < 2, MASKED, 0.0).astype(F32)
     own_values, far_values = values_of(own_ref, rows), values_of(far_ref, rows)
     for start in range(0, rows, chunk):
@@ -200,14 +198,14 @@
         out_ref[:, span] = out + matmul(far_values, jnp.where(own, 0.0, expo).astype(BF16))
 
 
-def near_kernel(q_ref, keys_ref, values_ref, mixed_ref, stats_ref, out_ref):
+def near_kernel(q_ref, near_ref, mixed_ref, stats_ref, out_ref):
     rows = q_ref.shape[0]
-    chunk = min(rows, 256)
+    chunk = rows
     bias = jnp.where(lax.axis_index("seq") < 1, MASKED, 0.0).astype(F32)
-    values = values_of(values_ref, 0)
+    values = values_of(near_ref, rows)
     for start in range(0, rows, chunk):
         span = slice(start, start + chunk)
-        scores = matmul(keys_ref[...], q_ref[span, :], NT) + bias
+        scores = matmul(near_ref[:rows, :], q_ref[span, :], NT) + bias
         before = stats_ref[0:1, span]
         highest = jnp.maximum(before, jnp.max(scores, axis=0, keepdims=True))
         expo = jnp.exp2(scores - highest)
@@ -245,7 +243,7 @@
     return copies
 
 
-def turn_kernel(width, mp, split, *refs):
+def turn_kernel(width, mp, split, sequence, *refs):
     pieces, (weight_ref, out_ref, own_ref, sem) = list(refs[:-5]), refs[-4:]
     half, window = own_ref.shape
     (copy,) = cut_copies(width, mp, [0], weight_ref, [own_ref], sem)
@@ -253,7 +251,7 @@
     chip = lax.axis_index("seq") // 2 % 2
     copy.wait()
     blocks = {-1: own_ref[...]}
-    for i in sorted(range(mp - 1), key=lambda i: not split[i]):
+    for i in sequence:
         block = pieces.pop(0)[...]
         if split[i]:
             other = pieces.pop(0)[...]
@@ -331,8 +329,8 @@
     shape = lambda *dims: jax.ShapeDtypeStruct(dims, BF16)
     large = 52 * 2**20
 
-    order = [2, 1, 3] if mp == 4 else list(range(1, mp))
-    split = [mp == 4 and d > 1 for d in order]
+    order = [3, 1, 2] if mp == 4 else list(range(1, mp))
+    split = [mp == 4 and d == 2 for d in order]
     counts = [half // 2 if in_two else half for in_two in split]
     scale = math.log2(math.e) / math.sqrt(168.0)
     queries, kv, *pieces = call(
@@ -349,11 +347,11 @@
     passed = call(
         pass_kernel,
         "pass_on",
-        [shape(rows, head), shape(rows, head)],
+        shape(*kv.shape),
         in_specs=[vmem] * 2,
-        out_specs=[vmem] * 2,
+        out_specs=vmem,
     )(kv, far)
-    near = [other_core(block) for block in passed]
+    near = other_core(passed)
     mixed, stats = call(
         mixed_kernel,
         "mixed_blocks",
@@ -366,9 +364,9 @@
         near_kernel,
         "near_block",
         shape(head, rows),
-        in_specs=[vmem] * 5,
+        in_specs=[vmem] * 4,
         out_specs=vmem,
-    )(queries, *near, mixed, stats)
+    )(queries, near, mixed, stats)
     heads = [head_out] + [exchanged(head_out, d) for d in order[:-1]]
     if mp == 4:
         last_head = exchanged(heads[1], 1)
@@ -376,10 +374,11 @@
         last_head = exchanged(head_out, order[-1])
 
     parts = []
-    for i in sorted(range(mp - 1), key=lambda i: not split[i]):
+    sequence = sorted(range(mp - 1), key=lambda i: (not split[i], -order[i]))
+    for i in sequence:
         parts += [mine[i], next_chip(mine[i])] if split[i] else [mine[i]]
     mine_turned = call(
-        functools.partial(turn_kernel, width, mp, split),
+        functools.partial(turn_kernel, width, mp, split, sequence),
         "turn_weight",
         shape(window, mp * half),
         in_specs=[vmem] * len(parts) + [anywhere, hbm],

time: 37.2 us -> 35.1 us (0.944)
  waiting for transfers between devices: 11.7 us -> 10.4 us
  starting transfers between devices: 14.8 us -> 14.3 us
  Pallas kernels: 9.79 us -> 9.3 us
    ppermute x6, starting transfers between devices: 9.11 us -> 10.6 us  [exchanged(): lax.ppermute(block, 'mp', [(i, partner(i, distance, mp)) for i in range(m...]
    ppermute x2 -> x1, starting transfers between devices: 2.03 us -> 0.6 us  [next_chip(): lax.ppermute(block, 'seq', [(i, i ^ 2) for i in range(lax.axis_size('seq'...]
    ppermute x3 -> x2, waiting for transfers between devices: 1.6 us -> 0.71 us  [other_core(): lax.ppermute(block, 'seq', [(i, i ^ 1) for i in range(lax.axis_size('seq'...]
    ppermute x3 -> x2, starting transfers between devices: 0.64 us -> 0.14 us  [other_core(): lax.ppermute(block, 'seq', [(i, i ^ 1) for i in range(lax.axis_size('seq'...]
    ppermute x2 -> x1, waiting for transfers between devices: 4.12 us -> 3.93 us  [next_chip(): lax.ppermute(block, 'seq', [(i, i ^ 2) for i in range(lax.axis_size('seq'...]
  transfers between devices with their start and end apart: 12 -> 10, of which waited for: 5 -> 4; matrix products, arithmetic and copies ran while one was open for 0% -> 0% of each run, Pallas kernels for 9% -> 8%
where the time goes in v4:
time: 35.1 us; the launch traced here: 34.9 us
  starting transfers between devices  14.3 us (41%)
  waiting for transfers between devices  10.4 us (30%)
  Pallas kernels  9.3 us (26%)
  local copies, waits for them, and re-layouts  0.74 us (2%)
    ppermute x6, starting transfers between devices, exchanged(): lax.ppermute(block, 'mp', [(i, partner(i, distance, mp)) for i in range(m...  10.6 us
    pallas_call x1, Pallas kernels, per_device(): call(functools.partial(project_all_kernel, scale, width, mp, BLOCKS, AHEA...  5.13 us
    ppermute x1, waiting for transfers between devices, next_chip(): lax.ppermute(block, 'seq', [(i, i ^ 2) for i in range(lax.axis_size('seq'...  3.93 us
    ppermute x1, waiting for transfers between devices, around(): lax.ppermute(block, axis, [(i, (i + distance) % size) for i in range(size)])  3.09 us
    ppermute x1, starting transfers between devices, around(): lax.ppermute(block, axis, [(i, (i + distance) % size) for i in range(size)])  2.99 us
    ppermute x6, waiting for transfers between devices, exchanged(): lax.ppermute(block, 'mp', [(i, partner(i, distance, mp)) for i in range(m...  2.7 us
    pallas_call x1, Pallas kernels, per_device(): call(functools.partial(output_kernel, width, mp, chunk), 'output', shape(...  1.38 us
    pallas_call x1, Pallas kernels, per_device(): call(first_heads_kernel, 'first_heads', jax.ShapeDtypeStruct((window, row...  0.9 us
  transfers between devices with their start and end apart: 10, of which 4 were waited for; matrix products, arithmetic and copies ran while one was open for 0% of the time, Pallas kernels for 8%

profile of v4, /device:TPU:0, one launch (start us, length us, event | category | flops | bytes accessed | tf_op | source)
XLA Modules:
  0.0 34.9 jit_solution(11663036322688641452)
XLA Ops:
  0.0 0.0 copy-start.1
  0.0 0.7 %copy-done.1 = f32[5376]{0:T(1024)S(1)} copy-done((f32[5376]{0:T(1024)S(1)}, f32[5376]{0:T(1024)}, u32[]{:S(2)}) %copy-start.1) | copy-done | bytes 21528
  0.7 5.1 %project.1 = (bf16[512,128]{1,0:T(8,128)(2,1)S(1)}, bf16[1024,128]{1,0:T(8,128)(2,1)S(1)}, bf16[64,1408]{1,0:T(8,128)(2,1)S(1)}, bf16[64,1408]{1,0:T(8,128)(2,1)S(1)}, bf16[32,1408]{1,0:T(8,128)(2,1)S(1)}) custom-call(bf16[512,5376]{1,0:T(8,128)(2,1)} %x_ref.1, f32[42,128]{1,0:T(8,128)S(1)} %bitcast.1, bf16[5376,256]{1,0:T(8,128)(2,1)} %refs_0_.1, ...), custom_call_target="tpu_custom_call" | custom-call | flops 1 | bytes 1 | tf_op jit(solution)/shard_map/project/pallas_call | solution.py:336
  5.9 3.0 %collective-permute-start.4 = (bf16[1024,128]{1,0:T(8,128)(2,1)S(1)}, bf16[1024,128]{1,0:T(8,128)(2,1)S(1)}, u32[]{:S(2)}, u32[]{:S(2)}) collective-permute-start(bf16[1024,128]{1,0:T(8,128)(2,1)S(1)} %get-tuple-element.16.own_ref), channel_id=1, source_target_pairs={{0,8},{4,12},{8,16},{12,20},{16,24},{20,28},{24,0},{28,4},{1,9},{5... | collective-permute-start | bytes 786440 | tf_op jit(solution)/shard_map/ppermute | solution.py:21
  8.9 2.6 %collective-permute-start = (bf16[32,1408]{1,0:T(8,128)(2,1)S(1)}, bf16[32,1408]{1,0:T(8,128)(2,1)S(1)}, u32[]{:S(2)}, u32[]{:S(2)}) collective-permute-start(bf16[32,1408]{1,0:T(8,128)(2,1)S(1)} %get-tuple-element.12), channel_id=1, source_target_pairs={{0,2},{1,3},{2,0},{3,1},{4,6},{5,7},{6,4},{7,5},{8,10},{9,11},{10,... | collective-permute-start | bytes 270344 | tf_op jit(solution)/shard_map/ppermute | solution.py:38
  11.5 1.3 %collective-permute-start.2 = (bf16[64,1408]{1,0:T(8,128)(2,1)S(1)}, bf16[64,1408]{1,0:T(8,128)(2,1)S(1)}, u32[]{:S(2)}, u32[]{:S(2)}) collective-permute-start(bf16[64,1408]{1,0:T(8,128)(2,1)S(1)} %get-tuple-element.13), channel_id=1, source_target_pairs={{0,3},{1,2},{2,1},{3,0},{4,7},{5,6},{6,5},{7,4},{8,11},{9,10},{10,... | collective-permute-start | bytes 540680 | tf_op jit(solution)/shard_map/ppermute | solution.py:38
  12.8 0.2 collective-permute-start.3
  13.0 3.1 %collective-permute-done.4.far_ref = bf16[1024,128]{1,0:T(8,128)(2,1)S(1)} collective-permute-done((bf16[1024,128]{1,0:T(8,128)(2,1)S(1)}, bf16[1024,128]{1,0:T(8,128)(2,1)S(1)}, u32[]{:S(2)}, u32[]{:S(2)}) %collective-permute-start.4) | collective-permute-done | bytes 262176 | tf_op jit(solution)/shard_map/ppermute | solution.py:21
  16.1 0.1 pass_on.1
  16.2 0.1 collective-permute-start.5
  16.3 0.0 copy-start
  16.3 0.8 %mixed_blocks.1 = (f32[128,512]{1,0:T(8,128)S(1)}, f32[2,512]{1,0:T(2,128)S(1)}) custom-call(bf16[512,128]{1,0:T(8,128)(2,1)S(1)} %get-tuple-element.15.q_ref, bf16[1024,128]{1,0:T(8,128)(2,1)S(1)} %get-tuple-element.16.own_ref, bf16[1024,128]{1,0:T(8,128)(2,1)S(1)} %collective-permute-done.4.far_ref), custom_call_target="tpu_custom_call" | custom-call | flops 99999997952 | bytes 1 | tf_op jit(solution)/shard_map/mixed_blocks/pallas_call | solution.py:355
  17.1 0.7 %collective-permute-done.5.near_ref = bf16[1024,128]{1,0:T(8,128)(2,1)S(1)} collective-permute-done((bf16[1024,128]{1,0:T(8,128)(2,1)S(1)}, bf16[1024,128]{1,0:T(8,128)(2,1)S(1)}, u32[]{:S(2)}, u32[]{:S(2)}) %collective-permute-start.5) | collective-permute-done | bytes 262176 | tf_op jit(solution)/shard_map/ppermute | solution.py:25
  17.8 0.7 %near_block.1.refs_4_.refs_0_ = bf16[128,512]{1,0:T(8,128)(2,1)S(1)} custom-call(bf16[512,128]{1,0:T(8,128)(2,1)S(1)} %get-tuple-element.15.q_ref, bf16[1024,128]{1,0:T(8,128)(2,1)S(1)} %collective-permute-done.5.near_ref, f32[128,512]{1,0:T(8,128)S(1)} %get-tuple-element.17.mixed_ref, f32[2,512]{1,0:T(2,128)S(1)} %get-tuple-element.18.stats_ref), custom_call_target="tpu_custom_call" | custom-call | flops 1 | bytes 1 | tf_op jit(solution)/shard_map/near_block/pallas_call | solution.py:363
  18.5 3.9 %collective-permute-start.7 = (bf16[128,512]{1,0:T(8,128)(2,1)S(1)}, bf16[128,512]{1,0:T(8,128)(2,1)S(1)}, u32[]{:S(2)}, u32[]{:S(2)}) collective-permute-start(bf16[128,512]{1,0:T(8,128)(2,1)S(1)} %near_block.1.refs_4_.refs_0_), channel_id=1, source_target_pairs={{0,3},{1,2},{2,1},{3,0},{4,7},{5,6},{6,5},{7,4},{8,11},{9,10},{10,... | collective-permute-start | bytes 393224 | tf_op jit(solution)/shard_map/ppermute | solution.py:38
  22.3 0.0 collective-permute-start.8
  22.3 0.0 collective-permute-done.refs_0_
  22.4 0.6 %collective-permute-start.1 = (bf16[32,1408]{1,0:T(8,128)(2,1)S(1)}, bf16[32,1408]{1,0:T(8,128)(2,1)S(1)}, u32[]{:S(2)}, u32[]{:S(2)}) collective-permute-start(bf16[32,1408]{1,0:T(8,128)(2,1)S(1)} %collective-permute-done.refs_0_), channel_id=1, source_target_pairs={{0,8},{4,12},{8,0},{12,4},{16,24},{20,28},{24,16},{28,20},{1,9},{5... | collective-permute-start | bytes 270344 | tf_op jit(solution)/shard_map/ppermute | solution.py:29
  22.9 3.9 %collective-permute-done.1.refs_1_ = bf16[32,1408]{1,0:T(8,128)(2,1)S(1)} collective-permute-done((bf16[32,1408]{1,0:T(8,128)(2,1)S(1)}, bf16[32,1408]{1,0:T(8,128)(2,1)S(1)}, u32[]{:S(2)}, u32[]{:S(2)}) %collective-permute-start.1) | collective-permute-done | bytes 90144 | tf_op jit(solution)/shard_map/ppermute | solution.py:29
  26.9 0.0 collective-permute-done.2.refs_2_
  26.9 0.0 collective-permute-done.3.refs_3_
  26.9 0.0 copy-done
  26.9 0.3 turn_weight.1.mine_ref
  27.2 0.1 collective-permute-start.6
  27.3 0.0 collective-permute-done.7.refs_1_
  27.3 2.5 %collective-permute-start.9 = (bf16[128,512]{1,0:T(8,128)(2,1)S(1)}, bf16[128,512]{1,0:T(8,128)(2,1)S(1)}, u32[]{:S(2)}, u32[]{:S(2)}) collective-permute-start(bf16[128,512]{1,0:T(8,128)(2,1)S(1)} %collective-permute-done.7.refs_1_), channel_id=1, source_target_pairs={{0,1},{1,0},{2,3},{3,2},{4,5},{5,4},{6,7},{7,6},{8,9},{9,8},{10,11... | collective-permute-start | bytes 393224 | tf_op jit(solution)/shard_map/ppermute | solution.py:38
  29.8 0.0 collective-permute-done.8.refs_2_
  29.9 0.0 collective-permute-done.6.theirs_ref
  29.9 0.9 %first_heads.1.first_ref = f32[1408,512]{1,0:T(8,128)S(1)} custom-call(bf16[1408,256]{1,0:T(8,128)(2,1)S(1)} %turn_weight.1.mine_ref, bf16[1408,256]{1,0:T(8,128)(2,1)S(1)} %collective-permute-done.6.theirs_ref, bf16[512,512]{1,0:T(8,128)(2,1)S(1)} %collect_heads.1.heads_ref), custom_call_target="tpu_custom_call" | custom-call | flops 1 | bytes 1 | tf_op jit(solution)/shard_map/first_heads/pallas_call | solution.py:397
  30.8 2.7 %collective-permute-done.9.last_ref = bf16[128,512]{1,0:T(8,128)(2,1)S(1)} collective-permute-done((bf16[128,512]{1,0:T(8,128)(2,1)S(1)}, bf16[128,512]{1,0:T(8,128)(2,1)S(1)}, u32[]{:S(2)}, u32[]{:S(2)}) %collective-permute-start.9) | collective-permute-done | bytes 131104 | tf_op jit(solution)/shard_map/ppermute | solution.py:38
  33.5 1.4 %output.1 = bf16[1344,512]{1,0:T(8,128)(2,1)} custom-call(bf16[1408,256]{1,0:T(8,128)(2,1)S(1)} %turn_weight.1.mine_ref, bf16[1408,256]{1,0:T(8,128)(2,1)S(1)} %collective-permute-done.6.theirs_ref, f32[1408,512]{1,0:T(8,128)S(1)} %first_heads.1.first_ref, bf16[128,512]{1,0:T(8,128)(2,1)S(1)} %collective-permute-done.9.last_ref), custom_call_target="tpu_custom_call" | custom-call | flops 1 | bytes 1 | tf_op jit(solution)/shard_map/output/pallas_call | solution.py:406
  (1 shorter events, 0.0 us)
Async XLA Ops:
  0.0 0.7 %copy-start.1 = (f32[5376]{0:T(1024)S(1)}, f32[5376]{0:T(1024)}, u32[]{:S(2)}) copy-start(f32[5376]{0:T(1024)} %param.6) | copy-start | bytes 64516
  5.9 10.3 %collective-permute-start.4 = (bf16[1024,128]{1,0:T(8,128)(2,1)S(1)}, bf16[1024,128]{1,0:T(8,128)(2,1)S(1)}, u32[]{:S(2)}, u32[]{:S(2)}) collective-permute-start(bf16[1024,128]{1,0:T(8,128)(2,1)S(1)} %get-tuple-element.16.own_ref), channel_id=1, source_target_pairs={{0,8},{4,12},{8,16},{12,20},{16,24},{20,28},{24,0},{28,4},{1,9},{5... | collective-permute-start | bytes 786440 | tf_op jit(solution)/shard_map/ppermute | solution.py:21
  8.9 13.5 %collective-permute-start = (bf16[32,1408]{1,0:T(8,128)(2,1)S(1)}, bf16[32,1408]{1,0:T(8,128)(2,1)S(1)}, u32[]{:S(2)}, u32[]{:S(2)}) collective-permute-start(bf16[32,1408]{1,0:T(8,128)(2,1)S(1)} %get-tuple-element.12), channel_id=1, source_target_pairs={{0,2},{1,3},{2,0},{3,1},{4,6},{5,7},{6,4},{7,5},{8,10},{9,11},{10,... | collective-permute-start | bytes 270344 | tf_op jit(solution)/shard_map/ppermute | solution.py:38
  11.5 15.4 %collective-permute-start.2 = (bf16[64,1408]{1,0:T(8,128)(2,1)S(1)}, bf16[64,1408]{1,0:T(8,128)(2,1)S(1)}, u32[]{:S(2)}, u32[]{:S(2)}) collective-permute-start(bf16[64,1408]{1,0:T(8,128)(2,1)S(1)} %get-tuple-element.13), channel_id=1, source_target_pairs={{0,3},{1,2},{2,1},{3,0},{4,7},{5,6},{6,5},{7,4},{8,11},{9,10},{10,... | collective-permute-start | bytes 540680 | tf_op jit(solution)/shard_map/ppermute | solution.py:38
  12.8 14.1 %collective-permute-start.3 = (bf16[64,1408]{1,0:T(8,128)(2,1)S(1)}, bf16[64,1408]{1,0:T(8,128)(2,1)S(1)}, u32[]{:S(2)}, u32[]{:S(2)}) collective-permute-start(bf16[64,1408]{1,0:T(8,128)(2,1)S(1)} %get-tuple-element.14), channel_id=1, source_target_pairs={{0,1},{1,0},{2,3},{3,2},{4,5},{5,4},{6,7},{7,6},{8,9},{9,8},{10,11... | collective-permute-start | bytes 540680 | tf_op jit(solution)/shard_map/ppermute | solution.py:38
  16.2 1.6 %collective-permute-start.5 = (bf16[1024,128]{1,0:T(8,128)(2,1)S(1)}, bf16[1024,128]{1,0:T(8,128)(2,1)S(1)}, u32[]{:S(2)}, u32[]{:S(2)}) collective-permute-start(bf16[1024,128]{1,0:T(8,128)(2,1)S(1)} %pass_on.1), channel_id=1, source_target_pairs={{0,4},{4,0},{8,12},{12,8},{16,20},{20,16},{24,28},{28,24},{1,5},{5... | collective-permute-start | bytes 786440 | tf_op jit(solution)/shard_map/ppermute | solution.py:25
  16.3 10.6 %copy-start = (bf16[128,5376]{1,0:T(8,128)(2,1)S(1)}, bf16[128,5376]{1,0:T(8,128)(2,1)}, u32[]{:S(2)}) copy-start(bf16[128,5376]{1,0:T(8,128)(2,1)} %refs_5_.1) | copy-start | bytes 4128772
  18.5 8.8 %collective-permute-start.7 = (bf16[128,512]{1,0:T(8,128)(2,1)S(1)}, bf16[128,512]{1,0:T(8,128)(2,1)S(1)}, u32[]{:S(2)}, u32[]{:S(2)}) collective-permute-start(bf16[128,512]{1,0:T(8,128)(2,1)S(1)} %near_block.1.refs_4_.refs_0_), channel_id=1, source_target_pairs={{0,3},{1,2},{2,1},{3,0},{4,7},{5,6},{6,5},{7,4},{8,11},{9,10},{10,... | collective-permute-start | bytes 393224 | tf_op jit(solution)/shard_map/ppermute | solution.py:38
  22.3 7.5 %collective-permute-start.8 = (bf16[128,512]{1,0:T(8,128)(2,1)S(1)}, bf16[128,512]{1,0:T(8,128)(2,1)S(1)}, u32[]{:S(2)}, u32[]{:S(2)}) collective-permute-start(bf16[128,512]{1,0:T(8,128)(2,1)S(1)} %near_block.1.refs_4_.refs_0_), channel_id=1, source_target_pairs={{0,1},{1,0},{2,3},{3,2},{4,5},{5,4},{6,7},{7,6},{8,9},{9,8},{10,11... | collective-permute-start | bytes 393224 | tf_op jit(solution)/shard_map/ppermute | solution.py:38
  22.4 4.5 %collective-permute-start.1 = (bf16[32,1408]{1,0:T(8,128)(2,1)S(1)}, bf16[32,1408]{1,0:T(8,128)(2,1)S(1)}, u32[]{:S(2)}, u32[]{:S(2)}) collective-permute-start(bf16[32,1408]{1,0:T(8,128)(2,1)S(1)} %collective-permute-done.refs_0_), channel_id=1, source_target_pairs={{0,8},{4,12},{8,0},{12,4},{16,24},{20,28},{24,16},{28,20},{1,9},{5... | collective-permute-start | bytes 270344 | tf_op jit(solution)/shard_map/ppermute | solution.py:29
  27.2 2.7 %collective-permute-start.6 = (bf16[1408,256]{1,0:T(8,128)(2,1)S(1)}, bf16[1408,256]{1,0:T(8,128)(2,1)S(1)}, u32[]{:S(2)}, u32[]{:S(2)}) collective-permute-start(bf16[1408,256]{1,0:T(8,128)(2,1)S(1)} %turn_weight.1.mine_ref), channel_id=1, source_target_pairs={{0,4},{4,0},{8,12},{12,8},{16,20},{20,16},{24,28},{28,24},{1,5},{5... | collective-permute-start | bytes 2162696 | tf_op jit(solution)/shard_map/ppermute | solution.py:25
  27.3 6.2 %collective-permute-start.9 = (bf16[128,512]{1,0:T(8,128)(2,1)S(1)}, bf16[128,512]{1,0:T(8,128)(2,1)S(1)}, u32[]{:S(2)}, u32[]{:S(2)}) collective-permute-start(bf16[128,512]{1,0:T(8,128)(2,1)S(1)} %collective-permute-done.7.refs_1_), channel_id=1, source_target_pairs={{0,1},{1,0},{2,3},{3,2},{4,5},{5,4},{6,7},{7,6},{8,9},{9,8},{10,11... | collective-permute-start | bytes 393224 | tf_op jit(solution)/shard_map/ppermute | solution.py:38

commit v5 on v4

--- a/solution.py
+++ b/solution.py
@@ -109,12 +109,11 @@
         for r in range(0, rows, chunk):
             part = None
             for t in range(end - size, end, LANES):
-                x = x_buf[r : r + chunk, t : t + LANES]
-                gain = gain_ref[t // LANES : t // LANES + 1, :].astype(BF16)
-                scaled_ref[r : r + chunk, t : t + LANES] = x * gain
+                x = x_buf[r : r + chunk, t : t + LANES].astype(F32)
+                gain = gain_ref[t // LANES : t // LANES + 1, :]
+                scaled_ref[r : r + chunk, t : t + LANES] = (x * gain).astype(BF16)
                 square = x * x
                 part = square if part is None else part + square
-            part = part.astype(F32)
             square_ref[r : r + chunk, :] = part if k == 0 else square_ref[r : r + chunk, :] + part
         span = slice(end - size, end)
         product = matmul(scaled_ref[:, span], weight_buf[span, :])

time: 35.1 us -> 35.1 us (level)
  no operation moved by 1% of the time
where the time goes in v5:
time: 35.1 us; the launch traced here: 34.9 us
  starting transfers between devices  14.3 us (41%)
  waiting for transfers between devices  10.4 us (30%)
  Pallas kernels  9.33 us (27%)
  local copies, waits for them, and re-layouts  0.74 us (2%)
    ppermute x6, starting transfers between devices, exchanged(): lax.ppermute(block, 'mp', [(i, partner(i, distance, mp)) for i in range(m...  10.6 us
    pallas_call x1, Pallas kernels, per_device(): call(functools.partial(project_all_kernel, scale, width, mp, BLOCKS, AHEA...  5.16 us
    ppermute x1, waiting for transfers between devices, next_chip(): lax.ppermute(block, 'seq', [(i, i ^ 2) for i in range(lax.axis_size('seq'...  3.94 us
    ppermute x1, waiting for transfers between devices, around(): lax.ppermute(block, axis, [(i, (i + distance) % size) for i in range(size)])  3.09 us
    ppermute x1, starting transfers between devices, around(): lax.ppermute(block, axis, [(i, (i + distance) % size) for i in range(size)])  3.01 us
    ppermute x6, waiting for transfers between devices, exchanged(): lax.ppermute(block, 'mp', [(i, partner(i, distance, mp)) for i in range(m...  2.7 us
    pallas_call x1, Pallas kernels, per_device(): call(functools.partial(output_kernel, width, mp, chunk), 'output', shape(...  1.38 us
    pallas_call x1, Pallas kernels, per_device(): call(first_heads_kernel, 'first_heads', jax.ShapeDtypeStruct((window, row...  0.9 us
  transfers between devices with their start and end apart: 10, of which 4 were waited for; matrix products, arithmetic and copies ran while one was open for 0% of the time, Pallas kernels for 8%

profile of v5, /device:TPU:0, one launch (start us, length us, event | category | flops | bytes accessed | tf_op | source)
XLA Modules:
  0.0 34.9 jit_solution(8303809023718298915)
XLA Ops:
  0.0 0.0 copy-start.1
  0.0 0.7 %copy-done.1 = f32[5376]{0:T(1024)S(1)} copy-done((f32[5376]{0:T(1024)S(1)}, f32[5376]{0:T(1024)}, u32[]{:S(2)}) %copy-start.1) | copy-done | bytes 21528
  0.7 5.2 %project.1 = (bf16[512,128]{1,0:T(8,128)(2,1)S(1)}, bf16[1024,128]{1,0:T(8,128)(2,1)S(1)}, bf16[64,1408]{1,0:T(8,128)(2,1)S(1)}, bf16[64,1408]{1,0:T(8,128)(2,1)S(1)}, bf16[32,1408]{1,0:T(8,128)(2,1)S(1)}) custom-call(bf16[512,5376]{1,0:T(8,128)(2,1)} %x_ref.1, f32[42,128]{1,0:T(8,128)S(1)} %bitcast.1, bf16[5376,256]{1,0:T(8,128)(2,1)} %refs_0_.1, ...), custom_call_target="tpu_custom_call" | custom-call | flops 1 | bytes 1 | tf_op jit(solution)/shard_map/project/pallas_call | solution.py:335
  5.9 3.0 %collective-permute-start.4 = (bf16[1024,128]{1,0:T(8,128)(2,1)S(1)}, bf16[1024,128]{1,0:T(8,128)(2,1)S(1)}, u32[]{:S(2)}, u32[]{:S(2)}) collective-permute-start(bf16[1024,128]{1,0:T(8,128)(2,1)S(1)} %get-tuple-element.16.own_ref), channel_id=1, source_target_pairs={{0,8},{4,12},{8,16},{12,20},{16,24},{20,28},{24,0},{28,4},{1,9},{5... | collective-permute-start | bytes 786440 | tf_op jit(solution)/shard_map/ppermute | solution.py:21
  8.9 2.6 %collective-permute-start = (bf16[32,1408]{1,0:T(8,128)(2,1)S(1)}, bf16[32,1408]{1,0:T(8,128)(2,1)S(1)}, u32[]{:S(2)}, u32[]{:S(2)}) collective-permute-start(bf16[32,1408]{1,0:T(8,128)(2,1)S(1)} %get-tuple-element.12), channel_id=1, source_target_pairs={{0,2},{1,3},{2,0},{3,1},{4,6},{5,7},{6,4},{7,5},{8,10},{9,11},{10,... | collective-permute-start | bytes 270344 | tf_op jit(solution)/shard_map/ppermute | solution.py:38
  11.5 1.3 %collective-permute-start.2 = (bf16[64,1408]{1,0:T(8,128)(2,1)S(1)}, bf16[64,1408]{1,0:T(8,128)(2,1)S(1)}, u32[]{:S(2)}, u32[]{:S(2)}) collective-permute-start(bf16[64,1408]{1,0:T(8,128)(2,1)S(1)} %get-tuple-element.13), channel_id=1, source_target_pairs={{0,3},{1,2},{2,1},{3,0},{4,7},{5,6},{6,5},{7,4},{8,11},{9,10},{10,... | collective-permute-start | bytes 540680 | tf_op jit(solution)/shard_map/ppermute | solution.py:38
  12.8 0.2 collective-permute-start.3
  13.1 3.1 %collective-permute-done.4.far_ref = bf16[1024,128]{1,0:T(8,128)(2,1)S(1)} collective-permute-done((bf16[1024,128]{1,0:T(8,128)(2,1)S(1)}, bf16[1024,128]{1,0:T(8,128)(2,1)S(1)}, u32[]{:S(2)}, u32[]{:S(2)}) %collective-permute-start.4) | collective-permute-done | bytes 262176 | tf_op jit(solution)/shard_map/ppermute | solution.py:21
  16.2 0.1 pass_on.1
  16.2 0.1 collective-permute-start.5
  16.3 0.0 copy-start
  16.3 0.8 %mixed_blocks.1 = (f32[128,512]{1,0:T(8,128)S(1)}, f32[2,512]{1,0:T(2,128)S(1)}) custom-call(bf16[512,128]{1,0:T(8,128)(2,1)S(1)} %get-tuple-element.15.q_ref, bf16[1024,128]{1,0:T(8,128)(2,1)S(1)} %get-tuple-element.16.own_ref, bf16[1024,128]{1,0:T(8,128)(2,1)S(1)} %collective-permute-done.4.far_ref), custom_call_target="tpu_custom_call" | custom-call | flops 99999997952 | bytes 1 | tf_op jit(solution)/shard_map/mixed_blocks/pallas_call | solution.py:354
  17.1 0.7 %collective-permute-done.5.near_ref = bf16[1024,128]{1,0:T(8,128)(2,1)S(1)} collective-permute-done((bf16[1024,128]{1,0:T(8,128)(2,1)S(1)}, bf16[1024,128]{1,0:T(8,128)(2,1)S(1)}, u32[]{:S(2)}, u32[]{:S(2)}) %collective-permute-start.5) | collective-permute-done | bytes 262176 | tf_op jit(solution)/shard_map/ppermute | solution.py:25
  17.8 0.7 %near_block.1.refs_4_.refs_0_ = bf16[128,512]{1,0:T(8,128)(2,1)S(1)} custom-call(bf16[512,128]{1,0:T(8,128)(2,1)S(1)} %get-tuple-element.15.q_ref, bf16[1024,128]{1,0:T(8,128)(2,1)S(1)} %collective-permute-done.5.near_ref, f32[128,512]{1,0:T(8,128)S(1)} %get-tuple-element.17.mixed_ref, f32[2,512]{1,0:T(2,128)S(1)} %get-tuple-element.18.stats_ref), custom_call_target="tpu_custom_call" | custom-call | flops 1 | bytes 1 | tf_op jit(solution)/shard_map/near_block/pallas_call | solution.py:362
  18.5 3.9 %collective-permute-start.7 = (bf16[128,512]{1,0:T(8,128)(2,1)S(1)}, bf16[128,512]{1,0:T(8,128)(2,1)S(1)}, u32[]{:S(2)}, u32[]{:S(2)}) collective-permute-start(bf16[128,512]{1,0:T(8,128)(2,1)S(1)} %near_block.1.refs_4_.refs_0_), channel_id=1, source_target_pairs={{0,3},{1,2},{2,1},{3,0},{4,7},{5,6},{6,5},{7,4},{8,11},{9,10},{10,... | collective-permute-start | bytes 393224 | tf_op jit(solution)/shard_map/ppermute | solution.py:38
  22.4 0.0 collective-permute-start.8
  22.4 0.0 collective-permute-done.refs_0_
  22.4 0.6 %collective-permute-start.1 = (bf16[32,1408]{1,0:T(8,128)(2,1)S(1)}, bf16[32,1408]{1,0:T(8,128)(2,1)S(1)}, u32[]{:S(2)}, u32[]{:S(2)}) collective-permute-start(bf16[32,1408]{1,0:T(8,128)(2,1)S(1)} %collective-permute-done.refs_0_), channel_id=1, source_target_pairs={{0,8},{4,12},{8,0},{12,4},{16,24},{20,28},{24,16},{28,20},{1,9},{5... | collective-permute-start | bytes 270344 | tf_op jit(solution)/shard_map/ppermute | solution.py:29
  23.0 3.9 %collective-permute-done.1.refs_1_ = bf16[32,1408]{1,0:T(8,128)(2,1)S(1)} collective-permute-done((bf16[32,1408]{1,0:T(8,128)(2,1)S(1)}, bf16[32,1408]{1,0:T(8,128)(2,1)S(1)}, u32[]{:S(2)}, u32[]{:S(2)}) %collective-permute-start.1) | collective-permute-done | bytes 90144 | tf_op jit(solution)/shard_map/ppermute | solution.py:29
  26.9 0.0 collective-permute-done.2.refs_2_
  26.9 0.0 collective-permute-done.3.refs_3_
  26.9 0.0 copy-done
  26.9 0.3 turn_weight.1.mine_ref
  27.3 0.1 collective-permute-start.6
  27.3 0.0 collective-permute-done.7.refs_1_
  27.4 2.5 %collective-permute-start.9 = (bf16[128,512]{1,0:T(8,128)(2,1)S(1)}, bf16[128,512]{1,0:T(8,128)(2,1)S(1)}, u32[]{:S(2)}, u32[]{:S(2)}) collective-permute-start(bf16[128,512]{1,0:T(8,128)(2,1)S(1)} %collective-permute-done.7.refs_1_), channel_id=1, source_target_pairs={{0,1},{1,0},{2,3},{3,2},{4,5},{5,4},{6,7},{7,6},{8,9},{9,8},{10,11... | collective-permute-start | bytes 393224 | tf_op jit(solution)/shard_map/ppermute | solution.py:38
  29.9 0.0 collective-permute-done.8.refs_2_
  29.9 0.0 collective-permute-done.6.theirs_ref
  29.9 0.9 %first_heads.1.first_ref = f32[1408,512]{1,0:T(8,128)S(1)} custom-call(bf16[1408,256]{1,0:T(8,128)(2,1)S(1)} %turn_weight.1.mine_ref, bf16[1408,256]{1,0:T(8,128)(2,1)S(1)} %collective-permute-done.6.theirs_ref, bf16[512,512]{1,0:T(8,128)(2,1)S(1)} %collect_heads.1.heads_ref), custom_call_target="tpu_custom_call" | custom-call | flops 1 | bytes 1 | tf_op jit(solution)/shard_map/first_heads/pallas_call | solution.py:396
  30.9 2.7 %collective-permute-done.9.last_ref = bf16[128,512]{1,0:T(8,128)(2,1)S(1)} collective-permute-done((bf16[128,512]{1,0:T(8,128)(2,1)S(1)}, bf16[128,512]{1,0:T(8,128)(2,1)S(1)}, u32[]{:S(2)}, u32[]{:S(2)}) %collective-permute-start.9) | collective-permute-done | bytes 131104 | tf_op jit(solution)/shard_map/ppermute | solution.py:38
  33.5 1.4 %output.1 = bf16[1344,512]{1,0:T(8,128)(2,1)} custom-call(bf16[1408,256]{1,0:T(8,128)(2,1)S(1)} %turn_weight.1.mine_ref, bf16[1408,256]{1,0:T(8,128)(2,1)S(1)} %collective-permute-done.6.theirs_ref, f32[1408,512]{1,0:T(8,128)S(1)} %first_heads.1.first_ref, bf16[128,512]{1,0:T(8,128)(2,1)S(1)} %collective-permute-done.9.last_ref), custom_call_target="tpu_custom_call" | custom-call | flops 1 | bytes 1 | tf_op jit(solution)/shard_map/output/pallas_call | solution.py:405
  (1 shorter events, 0.0 us)
Async XLA Ops:
  0.0 0.7 %copy-start.1 = (f32[5376]{0:T(1024)S(1)}, f32[5376]{0:T(1024)}, u32[]{:S(2)}) copy-start(f32[5376]{0:T(1024)} %param.6) | copy-start | bytes 64516
  5.9 10.3 %collective-permute-start.4 = (bf16[1024,128]{1,0:T(8,128)(2,1)S(1)}, bf16[1024,128]{1,0:T(8,128)(2,1)S(1)}, u32[]{:S(2)}, u32[]{:S(2)}) collective-permute-start(bf16[1024,128]{1,0:T(8,128)(2,1)S(1)} %get-tuple-element.16.own_ref), channel_id=1, source_target_pairs={{0,8},{4,12},{8,16},{12,20},{16,24},{20,28},{24,0},{28,4},{1,9},{5... | collective-permute-start | bytes 786440 | tf_op jit(solution)/shard_map/ppermute | solution.py:21
  8.9 13.5 %collective-permute-start = (bf16[32,1408]{1,0:T(8,128)(2,1)S(1)}, bf16[32,1408]{1,0:T(8,128)(2,1)S(1)}, u32[]{:S(2)}, u32[]{:S(2)}) collective-permute-start(bf16[32,1408]{1,0:T(8,128)(2,1)S(1)} %get-tuple-element.12), channel_id=1, source_target_pairs={{0,2},{1,3},{2,0},{3,1},{4,6},{5,7},{6,4},{7,5},{8,10},{9,11},{10,... | collective-permute-start | bytes 270344 | tf_op jit(solution)/shard_map/ppermute | solution.py:38
  11.5 15.4 %collective-permute-start.2 = (bf16[64,1408]{1,0:T(8,128)(2,1)S(1)}, bf16[64,1408]{1,0:T(8,128)(2,1)S(1)}, u32[]{:S(2)}, u32[]{:S(2)}) collective-permute-start(bf16[64,1408]{1,0:T(8,128)(2,1)S(1)} %get-tuple-element.13), channel_id=1, source_target_pairs={{0,3},{1,2},{2,1},{3,0},{4,7},{5,6},{6,5},{7,4},{8,11},{9,10},{10,... | collective-permute-start | bytes 540680 | tf_op jit(solution)/shard_map/ppermute | solution.py:38
  12.8 14.1 %collective-permute-start.3 = (bf16[64,1408]{1,0:T(8,128)(2,1)S(1)}, bf16[64,1408]{1,0:T(8,128)(2,1)S(1)}, u32[]{:S(2)}, u32[]{:S(2)}) collective-permute-start(bf16[64,1408]{1,0:T(8,128)(2,1)S(1)} %get-tuple-element.14), channel_id=1, source_target_pairs={{0,1},{1,0},{2,3},{3,2},{4,5},{5,4},{6,7},{7,6},{8,9},{9,8},{10,11... | collective-permute-start | bytes 540680 | tf_op jit(solution)/shard_map/ppermute | solution.py:38
  16.2 1.6 %collective-permute-start.5 = (bf16[1024,128]{1,0:T(8,128)(2,1)S(1)}, bf16[1024,128]{1,0:T(8,128)(2,1)S(1)}, u32[]{:S(2)}, u32[]{:S(2)}) collective-permute-start(bf16[1024,128]{1,0:T(8,128)(2,1)S(1)} %pass_on.1), channel_id=1, source_target_pairs={{0,4},{4,0},{8,12},{12,8},{16,20},{20,16},{24,28},{28,24},{1,5},{5... | collective-permute-start | bytes 786440 | tf_op jit(solution)/shard_map/ppermute | solution.py:25
  16.3 10.6 %copy-start = (bf16[128,5376]{1,0:T(8,128)(2,1)S(1)}, bf16[128,5376]{1,0:T(8,128)(2,1)}, u32[]{:S(2)}) copy-start(bf16[128,5376]{1,0:T(8,128)(2,1)} %refs_5_.1) | copy-start | bytes 4128772
  18.5 8.8 %collective-permute-start.7 = (bf16[128,512]{1,0:T(8,128)(2,1)S(1)}, bf16[128,512]{1,0:T(8,128)(2,1)S(1)}, u32[]{:S(2)}, u32[]{:S(2)}) collective-permute-start(bf16[128,512]{1,0:T(8,128)(2,1)S(1)} %near_block.1.refs_4_.refs_0_), channel_id=1, source_target_pairs={{0,3},{1,2},{2,1},{3,0},{4,7},{5,6},{6,5},{7,4},{8,11},{9,10},{10,... | collective-permute-start | bytes 393224 | tf_op jit(solution)/shard_map/ppermute | solution.py:38
  22.4 7.5 %collective-permute-start.8 = (bf16[128,512]{1,0:T(8,128)(2,1)S(1)}, bf16[128,512]{1,0:T(8,128)(2,1)S(1)}, u32[]{:S(2)}, u32[]{:S(2)}) collective-permute-start(bf16[128,512]{1,0:T(8,128)(2,1)S(1)} %near_block.1.refs_4_.refs_0_), channel_id=1, source_target_pairs={{0,1},{1,0},{2,3},{3,2},{4,5},{5,4},{6,7},{7,6},{8,9},{9,8},{10,11... | collective-permute-start | bytes 393224 | tf_op jit(solution)/shard_map/ppermute | solution.py:38
  22.4 4.5 %collective-permute-start.1 = (bf16[32,1408]{1,0:T(8,128)(2,1)S(1)}, bf16[32,1408]{1,0:T(8,128)(2,1)S(1)}, u32[]{:S(2)}, u32[]{:S(2)}) collective-permute-start(bf16[32,1408]{1,0:T(8,128)(2,1)S(1)} %collective-permute-done.refs_0_), channel_id=1, source_target_pairs={{0,8},{4,12},{8,0},{12,4},{16,24},{20,28},{24,16},{28,20},{1,9},{5... | collective-permute-start | bytes 270344 | tf_op jit(solution)/shard_map/ppermute | solution.py:29
  27.3 2.7 %collective-permute-start.6 = (bf16[1408,256]{1,0:T(8,128)(2,1)S(1)}, bf16[1408,256]{1,0:T(8,128)(2,1)S(1)}, u32[]{:S(2)}, u32[]{:S(2)}) collective-permute-start(bf16[1408,256]{1,0:T(8,128)(2,1)S(1)} %turn_weight.1.mine_ref), channel_id=1, source_target_pairs={{0,4},{4,0},{8,12},{12,8},{16,20},{20,16},{24,28},{28,24},{1,5},{5... | collective-permute-start | bytes 2162696 | tf_op jit(solution)/shard_map/ppermute | solution.py:25
  27.4 6.2 %collective-permute-start.9 = (bf16[128,512]{1,0:T(8,128)(2,1)S(1)}, bf16[128,512]{1,0:T(8,128)(2,1)S(1)}, u32[]{:S(2)}, u32[]{:S(2)}) collective-permute-start(bf16[128,512]{1,0:T(8,128)(2,1)S(1)} %collective-permute-done.7.refs_1_), channel_id=1, source_target_pairs={{0,1},{1,0},{2,3},{3,2},{4,5},{5,4},{6,7},{7,6},{8,9},{9,8},{10,11... | collective-permute-start | bytes 393224 | tf_op jit(solution)/shard_map/ppermute | solution.py:38

commit v6 on v4

--- a/solution.py
+++ b/solution.py
@@ -112,9 +112,9 @@
                 x = x_buf[r : r + chunk, t : t + LANES]
                 gain = gain_ref[t // LANES : t // LANES + 1, :].astype(BF16)
                 scaled_ref[r : r + chunk, t : t + LANES] = x * gain
+                x = x.astype(F32)
                 square = x * x
                 part = square if part is None else part + square
-            part = part.astype(F32)
             square_ref[r : r + chunk, :] = part if k == 0 else square_ref[r : r + chunk, :] + part
         span = slice(end - size, end)
         product = matmul(scaled_ref[:, span], weight_buf[span, :])
@@ -330,7 +330,7 @@
     large = 52 * 2**20
 
     order = [3, 1, 2] if mp == 4 else list(range(1, mp))
-    split = [mp == 4 and d == 2 for d in order]
+    split = [mp == 4 and d == 3 for d in order]
     counts = [half // 2 if in_two else half for in_two in split]
     scale = math.log2(math.e) / math.sqrt(168.0)
     queries, kv, *pieces = call(
@@ -402,7 +402,7 @@
         out_specs=vmem,
     )(mine_turned, theirs_turned, taken)
 
-    chunk = max(c for c in range(16, min(cols, 448) + 1, 16) if cols % c == 0)
+    chunk = max(c for c in range(16, min(cols, 224) + 1, 16) if cols % c == 0)
     return call(
         functools.partial(output_kernel, width, mp, chunk),
         "output",

time: 35.1 us -> 35 us (level)
  transfers between devices with their start and end apart: 10 -> 10, of which waited for: 4 -> 5; matrix products, arithmetic and copies ran while one was open for 0% -> 0% of each run, Pallas kernels for 8% -> 8%
where the time goes in v6:
time: 35 us; the launch traced here: 34.8 us
  starting transfers between devices  14.3 us (41%)
  waiting for transfers between devices  10.4 us (30%)
  Pallas kernels  9.27 us (26%)
  local copies, waits for them, and re-layouts  0.74 us (2%)
    ppermute x6, starting transfers between devices, exchanged(): lax.ppermute(block, 'mp', [(i, partner(i, distance, mp)) for i in range(m...  10.6 us
    pallas_call x1, Pallas kernels, per_device(): call(functools.partial(project_all_kernel, scale, width, mp, BLOCKS, AHEA...  5.16 us
    ppermute x1, waiting for transfers between devices, next_chip(): lax.ppermute(block, 'seq', [(i, i ^ 2) for i in range(lax.axis_size('seq'...  3.94 us
    ppermute x1, starting transfers between devices, around(): lax.ppermute(block, axis, [(i, (i + distance) % size) for i in range(size)])  2.99 us
    ppermute x6, waiting for transfers between devices, exchanged(): lax.ppermute(block, 'mp', [(i, partner(i, distance, mp)) for i in range(m...  2.92 us
    ppermute x1, waiting for transfers between devices, around(): lax.ppermute(block, axis, [(i, (i + distance) % size) for i in range(size)])  2.87 us
    pallas_call x1, Pallas kernels, per_device(): call(functools.partial(output_kernel, width, mp, chunk), 'output', shape(...  1.35 us
    pallas_call x1, Pallas kernels, per_device(): call(first_heads_kernel, 'first_heads', jax.ShapeDtypeStruct((window, row...  0.9 us
  transfers between devices with their start and end apart: 10, of which 5 were waited for; matrix products, arithmetic and copies ran while one was open for 0% of the time, Pallas kernels for 8%

profile of v6, /device:TPU:0, one launch (start us, length us, event | category | flops | bytes accessed | tf_op | source)
XLA Modules:
  0.0 34.8 jit_solution(8428013655775776892)
XLA Ops:
  0.0 0.0 copy-start.1
  0.0 0.7 %copy-done.1 = f32[5376]{0:T(1024)S(1)} copy-done((f32[5376]{0:T(1024)S(1)}, f32[5376]{0:T(1024)}, u32[]{:S(2)}) %copy-start.1) | copy-done | bytes 21528
  0.7 5.2 %project.1 = (bf16[512,128]{1,0:T(8,128)(2,1)S(1)}, bf16[1024,128]{1,0:T(8,128)(2,1)S(1)}, bf16[32,1408]{1,0:T(8,128)(2,1)S(1)}, bf16[64,1408]{1,0:T(8,128)(2,1)S(1)}, bf16[64,1408]{1,0:T(8,128)(2,1)S(1)}) custom-call(bf16[512,5376]{1,0:T(8,128)(2,1)} %x_ref.1, f32[42,128]{1,0:T(8,128)S(1)} %bitcast.1, bf16[5376,256]{1,0:T(8,128)(2,1)} %refs_0_.1, ...), custom_call_target="tpu_custom_call" | custom-call | flops 1 | bytes 1 | tf_op jit(solution)/shard_map/project/pallas_call | solution.py:336
  5.9 3.0 %collective-permute-start.4 = (bf16[1024,128]{1,0:T(8,128)(2,1)S(1)}, bf16[1024,128]{1,0:T(8,128)(2,1)S(1)}, u32[]{:S(2)}, u32[]{:S(2)}) collective-permute-start(bf16[1024,128]{1,0:T(8,128)(2,1)S(1)} %get-tuple-element.16.own_ref), channel_id=1, source_target_pairs={{0,8},{4,12},{8,16},{12,20},{16,24},{20,28},{24,0},{28,4},{1,9},{5... | collective-permute-start | bytes 786440 | tf_op jit(solution)/shard_map/ppermute | solution.py:21
  8.9 3.6 %collective-permute-start = (bf16[32,1408]{1,0:T(8,128)(2,1)S(1)}, bf16[32,1408]{1,0:T(8,128)(2,1)S(1)}, u32[]{:S(2)}, u32[]{:S(2)}) collective-permute-start(bf16[32,1408]{1,0:T(8,128)(2,1)S(1)} %get-tuple-element.12), channel_id=1, source_target_pairs={{0,3},{1,2},{2,1},{3,0},{4,7},{5,6},{6,5},{7,4},{8,11},{9,10},{10,... | collective-permute-start | bytes 270344 | tf_op jit(solution)/shard_map/ppermute | solution.py:38
  12.5 0.0 collective-permute-start.2
  12.5 0.8 %collective-permute-start.3 = (bf16[64,1408]{1,0:T(8,128)(2,1)S(1)}, bf16[64,1408]{1,0:T(8,128)(2,1)S(1)}, u32[]{:S(2)}, u32[]{:S(2)}) collective-permute-start(bf16[64,1408]{1,0:T(8,128)(2,1)S(1)} %get-tuple-element.14), channel_id=1, source_target_pairs={{0,1},{1,0},{2,3},{3,2},{4,5},{5,4},{6,7},{7,6},{8,9},{9,8},{10,11... | collective-permute-start | bytes 540680 | tf_op jit(solution)/shard_map/ppermute | solution.py:38
  13.3 2.9 %collective-permute-done.4.far_ref = bf16[1024,128]{1,0:T(8,128)(2,1)S(1)} collective-permute-done((bf16[1024,128]{1,0:T(8,128)(2,1)S(1)}, bf16[1024,128]{1,0:T(8,128)(2,1)S(1)}, u32[]{:S(2)}, u32[]{:S(2)}) %collective-permute-start.4) | collective-permute-done | bytes 262176 | tf_op jit(solution)/shard_map/ppermute | solution.py:21
  16.2 0.1 pass_on.1
  16.2 0.1 collective-permute-start.5
  16.3 0.0 copy-start
  16.3 0.8 %mixed_blocks.1 = (f32[128,512]{1,0:T(8,128)S(1)}, f32[2,512]{1,0:T(2,128)S(1)}) custom-call(bf16[512,128]{1,0:T(8,128)(2,1)S(1)} %get-tuple-element.15.q_ref, bf16[1024,128]{1,0:T(8,128)(2,1)S(1)} %get-tuple-element.16.own_ref, bf16[1024,128]{1,0:T(8,128)(2,1)S(1)} %collective-permute-done.4.far_ref), custom_call_target="tpu_custom_call" | custom-call | flops 99999997952 | bytes 1 | tf_op jit(solution)/shard_map/mixed_blocks/pallas_call | solution.py:355
  17.1 0.7 %collective-permute-done.5.near_ref = bf16[1024,128]{1,0:T(8,128)(2,1)S(1)} collective-permute-done((bf16[1024,128]{1,0:T(8,128)(2,1)S(1)}, bf16[1024,128]{1,0:T(8,128)(2,1)S(1)}, u32[]{:S(2)}, u32[]{:S(2)}) %collective-permute-start.5) | collective-permute-done | bytes 262176 | tf_op jit(solution)/shard_map/ppermute | solution.py:25
  17.8 0.7 %near_block.1.refs_4_.refs_0_ = bf16[128,512]{1,0:T(8,128)(2,1)S(1)} custom-call(bf16[512,128]{1,0:T(8,128)(2,1)S(1)} %get-tuple-element.15.q_ref, bf16[1024,128]{1,0:T(8,128)(2,1)S(1)} %collective-permute-done.5.near_ref, f32[128,512]{1,0:T(8,128)S(1)} %get-tuple-element.17.mixed_ref, f32[2,512]{1,0:T(2,128)S(1)} %get-tuple-element.18.stats_ref), custom_call_target="tpu_custom_call" | custom-call | flops 1 | bytes 1 | tf_op jit(solution)/shard_map/near_block/pallas_call | solution.py:363
  18.5 3.9 %collective-permute-start.7 = (bf16[128,512]{1,0:T(8,128)(2,1)S(1)}, bf16[128,512]{1,0:T(8,128)(2,1)S(1)}, u32[]{:S(2)}, u32[]{:S(2)}) collective-permute-start(bf16[128,512]{1,0:T(8,128)(2,1)S(1)} %near_block.1.refs_4_.refs_0_), channel_id=1, source_target_pairs={{0,3},{1,2},{2,1},{3,0},{4,7},{5,6},{6,5},{7,4},{8,11},{9,10},{10,... | collective-permute-start | bytes 393224 | tf_op jit(solution)/shard_map/ppermute | solution.py:38
  22.4 0.0 collective-permute-start.8
  22.4 0.0 collective-permute-done.refs_0_
  22.4 0.6 %collective-permute-start.1 = (bf16[32,1408]{1,0:T(8,128)(2,1)S(1)}, bf16[32,1408]{1,0:T(8,128)(2,1)S(1)}, u32[]{:S(2)}, u32[]{:S(2)}) collective-permute-start(bf16[32,1408]{1,0:T(8,128)(2,1)S(1)} %collective-permute-done.refs_0_), channel_id=1, source_target_pairs={{0,8},{4,12},{8,0},{12,4},{16,24},{20,28},{24,16},{28,20},{1,9},{5... | collective-permute-start | bytes 270344 | tf_op jit(solution)/shard_map/ppermute | solution.py:29
  23.0 3.9 %collective-permute-done.1.refs_1_ = bf16[32,1408]{1,0:T(8,128)(2,1)S(1)} collective-permute-done((bf16[32,1408]{1,0:T(8,128)(2,1)S(1)}, bf16[32,1408]{1,0:T(8,128)(2,1)S(1)}, u32[]{:S(2)}, u32[]{:S(2)}) %collective-permute-start.1) | collective-permute-done | bytes 90144 | tf_op jit(solution)/shard_map/ppermute | solution.py:29
  26.9 0.2 collective-permute-done.2.refs_2_
  27.1 0.0 collective-permute-done.3.refs_3_
  27.1 0.0 copy-done
  27.1 0.3 turn_weight.1.mine_ref
  27.4 0.1 collective-permute-start.6
  27.5 0.0 collective-permute-done.7.refs_1_
  27.5 2.3 %collective-permute-start.9 = (bf16[128,512]{1,0:T(8,128)(2,1)S(1)}, bf16[128,512]{1,0:T(8,128)(2,1)S(1)}, u32[]{:S(2)}, u32[]{:S(2)}) collective-permute-start(bf16[128,512]{1,0:T(8,128)(2,1)S(1)} %collective-permute-done.7.refs_1_), channel_id=1, source_target_pairs={{0,1},{1,0},{2,3},{3,2},{4,5},{5,4},{6,7},{7,6},{8,9},{9,8},{10,11... | collective-permute-start | bytes 393224 | tf_op jit(solution)/shard_map/ppermute | solution.py:38
  29.8 0.0 collective-permute-done.8.refs_2_
  29.9 0.0 collective-permute-done.6.theirs_ref
  29.9 0.9 %first_heads.1.first_ref = f32[1408,512]{1,0:T(8,128)S(1)} custom-call(bf16[1408,256]{1,0:T(8,128)(2,1)S(1)} %turn_weight.1.mine_ref, bf16[1408,256]{1,0:T(8,128)(2,1)S(1)} %collective-permute-done.6.theirs_ref, bf16[512,512]{1,0:T(8,128)(2,1)S(1)} %collect_heads.1.heads_ref), custom_call_target="tpu_custom_call" | custom-call | flops 1 | bytes 1 | tf_op jit(solution)/shard_map/first_heads/pallas_call | solution.py:397
  30.8 2.7 %collective-permute-done.9.last_ref = bf16[128,512]{1,0:T(8,128)(2,1)S(1)} collective-permute-done((bf16[128,512]{1,0:T(8,128)(2,1)S(1)}, bf16[128,512]{1,0:T(8,128)(2,1)S(1)}, u32[]{:S(2)}, u32[]{:S(2)}) %collective-permute-start.9) | collective-permute-done | bytes 131104 | tf_op jit(solution)/shard_map/ppermute | solution.py:38
  33.5 1.3 %output.1 = bf16[1344,512]{1,0:T(8,128)(2,1)} custom-call(bf16[1408,256]{1,0:T(8,128)(2,1)S(1)} %turn_weight.1.mine_ref, bf16[1408,256]{1,0:T(8,128)(2,1)S(1)} %collective-permute-done.6.theirs_ref, f32[1408,512]{1,0:T(8,128)S(1)} %first_heads.1.first_ref, bf16[128,512]{1,0:T(8,128)(2,1)S(1)} %collective-permute-done.9.last_ref), custom_call_target="tpu_custom_call" | custom-call | flops 1 | bytes 1 | tf_op jit(solution)/shard_map/output/pallas_call | solution.py:406
  (1 shorter events, 0.0 us)
Async XLA Ops:
  0.0 0.7 %copy-start.1 = (f32[5376]{0:T(1024)S(1)}, f32[5376]{0:T(1024)}, u32[]{:S(2)}) copy-start(f32[5376]{0:T(1024)} %param.6) | copy-start | bytes 64516
  5.9 10.3 %collective-permute-start.4 = (bf16[1024,128]{1,0:T(8,128)(2,1)S(1)}, bf16[1024,128]{1,0:T(8,128)(2,1)S(1)}, u32[]{:S(2)}, u32[]{:S(2)}) collective-permute-start(bf16[1024,128]{1,0:T(8,128)(2,1)S(1)} %get-tuple-element.16.own_ref), channel_id=1, source_target_pairs={{0,8},{4,12},{8,16},{12,20},{16,24},{20,28},{24,0},{28,4},{1,9},{5... | collective-permute-start | bytes 786440 | tf_op jit(solution)/shard_map/ppermute | solution.py:21
  8.9 13.5 %collective-permute-start = (bf16[32,1408]{1,0:T(8,128)(2,1)S(1)}, bf16[32,1408]{1,0:T(8,128)(2,1)S(1)}, u32[]{:S(2)}, u32[]{:S(2)}) collective-permute-start(bf16[32,1408]{1,0:T(8,128)(2,1)S(1)} %get-tuple-element.12), channel_id=1, source_target_pairs={{0,3},{1,2},{2,1},{3,0},{4,7},{5,6},{6,5},{7,4},{8,11},{9,10},{10,... | collective-permute-start | bytes 270344 | tf_op jit(solution)/shard_map/ppermute | solution.py:38
  12.5 14.6 %collective-permute-start.2 = (bf16[64,1408]{1,0:T(8,128)(2,1)S(1)}, bf16[64,1408]{1,0:T(8,128)(2,1)S(1)}, u32[]{:S(2)}, u32[]{:S(2)}) collective-permute-start(bf16[64,1408]{1,0:T(8,128)(2,1)S(1)} %get-tuple-element.13), channel_id=1, source_target_pairs={{0,2},{1,3},{2,0},{3,1},{4,6},{5,7},{6,4},{7,5},{8,10},{9,11},{10,... | collective-permute-start | bytes 540680 | tf_op jit(solution)/shard_map/ppermute | solution.py:38
  12.5 14.6 %collective-permute-start.3 = (bf16[64,1408]{1,0:T(8,128)(2,1)S(1)}, bf16[64,1408]{1,0:T(8,128)(2,1)S(1)}, u32[]{:S(2)}, u32[]{:S(2)}) collective-permute-start(bf16[64,1408]{1,0:T(8,128)(2,1)S(1)} %get-tuple-element.14), channel_id=1, source_target_pairs={{0,1},{1,0},{2,3},{3,2},{4,5},{5,4},{6,7},{7,6},{8,9},{9,8},{10,11... | collective-permute-start | bytes 540680 | tf_op jit(solution)/shard_map/ppermute | solution.py:38
  16.2 1.6 %collective-permute-start.5 = (bf16[1024,128]{1,0:T(8,128)(2,1)S(1)}, bf16[1024,128]{1,0:T(8,128)(2,1)S(1)}, u32[]{:S(2)}, u32[]{:S(2)}) collective-permute-start(bf16[1024,128]{1,0:T(8,128)(2,1)S(1)} %pass_on.1), channel_id=1, source_target_pairs={{0,4},{4,0},{8,12},{12,8},{16,20},{20,16},{24,28},{28,24},{1,5},{5... | collective-permute-start | bytes 786440 | tf_op jit(solution)/shard_map/ppermute | solution.py:25
  16.3 10.8 %copy-start = (bf16[128,5376]{1,0:T(8,128)(2,1)S(1)}, bf16[128,5376]{1,0:T(8,128)(2,1)}, u32[]{:S(2)}) copy-start(bf16[128,5376]{1,0:T(8,128)(2,1)} %refs_5_.1) | copy-start | bytes 4128772
  18.5 9.0 %collective-permute-start.7 = (bf16[128,512]{1,0:T(8,128)(2,1)S(1)}, bf16[128,512]{1,0:T(8,128)(2,1)S(1)}, u32[]{:S(2)}, u32[]{:S(2)}) collective-permute-start(bf16[128,512]{1,0:T(8,128)(2,1)S(1)} %near_block.1.refs_4_.refs_0_), channel_id=1, source_target_pairs={{0,3},{1,2},{2,1},{3,0},{4,7},{5,6},{6,5},{7,4},{8,11},{9,10},{10,... | collective-permute-start | bytes 393224 | tf_op jit(solution)/shard_map/ppermute | solution.py:38
  22.4 7.5 %collective-permute-start.8 = (bf16[128,512]{1,0:T(8,128)(2,1)S(1)}, bf16[128,512]{1,0:T(8,128)(2,1)S(1)}, u32[]{:S(2)}, u32[]{:S(2)}) collective-permute-start(bf16[128,512]{1,0:T(8,128)(2,1)S(1)} %near_block.1.refs_4_.refs_0_), channel_id=1, source_target_pairs={{0,1},{1,0},{2,3},{3,2},{4,5},{5,4},{6,7},{7,6},{8,9},{9,8},{10,11... | collective-permute-start | bytes 393224 | tf_op jit(solution)/shard_map/ppermute | solution.py:38
  22.4 4.5 %collective-permute-start.1 = (bf16[32,1408]{1,0:T(8,128)(2,1)S(1)}, bf16[32,1408]{1,0:T(8,128)(2,1)S(1)}, u32[]{:S(2)}, u32[]{:S(2)}) collective-permute-start(bf16[32,1408]{1,0:T(8,128)(2,1)S(1)} %collective-permute-done.refs_0_), channel_id=1, source_target_pairs={{0,8},{4,12},{8,0},{12,4},{16,24},{20,28},{24,16},{28,20},{1,9},{5... | collective-permute-start | bytes 270344 | tf_op jit(solution)/shard_map/ppermute | solution.py:29
  27.4 2.5 %collective-permute-start.6 = (bf16[1408,256]{1,0:T(8,128)(2,1)S(1)}, bf16[1408,256]{1,0:T(8,128)(2,1)S(1)}, u32[]{:S(2)}, u32[]{:S(2)}) collective-permute-start(bf16[1408,256]{1,0:T(8,128)(2,1)S(1)} %turn_weight.1.mine_ref), channel_id=1, source_target_pairs={{0,4},{4,0},{8,12},{12,8},{16,20},{20,16},{24,28},{28,24},{1,5},{5... | collective-permute-start | bytes 2162696 | tf_op jit(solution)/shard_map/ppermute | solution.py:25
  27.5 6.0 %collective-permute-start.9 = (bf16[128,512]{1,0:T(8,128)(2,1)S(1)}, bf16[128,512]{1,0:T(8,128)(2,1)S(1)}, u32[]{:S(2)}, u32[]{:S(2)}) collective-permute-start(bf16[128,512]{1,0:T(8,128)(2,1)S(1)} %collective-permute-done.7.refs_1_), channel_id=1, source_target_pairs={{0,1},{1,0},{2,3},{3,2},{4,5},{5,4},{6,7},{7,6},{8,9},{9,8},{10,11... | collective-permute-start | bytes 393224 | tf_op jit(solution)/shard_map/ppermute | solution.py:38

commit v7 on v6

--- a/solution.py
+++ b/solution.py
@@ -146,8 +146,8 @@
         copy.wait()
 
 
-BLOCKS = (1280, 1280, 1280, 1024, 512)
-AHEAD = 4
+BLOCKS = (768,) * 7
+AHEAD = 5
 MIXED_COST = 10**11
 
 

time: 35 us -> 35 us (level)
  no operation moved by 1% of the time
where the time goes in v7:
time: 35 us; the launch traced here: 34.8 us
  starting transfers between devices  14.3 us (41%)
  waiting for transfers between devices  10.4 us (30%)
  Pallas kernels  9.22 us (26%)
  local copies, waits for them, and re-layouts  0.74 us (2%)
    ppermute x6, starting transfers between devices, exchanged(): lax.ppermute(block, 'mp', [(i, partner(i, distance, mp)) for i in range(m...  10.6 us
    pallas_call x1, Pallas kernels, per_device(): call(functools.partial(project_all_kernel, scale, width, mp, BLOCKS, AHEA...  5.11 us
    ppermute x1, waiting for transfers between devices, next_chip(): lax.ppermute(block, 'seq', [(i, i ^ 2) for i in range(lax.axis_size('seq'...  3.95 us
    ppermute x1, starting transfers between devices, around(): lax.ppermute(block, axis, [(i, (i + distance) % size) for i in range(size)])  2.99 us
    ppermute x6, waiting for transfers between devices, exchanged(): lax.ppermute(block, 'mp', [(i, partner(i, distance, mp)) for i in range(m...  2.91 us
    ppermute x1, waiting for transfers between devices, around(): lax.ppermute(block, axis, [(i, (i + distance) % size) for i in range(size)])  2.87 us
    pallas_call x1, Pallas kernels, per_device(): call(functools.partial(output_kernel, width, mp, chunk), 'output', shape(...  1.35 us
    pallas_call x1, Pallas kernels, per_device(): call(first_heads_kernel, 'first_heads', jax.ShapeDtypeStruct((window, row...  0.91 us
  transfers between devices with their start and end apart: 10, of which 5 were waited for; matrix products, arithmetic and copies ran while one was open for 0% of the time, Pallas kernels for 8%

profile of v7, /device:TPU:0, one launch (start us, length us, event | category | flops | bytes accessed | tf_op | source)
XLA Modules:
  0.0 34.8 jit_solution(17028397306453769640)
XLA Ops:
  0.0 0.0 copy-start.1
  0.0 0.7 %copy-done.1 = f32[5376]{0:T(1024)S(1)} copy-done((f32[5376]{0:T(1024)S(1)}, f32[5376]{0:T(1024)}, u32[]{:S(2)}) %copy-start.1) | copy-done | bytes 21528
  0.7 5.1 %project.1 = (bf16[512,128]{1,0:T(8,128)(2,1)S(1)}, bf16[1024,128]{1,0:T(8,128)(2,1)S(1)}, bf16[32,1408]{1,0:T(8,128)(2,1)S(1)}, bf16[64,1408]{1,0:T(8,128)(2,1)S(1)}, bf16[64,1408]{1,0:T(8,128)(2,1)S(1)}) custom-call(bf16[512,5376]{1,0:T(8,128)(2,1)} %x_ref.1, f32[42,128]{1,0:T(8,128)S(1)} %bitcast.1, bf16[5376,256]{1,0:T(8,128)(2,1)} %refs_0_.1, ...), custom_call_target="tpu_custom_call" | custom-call | flops 1 | bytes 1 | tf_op jit(solution)/shard_map/project/pallas_call | solution.py:336
  5.9 3.0 %collective-permute-start.4 = (bf16[1024,128]{1,0:T(8,128)(2,1)S(1)}, bf16[1024,128]{1,0:T(8,128)(2,1)S(1)}, u32[]{:S(2)}, u32[]{:S(2)}) collective-permute-start(bf16[1024,128]{1,0:T(8,128)(2,1)S(1)} %get-tuple-element.16.own_ref), channel_id=1, source_target_pairs={{0,8},{4,12},{8,16},{12,20},{16,24},{20,28},{24,0},{28,4},{1,9},{5... | collective-permute-start | bytes 786440 | tf_op jit(solution)/shard_map/ppermute | solution.py:21
  8.8 3.6 %collective-permute-start = (bf16[32,1408]{1,0:T(8,128)(2,1)S(1)}, bf16[32,1408]{1,0:T(8,128)(2,1)S(1)}, u32[]{:S(2)}, u32[]{:S(2)}) collective-permute-start(bf16[32,1408]{1,0:T(8,128)(2,1)S(1)} %get-tuple-element.12), channel_id=1, source_target_pairs={{0,3},{1,2},{2,1},{3,0},{4,7},{5,6},{6,5},{7,4},{8,11},{9,10},{10,... | collective-permute-start | bytes 270344 | tf_op jit(solution)/shard_map/ppermute | solution.py:38
  12.4 0.0 collective-permute-start.2
  12.4 0.8 %collective-permute-start.3 = (bf16[64,1408]{1,0:T(8,128)(2,1)S(1)}, bf16[64,1408]{1,0:T(8,128)(2,1)S(1)}, u32[]{:S(2)}, u32[]{:S(2)}) collective-permute-start(bf16[64,1408]{1,0:T(8,128)(2,1)S(1)} %get-tuple-element.14), channel_id=1, source_target_pairs={{0,1},{1,0},{2,3},{3,2},{4,5},{5,4},{6,7},{7,6},{8,9},{9,8},{10,11... | collective-permute-start | bytes 540680 | tf_op jit(solution)/shard_map/ppermute | solution.py:38
  13.2 2.9 %collective-permute-done.4.far_ref = bf16[1024,128]{1,0:T(8,128)(2,1)S(1)} collective-permute-done((bf16[1024,128]{1,0:T(8,128)(2,1)S(1)}, bf16[1024,128]{1,0:T(8,128)(2,1)S(1)}, u32[]{:S(2)}, u32[]{:S(2)}) %collective-permute-start.4) | collective-permute-done | bytes 262176 | tf_op jit(solution)/shard_map/ppermute | solution.py:21
  16.1 0.1 pass_on.1
  16.2 0.1 collective-permute-start.5
  16.3 0.0 copy-start
  16.3 0.8 %mixed_blocks.1 = (f32[128,512]{1,0:T(8,128)S(1)}, f32[2,512]{1,0:T(2,128)S(1)}) custom-call(bf16[512,128]{1,0:T(8,128)(2,1)S(1)} %get-tuple-element.15.q_ref, bf16[1024,128]{1,0:T(8,128)(2,1)S(1)} %get-tuple-element.16.own_ref, bf16[1024,128]{1,0:T(8,128)(2,1)S(1)} %collective-permute-done.4.far_ref), custom_call_target="tpu_custom_call" | custom-call | flops 99999997952 | bytes 1 | tf_op jit(solution)/shard_map/mixed_blocks/pallas_call | solution.py:355
  17.1 0.7 %collective-permute-done.5.near_ref = bf16[1024,128]{1,0:T(8,128)(2,1)S(1)} collective-permute-done((bf16[1024,128]{1,0:T(8,128)(2,1)S(1)}, bf16[1024,128]{1,0:T(8,128)(2,1)S(1)}, u32[]{:S(2)}, u32[]{:S(2)}) %collective-permute-start.5) | collective-permute-done | bytes 262176 | tf_op jit(solution)/shard_map/ppermute | solution.py:25
  17.8 0.7 %near_block.1.refs_4_.refs_0_ = bf16[128,512]{1,0:T(8,128)(2,1)S(1)} custom-call(bf16[512,128]{1,0:T(8,128)(2,1)S(1)} %get-tuple-element.15.q_ref, bf16[1024,128]{1,0:T(8,128)(2,1)S(1)} %collective-permute-done.5.near_ref, f32[128,512]{1,0:T(8,128)S(1)} %get-tuple-element.17.mixed_ref, f32[2,512]{1,0:T(2,128)S(1)} %get-tuple-element.18.stats_ref), custom_call_target="tpu_custom_call" | custom-call | flops 1 | bytes 1 | tf_op jit(solution)/shard_map/near_block/pallas_call | solution.py:363
  18.5 3.9 %collective-permute-start.7 = (bf16[128,512]{1,0:T(8,128)(2,1)S(1)}, bf16[128,512]{1,0:T(8,128)(2,1)S(1)}, u32[]{:S(2)}, u32[]{:S(2)}) collective-permute-start(bf16[128,512]{1,0:T(8,128)(2,1)S(1)} %near_block.1.refs_4_.refs_0_), channel_id=1, source_target_pairs={{0,3},{1,2},{2,1},{3,0},{4,7},{5,6},{6,5},{7,4},{8,11},{9,10},{10,... | collective-permute-start | bytes 393224 | tf_op jit(solution)/shard_map/ppermute | solution.py:38
  22.3 0.0 collective-permute-start.8
  22.3 0.0 collective-permute-done.refs_0_
  22.3 0.6 %collective-permute-start.1 = (bf16[32,1408]{1,0:T(8,128)(2,1)S(1)}, bf16[32,1408]{1,0:T(8,128)(2,1)S(1)}, u32[]{:S(2)}, u32[]{:S(2)}) collective-permute-start(bf16[32,1408]{1,0:T(8,128)(2,1)S(1)} %collective-permute-done.refs_0_), channel_id=1, source_target_pairs={{0,8},{4,12},{8,0},{12,4},{16,24},{20,28},{24,16},{28,20},{1,9},{5... | collective-permute-start | bytes 270344 | tf_op jit(solution)/shard_map/ppermute | solution.py:29
  22.9 3.9 %collective-permute-done.1.refs_1_ = bf16[32,1408]{1,0:T(8,128)(2,1)S(1)} collective-permute-done((bf16[32,1408]{1,0:T(8,128)(2,1)S(1)}, bf16[32,1408]{1,0:T(8,128)(2,1)S(1)}, u32[]{:S(2)}, u32[]{:S(2)}) %collective-permute-start.1) | collective-permute-done | bytes 90144 | tf_op jit(solution)/shard_map/ppermute | solution.py:29
  26.9 0.2 collective-permute-done.2.refs_2_
  27.1 0.0 collective-permute-done.3.refs_3_
  27.1 0.0 copy-done
  27.1 0.3 turn_weight.1.mine_ref
  27.4 0.1 collective-permute-start.6
  27.4 0.0 collective-permute-done.7.refs_1_
  27.4 2.3 %collective-permute-start.9 = (bf16[128,512]{1,0:T(8,128)(2,1)S(1)}, bf16[128,512]{1,0:T(8,128)(2,1)S(1)}, u32[]{:S(2)}, u32[]{:S(2)}) collective-permute-start(bf16[128,512]{1,0:T(8,128)(2,1)S(1)} %collective-permute-done.7.refs_1_), channel_id=1, source_target_pairs={{0,1},{1,0},{2,3},{3,2},{4,5},{5,4},{6,7},{7,6},{8,9},{9,8},{10,11... | collective-permute-start | bytes 393224 | tf_op jit(solution)/shard_map/ppermute | solution.py:38
  29.8 0.0 collective-permute-done.8.refs_2_
  29.8 0.0 collective-permute-done.6.theirs_ref
  29.8 0.9 %first_heads.1.first_ref = f32[1408,512]{1,0:T(8,128)S(1)} custom-call(bf16[1408,256]{1,0:T(8,128)(2,1)S(1)} %turn_weight.1.mine_ref, bf16[1408,256]{1,0:T(8,128)(2,1)S(1)} %collective-permute-done.6.theirs_ref, bf16[512,512]{1,0:T(8,128)(2,1)S(1)} %collect_heads.1.heads_ref), custom_call_target="tpu_custom_call" | custom-call | flops 1 | bytes 1 | tf_op jit(solution)/shard_map/first_heads/pallas_call | solution.py:397
  30.7 2.7 %collective-permute-done.9.last_ref = bf16[128,512]{1,0:T(8,128)(2,1)S(1)} collective-permute-done((bf16[128,512]{1,0:T(8,128)(2,1)S(1)}, bf16[128,512]{1,0:T(8,128)(2,1)S(1)}, u32[]{:S(2)}, u32[]{:S(2)}) %collective-permute-start.9) | collective-permute-done | bytes 131104 | tf_op jit(solution)/shard_map/ppermute | solution.py:38
  33.5 1.3 %output.1 = bf16[1344,512]{1,0:T(8,128)(2,1)} custom-call(bf16[1408,256]{1,0:T(8,128)(2,1)S(1)} %turn_weight.1.mine_ref, bf16[1408,256]{1,0:T(8,128)(2,1)S(1)} %collective-permute-done.6.theirs_ref, f32[1408,512]{1,0:T(8,128)S(1)} %first_heads.1.first_ref, bf16[128,512]{1,0:T(8,128)(2,1)S(1)} %collective-permute-done.9.last_ref), custom_call_target="tpu_custom_call" | custom-call | flops 1 | bytes 1 | tf_op jit(solution)/shard_map/output/pallas_call | solution.py:406
  (1 shorter events, 0.0 us)
Async XLA Ops:
  0.0 0.7 %copy-start.1 = (f32[5376]{0:T(1024)S(1)}, f32[5376]{0:T(1024)}, u32[]{:S(2)}) copy-start(f32[5376]{0:T(1024)} %param.6) | copy-start | bytes 64516
  5.9 10.3 %collective-permute-start.4 = (bf16[1024,128]{1,0:T(8,128)(2,1)S(1)}, bf16[1024,128]{1,0:T(8,128)(2,1)S(1)}, u32[]{:S(2)}, u32[]{:S(2)}) collective-permute-start(bf16[1024,128]{1,0:T(8,128)(2,1)S(1)} %get-tuple-element.16.own_ref), channel_id=1, source_target_pairs={{0,8},{4,12},{8,16},{12,20},{16,24},{20,28},{24,0},{28,4},{1,9},{5... | collective-permute-start | bytes 786440 | tf_op jit(solution)/shard_map/ppermute | solution.py:21
  8.8 13.5 %collective-permute-start = (bf16[32,1408]{1,0:T(8,128)(2,1)S(1)}, bf16[32,1408]{1,0:T(8,128)(2,1)S(1)}, u32[]{:S(2)}, u32[]{:S(2)}) collective-permute-start(bf16[32,1408]{1,0:T(8,128)(2,1)S(1)} %get-tuple-element.12), channel_id=1, source_target_pairs={{0,3},{1,2},{2,1},{3,0},{4,7},{5,6},{6,5},{7,4},{8,11},{9,10},{10,... | collective-permute-start | bytes 270344 | tf_op jit(solution)/shard_map/ppermute | solution.py:38
  12.4 14.6 %collective-permute-start.2 = (bf16[64,1408]{1,0:T(8,128)(2,1)S(1)}, bf16[64,1408]{1,0:T(8,128)(2,1)S(1)}, u32[]{:S(2)}, u32[]{:S(2)}) collective-permute-start(bf16[64,1408]{1,0:T(8,128)(2,1)S(1)} %get-tuple-element.13), channel_id=1, source_target_pairs={{0,2},{1,3},{2,0},{3,1},{4,6},{5,7},{6,4},{7,5},{8,10},{9,11},{10,... | collective-permute-start | bytes 540680 | tf_op jit(solution)/shard_map/ppermute | solution.py:38
  12.4 14.6 %collective-permute-start.3 = (bf16[64,1408]{1,0:T(8,128)(2,1)S(1)}, bf16[64,1408]{1,0:T(8,128)(2,1)S(1)}, u32[]{:S(2)}, u32[]{:S(2)}) collective-permute-start(bf16[64,1408]{1,0:T(8,128)(2,1)S(1)} %get-tuple-element.14), channel_id=1, source_target_pairs={{0,1},{1,0},{2,3},{3,2},{4,5},{5,4},{6,7},{7,6},{8,9},{9,8},{10,11... | collective-permute-start | bytes 540680 | tf_op jit(solution)/shard_map/ppermute | solution.py:38
  16.2 1.6 %collective-permute-start.5 = (bf16[1024,128]{1,0:T(8,128)(2,1)S(1)}, bf16[1024,128]{1,0:T(8,128)(2,1)S(1)}, u32[]{:S(2)}, u32[]{:S(2)}) collective-permute-start(bf16[1024,128]{1,0:T(8,128)(2,1)S(1)} %pass_on.1), channel_id=1, source_target_pairs={{0,4},{4,0},{8,12},{12,8},{16,20},{20,16},{24,28},{28,24},{1,5},{5... | collective-permute-start | bytes 786440 | tf_op jit(solution)/shard_map/ppermute | solution.py:25
  16.3 10.8 %copy-start = (bf16[128,5376]{1,0:T(8,128)(2,1)S(1)}, bf16[128,5376]{1,0:T(8,128)(2,1)}, u32[]{:S(2)}) copy-start(bf16[128,5376]{1,0:T(8,128)(2,1)} %refs_5_.1) | copy-start | bytes 4128772
  18.5 9.0 %collective-permute-start.7 = (bf16[128,512]{1,0:T(8,128)(2,1)S(1)}, bf16[128,512]{1,0:T(8,128)(2,1)S(1)}, u32[]{:S(2)}, u32[]{:S(2)}) collective-permute-start(bf16[128,512]{1,0:T(8,128)(2,1)S(1)} %near_block.1.refs_4_.refs_0_), channel_id=1, source_target_pairs={{0,3},{1,2},{2,1},{3,0},{4,7},{5,6},{6,5},{7,4},{8,11},{9,10},{10,... | collective-permute-start | bytes 393224 | tf_op jit(solution)/shard_map/ppermute | solution.py:38
  22.3 7.5 %collective-permute-start.8 = (bf16[128,512]{1,0:T(8,128)(2,1)S(1)}, bf16[128,512]{1,0:T(8,128)(2,1)S(1)}, u32[]{:S(2)}, u32[]{:S(2)}) collective-permute-start(bf16[128,512]{1,0:T(8,128)(2,1)S(1)} %near_block.1.refs_4_.refs_0_), channel_id=1, source_target_pairs={{0,1},{1,0},{2,3},{3,2},{4,5},{5,4},{6,7},{7,6},{8,9},{9,8},{10,11... | collective-permute-start | bytes 393224 | tf_op jit(solution)/shard_map/ppermute | solution.py:38
  22.3 4.5 %collective-permute-start.1 = (bf16[32,1408]{1,0:T(8,128)(2,1)S(1)}, bf16[32,1408]{1,0:T(8,128)(2,1)S(1)}, u32[]{:S(2)}, u32[]{:S(2)}) collective-permute-start(bf16[32,1408]{1,0:T(8,128)(2,1)S(1)} %collective-permute-done.refs_0_), channel_id=1, source_target_pairs={{0,8},{4,12},{8,0},{12,4},{16,24},{20,28},{24,16},{28,20},{1,9},{5... | collective-permute-start | bytes 270344 | tf_op jit(solution)/shard_map/ppermute | solution.py:29
  27.4 2.5 %collective-permute-start.6 = (bf16[1408,256]{1,0:T(8,128)(2,1)S(1)}, bf16[1408,256]{1,0:T(8,128)(2,1)S(1)}, u32[]{:S(2)}, u32[]{:S(2)}) collective-permute-start(bf16[1408,256]{1,0:T(8,128)(2,1)S(1)} %turn_weight.1.mine_ref), channel_id=1, source_target_pairs={{0,4},{4,0},{8,12},{12,8},{16,20},{20,16},{24,28},{28,24},{1,5},{5... | collective-permute-start | bytes 2162696 | tf_op jit(solution)/shard_map/ppermute | solution.py:25
  27.4 6.0 %collective-permute-start.9 = (bf16[128,512]{1,0:T(8,128)(2,1)S(1)}, bf16[128,512]{1,0:T(8,128)(2,1)S(1)}, u32[]{:S(2)}, u32[]{:S(2)}) collective-permute-start(bf16[128,512]{1,0:T(8,128)(2,1)S(1)} %collective-permute-done.7.refs_1_), channel_id=1, source_target_pairs={{0,1},{1,0},{2,3},{3,2},{4,5},{5,4},{6,7},{7,6},{8,9},{9,8},{10,11... | collective-permute-start | bytes 393224 | tf_op jit(solution)/shard_map/ppermute | solution.py:38

commit v8 on v7

--- a/solution.py
+++ b/solution.py
@@ -147,7 +147,7 @@
 
 
 BLOCKS = (768,) * 7
-AHEAD = 5
+AHEAD = 7
 MIXED_COST = 10**11
 
 

time: 35 us -> 34.9 us (level)
  no operation moved by 1% of the time
where the time goes in v8:
time: 34.9 us; the launch traced here: 34.8 us
  starting transfers between devices  14.3 us (41%)
  waiting for transfers between devices  10.4 us (30%)
  Pallas kernels  9.18 us (26%)
  local copies, waits for them, and re-layouts  0.74 us (2%)
    ppermute x6, starting transfers between devices, exchanged(): lax.ppermute(block, 'mp', [(i, partner(i, distance, mp)) for i in range(m...  10.6 us
    pallas_call x1, Pallas kernels, per_device(): call(functools.partial(project_all_kernel, scale, width, mp, BLOCKS, AHEA...  5.07 us
    ppermute x1, waiting for transfers between devices, next_chip(): lax.ppermute(block, 'seq', [(i, i ^ 2) for i in range(lax.axis_size('seq'...  3.95 us
    ppermute x1, starting transfers between devices, around(): lax.ppermute(block, axis, [(i, (i + distance) % size) for i in range(size)])  3 us
    ppermute x6, waiting for transfers between devices, exchanged(): lax.ppermute(block, 'mp', [(i, partner(i, distance, mp)) for i in range(m...  2.91 us
    ppermute x1, waiting for transfers between devices, around(): lax.ppermute(block, axis, [(i, (i + distance) % size) for i in range(size)])  2.86 us
    pallas_call x1, Pallas kernels, per_device(): call(functools.partial(output_kernel, width, mp, chunk), 'output', shape(...  1.35 us
    pallas_call x1, Pallas kernels, per_device(): call(first_heads_kernel, 'first_heads', jax.ShapeDtypeStruct((window, row...  0.9 us
  transfers between devices with their start and end apart: 10, of which 5 were waited for; matrix products, arithmetic and copies ran while one was open for 0% of the time, Pallas kernels for 8%

profile of v8, /device:TPU:0, one launch (start us, length us, event | category | flops | bytes accessed | tf_op | source)
XLA Modules:
  0.0 34.8 jit_solution(8429069474434796343)
XLA Ops:
  0.0 0.0 copy-start.1
  0.0 0.7 %copy-done.1 = f32[5376]{0:T(1024)S(1)} copy-done((f32[5376]{0:T(1024)S(1)}, f32[5376]{0:T(1024)}, u32[]{:S(2)}) %copy-start.1) | copy-done | bytes 21528
  0.7 5.1 %project.1 = (bf16[512,128]{1,0:T(8,128)(2,1)S(1)}, bf16[1024,128]{1,0:T(8,128)(2,1)S(1)}, bf16[32,1408]{1,0:T(8,128)(2,1)S(1)}, bf16[64,1408]{1,0:T(8,128)(2,1)S(1)}, bf16[64,1408]{1,0:T(8,128)(2,1)S(1)}) custom-call(bf16[512,5376]{1,0:T(8,128)(2,1)} %x_ref.1, f32[42,128]{1,0:T(8,128)S(1)} %bitcast.1, bf16[5376,256]{1,0:T(8,128)(2,1)} %refs_0_.1, ...), custom_call_target="tpu_custom_call" | custom-call | flops 1 | bytes 1 | tf_op jit(solution)/shard_map/project/pallas_call | solution.py:336
  5.8 3.0 %collective-permute-start.4 = (bf16[1024,128]{1,0:T(8,128)(2,1)S(1)}, bf16[1024,128]{1,0:T(8,128)(2,1)S(1)}, u32[]{:S(2)}, u32[]{:S(2)}) collective-permute-start(bf16[1024,128]{1,0:T(8,128)(2,1)S(1)} %get-tuple-element.16.own_ref), channel_id=1, source_target_pairs={{0,8},{4,12},{8,16},{12,20},{16,24},{20,28},{24,0},{28,4},{1,9},{5... | collective-permute-start | bytes 786440 | tf_op jit(solution)/shard_map/ppermute | solution.py:21
  8.8 3.6 %collective-permute-start = (bf16[32,1408]{1,0:T(8,128)(2,1)S(1)}, bf16[32,1408]{1,0:T(8,128)(2,1)S(1)}, u32[]{:S(2)}, u32[]{:S(2)}) collective-permute-start(bf16[32,1408]{1,0:T(8,128)(2,1)S(1)} %get-tuple-element.12), channel_id=1, source_target_pairs={{0,3},{1,2},{2,1},{3,0},{4,7},{5,6},{6,5},{7,4},{8,11},{9,10},{10,... | collective-permute-start | bytes 270344 | tf_op jit(solution)/shard_map/ppermute | solution.py:38
  12.4 0.0 collective-permute-start.2
  12.4 0.8 %collective-permute-start.3 = (bf16[64,1408]{1,0:T(8,128)(2,1)S(1)}, bf16[64,1408]{1,0:T(8,128)(2,1)S(1)}, u32[]{:S(2)}, u32[]{:S(2)}) collective-permute-start(bf16[64,1408]{1,0:T(8,128)(2,1)S(1)} %get-tuple-element.14), channel_id=1, source_target_pairs={{0,1},{1,0},{2,3},{3,2},{4,5},{5,4},{6,7},{7,6},{8,9},{9,8},{10,11... | collective-permute-start | bytes 540680 | tf_op jit(solution)/shard_map/ppermute | solution.py:38
  13.2 2.9 %collective-permute-done.4.far_ref = bf16[1024,128]{1,0:T(8,128)(2,1)S(1)} collective-permute-done((bf16[1024,128]{1,0:T(8,128)(2,1)S(1)}, bf16[1024,128]{1,0:T(8,128)(2,1)S(1)}, u32[]{:S(2)}, u32[]{:S(2)}) %collective-permute-start.4) | collective-permute-done | bytes 262176 | tf_op jit(solution)/shard_map/ppermute | solution.py:21
  16.1 0.1 pass_on.1
  16.1 0.1 collective-permute-start.5
  16.2 0.0 copy-start
  16.2 0.8 %mixed_blocks.1 = (f32[128,512]{1,0:T(8,128)S(1)}, f32[2,512]{1,0:T(2,128)S(1)}) custom-call(bf16[512,128]{1,0:T(8,128)(2,1)S(1)} %get-tuple-element.15.q_ref, bf16[1024,128]{1,0:T(8,128)(2,1)S(1)} %get-tuple-element.16.own_ref, bf16[1024,128]{1,0:T(8,128)(2,1)S(1)} %collective-permute-done.4.far_ref), custom_call_target="tpu_custom_call" | custom-call | flops 99999997952 | bytes 1 | tf_op jit(solution)/shard_map/mixed_blocks/pallas_call | solution.py:355
  17.0 0.7 %collective-permute-done.5.near_ref = bf16[1024,128]{1,0:T(8,128)(2,1)S(1)} collective-permute-done((bf16[1024,128]{1,0:T(8,128)(2,1)S(1)}, bf16[1024,128]{1,0:T(8,128)(2,1)S(1)}, u32[]{:S(2)}, u32[]{:S(2)}) %collective-permute-start.5) | collective-permute-done | bytes 262176 | tf_op jit(solution)/shard_map/ppermute | solution.py:25
  17.7 0.7 %near_block.1.refs_4_.refs_0_ = bf16[128,512]{1,0:T(8,128)(2,1)S(1)} custom-call(bf16[512,128]{1,0:T(8,128)(2,1)S(1)} %get-tuple-element.15.q_ref, bf16[1024,128]{1,0:T(8,128)(2,1)S(1)} %collective-permute-done.5.near_ref, f32[128,512]{1,0:T(8,128)S(1)} %get-tuple-element.17.mixed_ref, f32[2,512]{1,0:T(2,128)S(1)} %get-tuple-element.18.stats_ref), custom_call_target="tpu_custom_call" | custom-call | flops 1 | bytes 1 | tf_op jit(solution)/shard_map/near_block/pallas_call | solution.py:363
  18.4 3.9 %collective-permute-start.7 = (bf16[128,512]{1,0:T(8,128)(2,1)S(1)}, bf16[128,512]{1,0:T(8,128)(2,1)S(1)}, u32[]{:S(2)}, u32[]{:S(2)}) collective-permute-start(bf16[128,512]{1,0:T(8,128)(2,1)S(1)} %near_block.1.refs_4_.refs_0_), channel_id=1, source_target_pairs={{0,3},{1,2},{2,1},{3,0},{4,7},{5,6},{6,5},{7,4},{8,11},{9,10},{10,... | collective-permute-start | bytes 393224 | tf_op jit(solution)/shard_map/ppermute | solution.py:38
  22.3 0.0 collective-permute-start.8
  22.3 0.0 collective-permute-done.refs_0_
  22.3 0.6 %collective-permute-start.1 = (bf16[32,1408]{1,0:T(8,128)(2,1)S(1)}, bf16[32,1408]{1,0:T(8,128)(2,1)S(1)}, u32[]{:S(2)}, u32[]{:S(2)}) collective-permute-start(bf16[32,1408]{1,0:T(8,128)(2,1)S(1)} %collective-permute-done.refs_0_), channel_id=1, source_target_pairs={{0,8},{4,12},{8,0},{12,4},{16,24},{20,28},{24,16},{28,20},{1,9},{5... | collective-permute-start | bytes 270344 | tf_op jit(solution)/shard_map/ppermute | solution.py:29
  22.9 3.9 %collective-permute-done.1.refs_1_ = bf16[32,1408]{1,0:T(8,128)(2,1)S(1)} collective-permute-done((bf16[32,1408]{1,0:T(8,128)(2,1)S(1)}, bf16[32,1408]{1,0:T(8,128)(2,1)S(1)}, u32[]{:S(2)}, u32[]{:S(2)}) %collective-permute-start.1) | collective-permute-done | bytes 90144 | tf_op jit(solution)/shard_map/ppermute | solution.py:29
  26.8 0.2 collective-permute-done.2.refs_2_
  27.0 0.0 collective-permute-done.3.refs_3_
  27.0 0.0 copy-done
  27.0 0.3 turn_weight.1.mine_ref
  27.3 0.1 collective-permute-start.6
  27.4 0.0 collective-permute-done.7.refs_1_
  27.4 2.3 %collective-permute-start.9 = (bf16[128,512]{1,0:T(8,128)(2,1)S(1)}, bf16[128,512]{1,0:T(8,128)(2,1)S(1)}, u32[]{:S(2)}, u32[]{:S(2)}) collective-permute-start(bf16[128,512]{1,0:T(8,128)(2,1)S(1)} %collective-permute-done.7.refs_1_), channel_id=1, source_target_pairs={{0,1},{1,0},{2,3},{3,2},{4,5},{5,4},{6,7},{7,6},{8,9},{9,8},{10,11... | collective-permute-start | bytes 393224 | tf_op jit(solution)/shard_map/ppermute | solution.py:38
  29.7 0.0 collective-permute-done.8.refs_2_
  29.8 0.0 collective-permute-done.6.theirs_ref
  29.8 0.9 %first_heads.1.first_ref = f32[1408,512]{1,0:T(8,128)S(1)} custom-call(bf16[1408,256]{1,0:T(8,128)(2,1)S(1)} %turn_weight.1.mine_ref, bf16[1408,256]{1,0:T(8,128)(2,1)S(1)} %collective-permute-done.6.theirs_ref, bf16[512,512]{1,0:T(8,128)(2,1)S(1)} %collect_heads.1.heads_ref), custom_call_target="tpu_custom_call" | custom-call | flops 1 | bytes 1 | tf_op jit(solution)/shard_map/first_heads/pallas_call | solution.py:397
  30.7 2.7 %collective-permute-done.9.last_ref = bf16[128,512]{1,0:T(8,128)(2,1)S(1)} collective-permute-done((bf16[128,512]{1,0:T(8,128)(2,1)S(1)}, bf16[128,512]{1,0:T(8,128)(2,1)S(1)}, u32[]{:S(2)}, u32[]{:S(2)}) %collective-permute-start.9) | collective-permute-done | bytes 131104 | tf_op jit(solution)/shard_map/ppermute | solution.py:38
  33.4 1.3 %output.1 = bf16[1344,512]{1,0:T(8,128)(2,1)} custom-call(bf16[1408,256]{1,0:T(8,128)(2,1)S(1)} %turn_weight.1.mine_ref, bf16[1408,256]{1,0:T(8,128)(2,1)S(1)} %collective-permute-done.6.theirs_ref, f32[1408,512]{1,0:T(8,128)S(1)} %first_heads.1.first_ref, bf16[128,512]{1,0:T(8,128)(2,1)S(1)} %collective-permute-done.9.last_ref), custom_call_target="tpu_custom_call" | custom-call | flops 1 | bytes 1 | tf_op jit(solution)/shard_map/output/pallas_call | solution.py:406
  (1 shorter events, 0.0 us)
Async XLA Ops:
  0.0 0.7 %copy-start.1 = (f32[5376]{0:T(1024)S(1)}, f32[5376]{0:T(1024)}, u32[]{:S(2)}) copy-start(f32[5376]{0:T(1024)} %param.6) | copy-start | bytes 64516
  5.8 10.3 %collective-permute-start.4 = (bf16[1024,128]{1,0:T(8,128)(2,1)S(1)}, bf16[1024,128]{1,0:T(8,128)(2,1)S(1)}, u32[]{:S(2)}, u32[]{:S(2)}) collective-permute-start(bf16[1024,128]{1,0:T(8,128)(2,1)S(1)} %get-tuple-element.16.own_ref), channel_id=1, source_target_pairs={{0,8},{4,12},{8,16},{12,20},{16,24},{20,28},{24,0},{28,4},{1,9},{5... | collective-permute-start | bytes 786440 | tf_op jit(solution)/shard_map/ppermute | solution.py:21
  8.8 13.5 %collective-permute-start = (bf16[32,1408]{1,0:T(8,128)(2,1)S(1)}, bf16[32,1408]{1,0:T(8,128)(2,1)S(1)}, u32[]{:S(2)}, u32[]{:S(2)}) collective-permute-start(bf16[32,1408]{1,0:T(8,128)(2,1)S(1)} %get-tuple-element.12), channel_id=1, source_target_pairs={{0,3},{1,2},{2,1},{3,0},{4,7},{5,6},{6,5},{7,4},{8,11},{9,10},{10,... | collective-permute-start | bytes 270344 | tf_op jit(solution)/shard_map/ppermute | solution.py:38
  12.4 14.6 %collective-permute-start.2 = (bf16[64,1408]{1,0:T(8,128)(2,1)S(1)}, bf16[64,1408]{1,0:T(8,128)(2,1)S(1)}, u32[]{:S(2)}, u32[]{:S(2)}) collective-permute-start(bf16[64,1408]{1,0:T(8,128)(2,1)S(1)} %get-tuple-element.13), channel_id=1, source_target_pairs={{0,2},{1,3},{2,0},{3,1},{4,6},{5,7},{6,4},{7,5},{8,10},{9,11},{10,... | collective-permute-start | bytes 540680 | tf_op jit(solution)/shard_map/ppermute | solution.py:38
  12.4 14.6 %collective-permute-start.3 = (bf16[64,1408]{1,0:T(8,128)(2,1)S(1)}, bf16[64,1408]{1,0:T(8,128)(2,1)S(1)}, u32[]{:S(2)}, u32[]{:S(2)}) collective-permute-start(bf16[64,1408]{1,0:T(8,128)(2,1)S(1)} %get-tuple-element.14), channel_id=1, source_target_pairs={{0,1},{1,0},{2,3},{3,2},{4,5},{5,4},{6,7},{7,6},{8,9},{9,8},{10,11... | collective-permute-start | bytes 540680 | tf_op jit(solution)/shard_map/ppermute | solution.py:38
  16.1 1.6 %collective-permute-start.5 = (bf16[1024,128]{1,0:T(8,128)(2,1)S(1)}, bf16[1024,128]{1,0:T(8,128)(2,1)S(1)}, u32[]{:S(2)}, u32[]{:S(2)}) collective-permute-start(bf16[1024,128]{1,0:T(8,128)(2,1)S(1)} %pass_on.1), channel_id=1, source_target_pairs={{0,4},{4,0},{8,12},{12,8},{16,20},{20,16},{24,28},{28,24},{1,5},{5... | collective-permute-start | bytes 786440 | tf_op jit(solution)/shard_map/ppermute | solution.py:25
  16.2 10.8 %copy-start = (bf16[128,5376]{1,0:T(8,128)(2,1)S(1)}, bf16[128,5376]{1,0:T(8,128)(2,1)}, u32[]{:S(2)}) copy-start(bf16[128,5376]{1,0:T(8,128)(2,1)} %refs_5_.1) | copy-start | bytes 4128772
  18.4 9.0 %collective-permute-start.7 = (bf16[128,512]{1,0:T(8,128)(2,1)S(1)}, bf16[128,512]{1,0:T(8,128)(2,1)S(1)}, u32[]{:S(2)}, u32[]{:S(2)}) collective-permute-start(bf16[128,512]{1,0:T(8,128)(2,1)S(1)} %near_block.1.refs_4_.refs_0_), channel_id=1, source_target_pairs={{0,3},{1,2},{2,1},{3,0},{4,7},{5,6},{6,5},{7,4},{8,11},{9,10},{10,... | collective-permute-start | bytes 393224 | tf_op jit(solution)/shard_map/ppermute | solution.py:38
  22.3 7.5 %collective-permute-start.8 = (bf16[128,512]{1,0:T(8,128)(2,1)S(1)}, bf16[128,512]{1,0:T(8,128)(2,1)S(1)}, u32[]{:S(2)}, u32[]{:S(2)}) collective-permute-start(bf16[128,512]{1,0:T(8,128)(2,1)S(1)} %near_block.1.refs_4_.refs_0_), channel_id=1, source_target_pairs={{0,1},{1,0},{2,3},{3,2},{4,5},{5,4},{6,7},{7,6},{8,9},{9,8},{10,11... | collective-permute-start | bytes 393224 | tf_op jit(solution)/shard_map/ppermute | solution.py:38
  22.3 4.5 %collective-permute-start.1 = (bf16[32,1408]{1,0:T(8,128)(2,1)S(1)}, bf16[32,1408]{1,0:T(8,128)(2,1)S(1)}, u32[]{:S(2)}, u32[]{:S(2)}) collective-permute-start(bf16[32,1408]{1,0:T(8,128)(2,1)S(1)} %collective-permute-done.refs_0_), channel_id=1, source_target_pairs={{0,8},{4,12},{8,0},{12,4},{16,24},{20,28},{24,16},{28,20},{1,9},{5... | collective-permute-start | bytes 270344 | tf_op jit(solution)/shard_map/ppermute | solution.py:29
  27.3 2.5 %collective-permute-start.6 = (bf16[1408,256]{1,0:T(8,128)(2,1)S(1)}, bf16[1408,256]{1,0:T(8,128)(2,1)S(1)}, u32[]{:S(2)}, u32[]{:S(2)}) collective-permute-start(bf16[1408,256]{1,0:T(8,128)(2,1)S(1)} %turn_weight.1.mine_ref), channel_id=1, source_target_pairs={{0,4},{4,0},{8,12},{12,8},{16,20},{20,16},{24,28},{28,24},{1,5},{5... | collective-permute-start | bytes 2162696 | tf_op jit(solution)/shard_map/ppermute | solution.py:25
  27.4 6.0 %collective-permute-start.9 = (bf16[128,512]{1,0:T(8,128)(2,1)S(1)}, bf16[128,512]{1,0:T(8,128)(2,1)S(1)}, u32[]{:S(2)}, u32[]{:S(2)}) collective-permute-start(bf16[128,512]{1,0:T(8,128)(2,1)S(1)} %collective-permute-done.7.refs_1_), channel_id=1, source_target_pairs={{0,1},{1,0},{2,3},{3,2},{4,5},{5,4},{6,7},{7,6},{8,9},{9,8},{10,11... | collective-permute-start | bytes 393224 | tf_op jit(solution)/shard_map/ppermute | solution.py:38
